TPU v7x, 32 devices: a whole 2x2x4 slice. The times are simulated.
32 devices in a mesh: tmpl: 4 (over y, x), freq: 8 (over z, core).
Axes of the slice: x: 2, y: 2, z: 4, core: 2. Of those that a mesh axis runs over, the one named last changes fastest.
Arguments:
- strain: float32 [64, 524288], P('tmpl', 'freq'), may hold values from -6 to 6
- psd: float32 [512, 512], P(None, 'freq'), may hold values from 0.1 to 10
- templates: bfloat16 [1024, 2, 512, 512], P('tmpl', None, 'freq'), may hold values from -0.0234375 to 0.0234375
- cutoffs: int32 [1024], P('tmpl'), may hold values from 1 to 512, as said below
- lags: int32 [16], replicated, may hold values from 0 to 524287
Outputs:
- intersections: float32 [64, 32, 1024], P('freq', None, 'tmpl')
Inputs may be any that keep to these rules, and one draw needn't show every extreme that they name: `cutoffs`: the cutoff counts do not increase along the template index.
All inputs are finite; a program needn't handle non-finite values.
Results may differ from a plain program's by a relative error of at most 0.004.
Values may be sent and summed in bfloat16 or wider, within the bound.
No kernel may reach another device: no remote copies, remote signals or barrier semaphores. Data moves between devices by JAX's collectives and lax.ppermute only.
A program may use at most 192 MiB of HBM per device.

v0:
```python
import math

import jax
import jax.numpy as jnp
from jax import lax
from jax.sharding import PartitionSpec as P

A = 512
B = 1024
LEN = 524288
NB = 512


two_pi = 2.0 * math.pi


def cos_sin_table(row_ids, col_ids, modulus):
    product = row_ids[:, None] * col_ids[None, :] % modulus
    phase_angle = product.astype(jnp.float32) * (two_pi / modulus)
    return (jnp.cos(phase_angle), jnp.sin(phase_angle))


def on_device(strain, psd, templates, cutoffs, lags):
    freq_count = lax.axis_size("freq")
    freq_index = lax.axis_index("freq")
    seg_local = strain.shape[0]
    step_time = B // freq_count
    highest = lax.Precision.HIGHEST
    first_cos, first_sin = cos_sin_table(
        jnp.arange(A, dtype=jnp.int32), jnp.arange(A, dtype=jnp.int32), A
    )
    first_table = jnp.concatenate([first_cos, -first_sin], axis=0)
    time_ids = freq_index * step_time + jnp.arange(step_time, dtype=jnp.int32)
    twist_cos, twist_sin = cos_sin_table(jnp.arange(A, dtype=jnp.int32), time_ids, LEN)
    slab_blocks = strain.reshape(seg_local, A // freq_count, B)
    both_parts = jnp.einsum(
        "kn,snb->skb",
        first_table,
        lax.all_to_all(slab_blocks, "freq", split_axis=2, concat_axis=1, tiled=True),
        precision=highest,
    )
    half_rows = first_table.shape[0] // 2
    real_part = both_parts[:, :half_rows]
    imag_part = both_parts[:, half_rows:]
    second_cos, second_sin = cos_sin_table(
        jnp.arange(B, dtype=jnp.int32), jnp.arange(NB, dtype=jnp.int32), B
    )
    rotation = jnp.concatenate(
        [
            jnp.concatenate([second_cos, -second_sin], axis=1),
            jnp.concatenate([second_sin, second_cos], axis=1),
        ],
        axis=0,
    )
    amplitude = jnp.sqrt(LEN * psd)
    real_in = lax.all_to_all(
        real_part * twist_cos + imag_part * twist_sin,
        "freq",
        split_axis=1,
        concat_axis=2,
        tiled=True,
    )
    imag_in = lax.all_to_all(
        imag_part * twist_cos - real_part * twist_sin,
        "freq",
        split_axis=1,
        concat_axis=2,
        tiled=True,
    )
    joined = jnp.concatenate([real_in, imag_in], axis=2)
    both_out = jnp.einsum("spc,cm->smp", joined, rotation, precision=highest)
    both_out = both_out.reshape(joined.shape[0], 2, NB, joined.shape[1])
    whitened = (both_out / amplitude).astype(jnp.bfloat16)
    local_data = lax.all_to_all(whitened, "freq", split_axis=2, concat_axis=3, tiled=True)
    first_block = freq_index * (NB // freq_count)
    position = jnp.arange(A, dtype=jnp.int32)
    blocks_here = local_data.shape[2]
    width_here = local_data.shape[3]
    per_span = min(blocks_here, max(1, 512 // width_here))
    span_total = blocks_here // per_span
    tmpl_local = templates.shape[0]
    group_size = min(128, tmpl_local)
    group_total = tmpl_local // group_size
    group_top = jnp.max(cutoffs.reshape(group_total, group_size), axis=1)
    lag_total = lags.shape[0]

    def multiply(lhs_rows, tmpl_cols):
        return lax.dot_general(
            lhs_rows, tmpl_cols, (((1,), (1,)), ((), ())), preferred_element_type=jnp.float32
        )

    def skipped(lhs_rows, tmpl_cols):
        return jnp.zeros((lhs_rows.shape[0], tmpl_cols.shape[0]), jnp.float32)

    seg_piece = lax.all_gather(local_data, "tmpl", axis=0, tiled=True)
    seg_count = seg_piece.shape[0]

    def one_span(span_idx, running):
        offset = span_idx * per_span
        block_ids = first_block + offset + jnp.arange(per_span, dtype=jnp.int32)
        data_part = lax.dynamic_slice_in_dim(seg_piece, offset, per_span, 2).astype(jnp.float32)
        tmpl_part = lax.dynamic_slice_in_dim(templates, offset, per_span, 2)
        phase_int = (A * (lags[:, None] * block_ids[None, :] % B))[:, :, None] + (
            lags[:, None] * position[None, :] % LEN
        )[:, None, :]
        phase_angle = (phase_int % LEN).astype(jnp.float32) * (two_pi / LEN)
        lag_cos = jnp.cos(phase_angle)[None]
        lag_sin = jnp.sin(phase_angle)[None]
        data_real = data_part[:, 0][:, None]
        data_imag = data_part[:, 1][:, None]
        real_q = (data_real * lag_cos - data_imag * lag_sin).astype(jnp.bfloat16)
        imag_q = (data_real * lag_sin + data_imag * lag_cos).astype(jnp.bfloat16)
        real_rows = jnp.stack([real_q, imag_q], axis=2)
        imag_rows = jnp.stack([imag_q, -real_q], axis=2)
        lhs_rows = jnp.stack([real_rows, imag_rows], axis=1).reshape(
            seg_count * 2 * lag_total, 2 * per_span * width_here
        )
        keep_mask = (block_ids[None, :] < cutoffs[:, None]).astype(jnp.bfloat16)
        masked = (tmpl_part * keep_mask[:, None, :, None]).reshape(
            tmpl_local, 2 * per_span * width_here
        )
        outputs = []
        for group_idx in range(group_total):
            tmpl_cols = masked[group_idx * group_size : (group_idx + 1) * group_size]
            outputs.append(
                lax.cond(
                    group_top[group_idx] > block_ids[0], multiply, skipped, lhs_rows, tmpl_cols
                )
            )
        return running + jnp.concatenate(outputs, axis=1)

    start_sum = jnp.zeros((seg_count * 2 * lag_total, tmpl_local), jnp.float32)
    running = lax.fori_loop(0, span_total, one_span, start_sum)
    partial_sums = running.reshape(seg_count, 2 * lag_total, tmpl_local)
    return lax.psum_scatter(partial_sums, "freq", scatter_dimension=0, tiled=True)


def solution(mesh):
    placed = (P("tmpl", "freq"), P(None, "freq"), P("tmpl", None, "freq", None), P("tmpl"), P())
    return jax.shard_map(
        on_device, mesh=mesh, in_specs=placed, out_specs=P("freq", None, "tmpl"), check_vma=False
    )
```

profile of v0, /device:TPU:0, one launch (start us, length us, event | category | flops | bytes accessed | tf_op | source)
XLA Modules:
  0.0 3387.5 jit_solution(2716538451302394058)
XLA Ops:
  42.8 88.9 %all-to-all-done = f32[8,1,131072]{2,1,0:T(1,128)} async-done(((f32[8,1,131072]{2,1,0:T(1,128)}), f32[8,1,131072]{2,1,0:T(1,128)}, u32[]{:S(2)}, u32[]{:S(2)}) %all-to-all-start) | async-done | bytes 4194336 | tf_op jit(solution)/shard_map/all_to_all | solution.py:39
  132.2 13.7 reduce
  161.4 16.3 convolution_bitcast_fusion
  196.5 87.4 %all-to-all-done.1 = f32[16,512,128]{2,0,1:T(8,128)} async-done(((f32[16,512,128]{2,0,1:T(8,128)}), f32[16,512,128]{2,0,1:T(8,128)}, u32[]{:S(2)}, u32[]{:S(2)}) %all-to-all-start.1) | async-done | bytes 4194336 | tf_op jit(solution)/shard_map/all_to_all | solution.py:56
  317.8 64.7 %all-to-all-done.2 = f32[16,512,128]{2,0,1:T(8,128)} async-done(((f32[16,512,128]{2,0,1:T(8,128)}), f32[16,512,128]{2,0,1:T(8,128)}, u32[]{:S(2)}, u32[]{:S(2)}) %all-to-all-start.2) | async-done | bytes 4194336 | tf_op jit(solution)/shard_map/all_to_all | solution.py:63
  393.9 34.6 %fusion.24 = f32[16,1024,64]{1,2,0:T(8,128)} fusion(f32[16,64,1024]{2,1,0:T(8,128)} %all_to_all.63, f32[16,64,1024]{2,1,0:T(8,128)} %all_to_all.59, f32[1024,512]{1,0:T(8,128)} %get-tuple-element.396, f32[1024,512]{1,0:T(8,128)S(1)} %get-tuple-element.395, f32[1024,512]{1,0:T(8,128)} %fusion.43), kind=kOutput, calls=%fused_computation.54 | convolution fusion | flops 25778192384 | bytes 18874368 | tf_op jit(solution)/shard_map/spc,cm->smp/dot_general | solution.py:71
  456.8 52.7 %all_to_all.72 = bf16[8,2,65536]{2,1,0:T(2,128)(2,1)} all-to-all(bf16[8,2,65536]{2,1,0:T(2,128)(2,1)S(1)} %reshape.318), channel_id=1, replica_groups=mesh['tmpl'=4,'freq'=8] {'freq'}, dimensions={0} | all-to-all | bytes 4194304 | tf_op jit(solution)/shard_map/all_to_all | solution.py:74
  532.4 47.0 %copy.62 = bf16[256,2,64,512]{0,3,1,2:T(8,128)(2,1)} copy(bf16[256,2,64,512]{3,2,1,0:T(8,128)(2,1)} %param.13) | data formatting | bytes 67108864
  579.5 39.4 %all-gather.2.cloned.1.call-done = bf16[64,2,64,512]{3,0,2,1:T(8,128)(2,1)} async-done(((bf16[16,2,64,512]{3,0,2,1:T(8,128)(2,1)}), bf16[64,2,64,512]{3,0,2,1:T(8,128)(2,1)}) %all-gather.2.cloned.1.call-update) | async-done | bytes 8388624 | tf_op jit(solution)/shard_map/all_gather | solution.py:95
  619.0 2727.3 %while.17 = (s32[]{:T(128)}, f32[2048,256]{1,0:T(8,128)}, s32[2]{0:T(128)S(1)}, s32[]{:T(128)}, bf16[64,2,64,512]{3,0,2,1:T(8,128)(2,1)}, /*index=5*/s32[16]{0:T...) while((s32[]{:T(128)}, f32[2048,256]{1,0:T(8,128)}, ...), condition=%wide.region_6.7_spmd.clone, body=%wide.region_1.6_spmd.clone.sunk | while | flops 1091060480 | bytes 48302564 | solution.py:133
  628.0 10.4 maximum_bitcast_fusion.9
  669.0 10.4 maximum_bitcast_fusion.9
  711.6 10.4 maximum_bitcast_fusion.9
  754.3 10.4 maximum_bitcast_fusion.9
  796.9 10.4 maximum_bitcast_fusion.9
  839.6 10.4 maximum_bitcast_fusion.9
  882.2 10.4 maximum_bitcast_fusion.9
  924.8 10.4 maximum_bitcast_fusion.9
  967.5 10.4 maximum_bitcast_fusion.9
  1010.1 10.4 maximum_bitcast_fusion.9
  1052.7 10.4 maximum_bitcast_fusion.9
  1095.4 10.4 maximum_bitcast_fusion.9
  1138.0 10.4 maximum_bitcast_fusion.9
  1180.6 10.4 maximum_bitcast_fusion.9
  1223.3 10.4 maximum_bitcast_fusion.9
  1265.9 10.4 maximum_bitcast_fusion.9
  1308.6 10.4 maximum_bitcast_fusion.9
  1351.2 10.4 maximum_bitcast_fusion.9
  1393.8 10.4 maximum_bitcast_fusion.9
  1436.5 10.4 maximum_bitcast_fusion.9
  1479.1 10.4 maximum_bitcast_fusion.9
  1521.7 10.4 maximum_bitcast_fusion.9
  1564.4 10.4 maximum_bitcast_fusion.9
  1607.0 10.4 maximum_bitcast_fusion.9
  1649.6 10.4 maximum_bitcast_fusion.9
  1692.3 10.4 maximum_bitcast_fusion.9
  1734.9 10.4 maximum_bitcast_fusion.9
  1777.5 10.4 maximum_bitcast_fusion.9
  1820.2 10.4 maximum_bitcast_fusion.9
  1862.8 10.4 maximum_bitcast_fusion.9
  1905.5 10.4 maximum_bitcast_fusion.9
  1948.1 10.4 maximum_bitcast_fusion.9
  1990.7 10.4 maximum_bitcast_fusion.9
  2033.4 10.4 maximum_bitcast_fusion.9
  2076.0 10.4 maximum_bitcast_fusion.9
  2118.6 10.4 maximum_bitcast_fusion.9
  2161.3 10.4 maximum_bitcast_fusion.9
  2203.9 10.4 maximum_bitcast_fusion.9
  2289.2 10.4 maximum_bitcast_fusion.9
  2374.4 10.4 maximum_bitcast_fusion.9
  2459.7 10.4 maximum_bitcast_fusion.9
  2545.0 10.4 maximum_bitcast_fusion.9
  2587.6 10.4 maximum_bitcast_fusion.9
  2630.3 10.4 maximum_bitcast_fusion.9
  2672.9 10.4 maximum_bitcast_fusion.9
  2758.2 10.4 maximum_bitcast_fusion.9
  2843.4 10.4 maximum_bitcast_fusion.9
  2928.7 10.4 maximum_bitcast_fusion.9
  3014.0 10.4 maximum_bitcast_fusion.9
  3099.3 10.4 maximum_bitcast_fusion.9
  3184.5 10.4 maximum_bitcast_fusion.9
  3227.2 10.4 maximum_bitcast_fusion.9
  3269.8 10.4 maximum_bitcast_fusion.9
  3346.3 34.2 %reduce-scatter.2.cloned.1.call-done = f32[8,32,256]{2,1,0:T(8,128)} async-done(((f32[64,32,256]{2,1,0:T(8,128)}), f32[8,32,256]{2,1,0:T(8,128)}) %reduce-scatter.2.cloned.1.call-update) | async-done | bytes 262160 | tf_op jit(solution)/shard_map/reduce_scatter | solution.py:135
  (1205 shorter events, 2702.0 us)
Async XLA Ops:
  31.1 100.6 %all-to-all-start = ((f32[8,1,131072]{2,1,0:T(1,128)}), f32[8,1,131072]{2,1,0:T(1,128)}, u32[]{:S(2)}, u32[]{:S(2)}) async-start(f32[8,1,131072]{2,1,0:T(1,128)} %reshape.316), calls=%async_computation | async-start | bytes 8388608 | tf_op jit(solution)/shard_map/all_to_all | solution.py:39
  184.9 99.0 %all-to-all-start.1 = ((f32[16,512,128]{2,0,1:T(8,128)}), f32[16,512,128]{2,0,1:T(8,128)}, u32[]{:S(2)}, u32[]{:S(2)}) async-start(f32[16,512,128]{2,0,1:T(8,128)} %copy.55), calls=%async_computation.1 | async-start | bytes 8388608 | tf_op jit(solution)/shard_map/all_to_all | solution.py:56
  196.4 92.1 %copy-start = (f32[512,64]{0,1:T(8,128)S(1)}, f32[512,64]{0,1:T(8,128)}, u32[]{:S(2)}) copy-start(f32[512,64]{0,1:T(8,128)} %param.12) | copy-start | bytes 393220
  283.9 98.6 %all-to-all-start.2 = ((f32[16,512,128]{2,0,1:T(8,128)}), f32[16,512,128]{2,0,1:T(8,128)}, u32[]{:S(2)}, u32[]{:S(2)}) async-start(f32[16,512,128]{2,0,1:T(8,128)} %copy.57), calls=%async_computation.2 | async-start | bytes 8388608 | tf_op jit(solution)/shard_map/all_to_all | solution.py:63
  288.5 330.5 %all-gather.2.cloned.1.call-start = ((), (), s32[]{:S(2)}) async-start(), calls=%async_computation.5 | async-start | bytes 10485760 | tf_op jit(solution)/shard_map/all_gather | solution.py:95
  532.3 2848.2 %reduce-scatter.2.cloned.1.call-start = ((), (), s32[]{:S(2)}) async-start(), calls=%async_computation.6 | async-start | bytes 2359296 | tf_op jit(solution)/shard_map/reduce_scatter | solution.py:135
  532.4 47.1 %copy-start.1 = (s32[256]{0:T(256)S(1)}, s32[256]{0:T(256)}, u32[]{:S(2)}) copy-start(s32[256]{0:T(256)} %param.14) | copy-start | bytes 3076
  532.4 86.6 %copy-start.2 = (s32[16]{0:T(128)S(1)}, s32[16]{0:T(128)}, u32[]{:S(2)}) copy-start(s32[16]{0:T(128)} %param.15) | copy-start | bytes 196
Sparse Core Ops, SparseCore 0:
  532.4 86.5 all-gather.1
  3346.4 34.0 reduce-scatter.1
where the time goes:
time: 3410 us; the launch traced here: 3390 us
  other arithmetic  2000 us (59%)
  matrix products  491 us (14%)
  local copies, waits for them, and re-layouts  412 us (12%)
  waiting for transfers between devices  315 us (9%)
  loops' own time  88.3 us (3%)
  blocking collectives  52.7 us (2%)
    another operation x128, other arithmetic, one_span(): jnp.stack([real_rows, imag_rows], axis=1)  1120 us
    dot_general x128, matrix products, multiply(): lax.dot_general(lhs_rows, tmpl_cols, (((1,), (1,)), ((), ())), preferred_...  440 us
    neg x64, other arithmetic, one_span(): imag_rows = jnp.stack([imag_q, -real_q], axis=2)  307 us
    while x64, local copies, waits for them, and re-layouts  200 us
    add x64, other arithmetic, one_span(): return running + jnp.concatenate(outputs, axis=1)  200 us
    convert_element_type x64, other arithmetic, one_span(): imag_q = (data_real * lag_sin + data_imag * lag_cos).astype(jnp.bfloat16)  179 us
    all_to_all x1, waiting for transfers between devices, on_device(): lax.all_to_all(slab_blocks, 'freq', split_axis=2, concat_axis=1, tiled=True)  88.9 us
    all_to_all x1, waiting for transfers between devices, on_device(): lax.all_to_all(real_part * twist_cos + imag_part * twist_sin, 'freq', spl...  87.4 us
  transfers between devices with their start and end apart: 5, of which 5 were waited for; matrix products, arithmetic and copies ran while one was open for 2% of the time, Pallas kernels for 0%

commit v1 on v0

v1 whole, which is shorter than its diff:
```python
import math

import jax
import jax.numpy as jnp
import ml_dtypes
import numpy as np
from jax import lax
from jax.experimental import pallas as pl
from jax.experimental.pallas import tpu as pltpu
from jax.sharding import PartitionSpec as P

A = 512
B = 1024
LEN = 524288
NB = 512
HALF = A // 2

STRAIN_SCALE = 8192.0
COEF_SCALE = 16.0

two_pi = 2.0 * math.pi


def cos_sin_table(row_ids, col_ids, modulus):
    product = row_ids[:, None] * col_ids[None, :] % modulus
    phase_angle = product.astype(jnp.float32) * (two_pi / modulus)
    return (jnp.cos(phase_angle), jnp.sin(phase_angle))


def split_const(table):
    high = table.astype(ml_dtypes.bfloat16)
    low = (table - high.astype(np.float64)).astype(ml_dtypes.bfloat16)
    return high, low


def first_table():
    angle = two_pi * (np.outer(np.arange(HALF), np.arange(A)) % A) / A
    table = np.concatenate([np.cos(angle), -np.sin(angle)], axis=0)
    table[HALF] = 1.0 - 2.0 * (np.arange(A) % 2)
    return split_const(table)


def second_tables():
    angle = two_pi * (np.outer(np.arange(528), np.arange(B)) % B) / B
    return split_const(np.cos(angle)) + split_const(np.sin(angle))


def twist_tables():
    angle = two_pi * np.outer(np.arange(HALF), np.arange(B)) / LEN
    edge = two_pi * HALF * np.arange(B)[None, :] / LEN
    return (
        np.cos(angle).astype(np.float32),
        np.sin(angle).astype(np.float32),
        np.cos(edge).astype(np.float32),
        np.sin(edge).astype(np.float32),
    )


def mirror_table():
    table = np.zeros((HALF, HALF), np.float32)
    table[0, 0] = 1.0
    table[np.arange(1, HALF), HALF - np.arange(1, HALF)] = 1.0
    return table


def split_parts(value):
    high = value.astype(jnp.bfloat16)
    low = (value - high.astype(jnp.float32)).astype(jnp.bfloat16)
    return high, low


def dot_nn(lhs, rhs):
    return lax.dot_general(lhs, rhs, (((1,), (0,)), ((), ())), preferred_element_type=jnp.float32)


def dot_nt(lhs, rhs):
    return lax.dot_general(lhs, rhs, (((1,), (1,)), ((), ())), preferred_element_type=jnp.float32)


def first_kernel(x_ref, high_ref, low_ref, out_ref):
    parts = x_ref.shape[0]
    pair = x_ref.shape[1]
    columns = []
    for s in range(pair):
        columns.append(jnp.concatenate([x_ref[f, s] for f in range(parts)], axis=0))
    value = jnp.concatenate(columns, axis=1)
    high, low = split_parts(value)
    result = dot_nn(high_ref[...], high) + dot_nn(high_ref[...], low) + dot_nn(low_ref[...], high)
    width = x_ref.shape[3]
    for s in range(pair):
        out_ref[s] = result[:, s * width : (s + 1) * width]


def first_section(received, tables):
    parts, segs, rows, width = received.shape
    pair = 2
    return pl.pallas_call(
        first_kernel,
        grid=(segs // pair,),
        in_specs=[
            pl.BlockSpec((parts, pair, rows, width), lambda i: (0, i, 0, 0)),
            pl.BlockSpec((A, A), lambda i: (0, 0)),
            pl.BlockSpec((A, A), lambda i: (0, 0)),
        ],
        out_specs=pl.BlockSpec((pair, A, width), lambda i: (i, 0, 0)),
        out_shape=jax.ShapeDtypeStruct((segs, A, width), jnp.float32),
        compiler_params=pltpu.CompilerParams(vmem_limit_bytes=40 * 2**20),
        cost_estimate=pl.CostEstimate(
            flops=2 * 3 * segs * A * A * width, bytes_accessed=segs * A * width * 8, transcendentals=0
        ),
        name="first_section",
    )(received, *tables)


def second_kernel(
    y_ref, tc_ref, ts_ref, ec_ref, es_ref, ch_ref, cl_ref, sh_ref, sl_ref, wa_ref, wm_ref, q_ref, out_ref
):
    parts = y_ref.shape[0]
    joined = jnp.concatenate([y_ref[f, 0] for f in range(parts)], axis=1)
    real_raw = joined[:HALF]
    imag_raw = joined[HALF:]
    row_ids = lax.broadcasted_iota(jnp.int32, (HALF, B), 0)
    imag_in = jnp.where(row_ids == 0, 0.0, imag_raw)
    twist_cos = tc_ref[...]
    twist_sin = ts_ref[...]
    real_u = real_raw * twist_cos + imag_in * twist_sin
    imag_u = imag_in * twist_cos - real_raw * twist_sin
    edge = imag_raw[0:1]
    edge_rows = jnp.where(
        lax.broadcasted_iota(jnp.int32, (16, B), 0) == 0,
        edge * ec_ref[...],
        jnp.where(lax.broadcasted_iota(jnp.int32, (16, B), 0) == 1, -edge * es_ref[...], 0.0),
    )
    u_high, u_low = split_parts(jnp.concatenate([real_u, imag_u], axis=0))
    e_high, e_low = split_parts(edge_rows)

    def three(high_ref, low_ref, high, low):
        return (
            dot_nt(high_ref[...], high) + dot_nt(high_ref[...], low) + dot_nt(low_ref[...], high)
        )

    by_cos = three(ch_ref, cl_ref, u_high, u_low)
    by_sin = three(sh_ref, sl_ref, u_high, u_low)
    edge_cos = three(ch_ref, cl_ref, e_high, e_low)[:NB]
    edge_sin = three(sh_ref, sl_ref, e_high, e_low)[:NB]
    white = wa_ref[...]
    real_out = ((by_cos[:NB, :HALF] + by_sin[:NB, HALF:]) * white).astype(jnp.bfloat16)
    imag_out = ((by_cos[:NB, HALF:] - by_sin[:NB, :HALF]) * white).astype(jnp.bfloat16)
    next_cos = by_cos[1 : NB + 1]
    next_sin = by_sin[1 : NB + 1]
    lane = lax.broadcasted_iota(jnp.int32, (NB, HALF), 1)
    real_edge = edge_cos[:, 0:1] + edge_sin[:, 1:2]
    imag_edge = edge_cos[:, 1:2] - edge_sin[:, 0:1]
    real_far = jnp.where(lane == 0, real_edge, next_cos[:, :HALF] - next_sin[:, HALF:])
    imag_far = jnp.where(lane == 0, imag_edge, -next_cos[:, HALF:] - next_sin[:, :HALF])
    white_far = wm_ref[...]
    order = q_ref[...]
    real_far = dot_nn((real_far * white_far).astype(jnp.bfloat16), order).astype(jnp.bfloat16)
    imag_far = dot_nn((imag_far * white_far).astype(jnp.bfloat16), order).astype(jnp.bfloat16)
    rows = NB // parts
    for f in range(parts):
        here = slice(f * rows, (f + 1) * rows)
        out_ref[f, 0, 0, :, :HALF] = real_out[here]
        out_ref[f, 0, 0, :, HALF:] = real_far[here]
        out_ref[f, 0, 1, :, :HALF] = imag_out[here]
        out_ref[f, 0, 1, :, HALF:] = imag_far[here]


def second_section(received, tables, white, white_far):
    parts, segs, rows, width = received.shape
    twists, seconds, order = tables

    def whole(array):
        return pl.BlockSpec(array.shape, lambda i: (0,) * array.ndim)

    fixed = (*twists, *seconds, white, white_far, order)
    return pl.pallas_call(
        second_kernel,
        grid=(segs,),
        in_specs=[pl.BlockSpec((parts, 1, rows, width), lambda i: (0, i, 0, 0))]
        + [whole(array) for array in fixed],
        out_specs=pl.BlockSpec((parts, 1, 2, NB // parts, A), lambda i: (0, i, 0, 0, 0)),
        out_shape=jax.ShapeDtypeStruct((parts, segs, 2, NB // parts, A), jnp.bfloat16),
        compiler_params=pltpu.CompilerParams(vmem_limit_bytes=60 * 2**20),
        cost_estimate=pl.CostEstimate(
            flops=2 * 6 * segs * 528 * B * A, bytes_accessed=segs * A * B * 6, transcendentals=0
        ),
        name="second_section",
    )(received, *fixed)


def lag_kernel(w_ref, t_ref, c_ref, s_ref, out_ref, acc_ref, p_ref, wf_ref):
    segs, _, blocks, _ = w_ref.shape
    quads = t_ref.shape[0]
    per_quad = blocks // quads
    lag_total = c_ref.shape[1]
    tmpl = out_ref.shape[2]
    step = pl.program_id(0)

    @pl.when(step == 0)
    def _():
        acc_ref[...] = jnp.zeros_like(acc_ref)

    unroll = 8

    @pl.loop(0, segs // unroll)
    def _(group):
        some = pl.ds(pl.multiple_of(group * unroll, unroll), unroll)
        for part in range(2):
            value = w_ref[some, part].astype(jnp.float32)
            wf_ref[part, :, some, :] = jnp.swapaxes(value, 0, 1)

    @pl.loop(0, quads)
    def _(quad):
        for jj in range(per_quad):
            block = quad * per_quad + jj
            for chunk in range(A // 128):
                lanes = slice(chunk * 128, (chunk + 1) * 128)
                lag_cos = c_ref[block, :, lanes]
                lag_sin = s_ref[block, :, lanes]
                out_lanes = slice(jj * A + chunk * 128, jj * A + (chunk + 1) * 128)

                @pl.loop(0, segs // unroll)
                def _(group):
                    some = pl.ds(pl.multiple_of(group * unroll, unroll), unroll)
                    reals = wf_ref[0, block, some, lanes]
                    imags = wf_ref[1, block, some, lanes]
                    for inner in range(unroll):
                        real = reals[inner : inner + 1]
                        imag = imags[inner : inner + 1]
                        first_row = (group * unroll + inner) * lag_total
                        rows = pl.ds(pl.multiple_of(first_row, lag_total), lag_total)
                        p_ref[0, rows, out_lanes] = (real * lag_cos - imag * lag_sin).astype(
                            jnp.bfloat16
                        )
                        p_ref[1, rows, out_lanes] = (real * lag_sin + imag * lag_cos).astype(
                            jnp.bfloat16
                        )

        for part in range(2):
            acc_ref[part] += dot_nt(p_ref[part], t_ref[quad])

    @pl.when(step == pl.num_programs(0) - 1)
    def _():
        shape = (segs, lag_total, tmpl)
        out_ref[:, :lag_total] = (acc_ref[0, :, :tmpl] + acc_ref[1, :, tmpl:]).reshape(shape)
        out_ref[:, lag_total:] = (acc_ref[1, :, :tmpl] - acc_ref[0, :, tmpl:]).reshape(shape)


def lag_products(data, laid, lag_cos, lag_sin):
    segs, _, blocks, _ = data.shape
    quads, tmpl2, depth = laid.shape
    per_quad = depth // A
    per_step = min(16, blocks)
    steps = blocks // per_step
    lag_total = lag_cos.shape[1]
    return pl.pallas_call(
        lag_kernel,
        grid=(steps,),
        in_specs=[
            pl.BlockSpec((segs, 2, per_step, A), lambda i: (0, 0, i, 0)),
            pl.BlockSpec((per_step // per_quad, tmpl2, depth), lambda i: (i, 0, 0)),
            pl.BlockSpec((per_step, lag_total, A), lambda i: (i, 0, 0)),
            pl.BlockSpec((per_step, lag_total, A), lambda i: (i, 0, 0)),
        ],
        out_specs=pl.BlockSpec((segs, 2 * lag_total, tmpl2 // 2), lambda i: (0, 0, 0)),
        out_shape=jax.ShapeDtypeStruct((segs, 2 * lag_total, tmpl2 // 2), jnp.float32),
        scratch_shapes=[
            pltpu.VMEM((2, segs * lag_total, tmpl2), jnp.float32),
            pltpu.VMEM((2, segs * lag_total, depth), jnp.bfloat16),
            pltpu.VMEM((2, per_step, segs, A), jnp.float32),
        ],
        compiler_params=pltpu.CompilerParams(vmem_limit_bytes=60 * 2**20),
        cost_estimate=pl.CostEstimate(
            flops=4 * segs * lag_total * tmpl2 * blocks * A,
            bytes_accessed=blocks * A * (tmpl2 * 2 + segs * 4),
            transcendentals=0,
        ),
        name="lag_products",
    )(data, laid, lag_cos, lag_sin)


def general_transform(strain, psd):
    freq_count = lax.axis_size("freq")
    freq_index = lax.axis_index("freq")
    seg_local = strain.shape[0]
    step_time = B // freq_count
    highest = lax.Precision.HIGHEST
    first_cos, first_sin = cos_sin_table(
        jnp.arange(A, dtype=jnp.int32), jnp.arange(A, dtype=jnp.int32), A
    )
    table = jnp.concatenate([first_cos, -first_sin], axis=0)
    time_ids = freq_index * step_time + jnp.arange(step_time, dtype=jnp.int32)
    twist_cos, twist_sin = cos_sin_table(jnp.arange(A, dtype=jnp.int32), time_ids, LEN)
    slab_blocks = strain.reshape(seg_local, A // freq_count, B)
    both_parts = jnp.einsum(
        "kn,snb->skb",
        table,
        lax.all_to_all(slab_blocks, "freq", split_axis=2, concat_axis=1, tiled=True),
        precision=highest,
    )
    real_part = both_parts[:, :A]
    imag_part = both_parts[:, A:]
    second_cos, second_sin = cos_sin_table(
        jnp.arange(B, dtype=jnp.int32), jnp.arange(NB, dtype=jnp.int32), B
    )
    rotation = jnp.concatenate(
        [
            jnp.concatenate([second_cos, -second_sin], axis=1),
            jnp.concatenate([second_sin, second_cos], axis=1),
        ],
        axis=0,
    )
    amplitude = jnp.sqrt(LEN * psd)
    real_in = lax.all_to_all(
        real_part * twist_cos + imag_part * twist_sin, "freq", split_axis=1, concat_axis=2, tiled=True
    )
    imag_in = lax.all_to_all(
        imag_part * twist_cos - real_part * twist_sin, "freq", split_axis=1, concat_axis=2, tiled=True
    )
    joined = jnp.concatenate([real_in, imag_in], axis=2)
    both_out = jnp.einsum("spc,cm->smp", joined, rotation, precision=highest)
    both_out = both_out.reshape(joined.shape[0], 2, NB, joined.shape[1])
    whitened = (both_out / amplitude).astype(jnp.bfloat16)
    return lax.all_to_all(whitened, "freq", split_axis=2, concat_axis=3, tiled=True)


def sliced_transform(strain, tables, white, white_far):
    freq_count = lax.axis_size("freq")
    seg_local = strain.shape[0]
    first, second = tables
    width = B // freq_count
    sent = (strain * STRAIN_SCALE).astype(jnp.float16)
    sent = sent.reshape(seg_local, A // freq_count, freq_count, width).transpose(2, 0, 1, 3)
    received = lax.all_to_all(sent, "freq", split_axis=0, concat_axis=0, tiled=True)
    received = received.astype(jnp.float32) * (1.0 / STRAIN_SCALE)
    coefs = first_section(received, first)
    sent = (coefs * COEF_SCALE).astype(jnp.float16).reshape(freq_count, seg_local // freq_count, A, width)
    received = lax.all_to_all(sent, "freq", split_axis=0, concat_axis=0, tiled=True)
    received = received.astype(jnp.float32) * (1.0 / COEF_SCALE)
    whitened = second_section(received, second, white, white_far)
    local_data = lax.all_to_all(whitened, "freq", split_axis=0, concat_axis=0, tiled=True)
    return local_data.reshape(seg_local, 2, NB // freq_count, A)


def on_device(strain, psd, templates, cutoffs, lags):
    freq_count = lax.axis_size("freq")
    freq_index = lax.axis_index("freq")
    seg_local = strain.shape[0]
    tmpl_local = templates.shape[0]
    blocks_here = templates.shape[2]
    lag_total = lags.shape[0]
    first_block = freq_index * blocks_here
    block_ids = first_block + jnp.arange(blocks_here, dtype=jnp.int32)

    per_quad = min(4, blocks_here)
    quads = blocks_here // per_quad
    keep = block_ids[None, :] < cutoffs[:, None]
    masked = jnp.where(keep[:, None, :, None], templates, jnp.bfloat16(0))
    laid = masked.reshape(tmpl_local, 2, quads, per_quad, A).transpose(2, 1, 0, 3, 4)
    laid = laid.reshape(quads, 2 * tmpl_local, per_quad * A)

    block_cos, block_sin = cos_sin_table(block_ids, lags % B, B)
    place = lags[:, None] * jnp.arange(A, dtype=jnp.int32)[None, :] % LEN
    place_angle = place.astype(jnp.float32) * (two_pi / LEN)
    place_cos = jnp.cos(place_angle)[None]
    place_sin = jnp.sin(place_angle)[None]
    block_cos = block_cos[:, :, None]
    block_sin = block_sin[:, :, None]
    lag_cos = block_cos * place_cos - block_sin * place_sin
    lag_sin = block_sin * place_cos + block_cos * place_sin

    sliced = seg_local % freq_count == 0 and (NB // freq_count) % 16 == 0 and B // freq_count == 128
    if not sliced:
        data = lax.all_gather(general_transform(strain, psd), "tmpl", axis=0, tiled=True)
        sums = lag_products(data, laid, lag_cos, lag_sin)
        return lax.psum_scatter(sums, "freq", scatter_dimension=0, tiled=True)

    order = mirror_table()
    psd_all = lax.all_gather(psd, "freq", axis=1, tiled=True)
    psd_far = jnp.dot(psd_all[:, HALF:], order.T, precision=lax.Precision.HIGHEST)
    white = lax.rsqrt(LEN * psd_all[:, :HALF])
    white_far = lax.rsqrt(LEN * psd_far)
    tables = (first_table(), (twist_tables(), second_tables(), order.astype(ml_dtypes.bfloat16)))

    group_total = seg_local // freq_count
    seg_out = seg_local * lax.axis_size("tmpl") // freq_count
    owners = seg_local // seg_out
    by_owner = strain.reshape(owners, group_total, seg_out // group_total, strain.shape[1])
    outputs = []
    for group in range(group_total):
        part = by_owner[:, group].reshape(seg_local // group_total, strain.shape[1])
        whitened = sliced_transform(part, tables, white, white_far)
        data = lax.all_gather(whitened, "tmpl", axis=0, tiled=True)
        sums = lag_products(data, laid, lag_cos, lag_sin)
        outputs.append(lax.psum_scatter(sums, "freq", scatter_dimension=0, tiled=True))
    return jnp.concatenate(outputs, axis=0)


def solution(mesh):
    placed = (P("tmpl", "freq"), P(None, "freq"), P("tmpl", None, "freq", None), P("tmpl"), P())
    return jax.shard_map(
        on_device, mesh=mesh, in_specs=placed, out_specs=P("freq", None, "tmpl"), check_vma=False
    )
```

time: 3410 us -> 583 us (0.17)
  other arithmetic: 2000 us -> 38.5 us
  matrix products: 491 us -> 2.85 us
  local copies, waits for them, and re-layouts: 412 us -> 136 us
  Pallas kernels: 0 us -> 175 us
  waiting for transfers between devices: 315 us -> 163 us
  loops' own time: 88.3 us -> 0 us
    another operation x128 -> x0, other arithmetic: 1120 us -> none  [one_span(): jnp.stack([real_rows, imag_rows], axis=1)]
    dot_general x130 -> x1, matrix products: 491 us -> 2.85 us  [on_device(): jnp.dot(psd_all[:, HALF:], order.T, precision=lax.Precision.HIGHEST)]
    neg x66 -> x0, other arithmetic: 320 us -> none  [the longest x64 307 us: one_span(): imag_rows = jnp.stack([imag_q, -real_q], axis=2)]
    convert_element_type x192 -> x1, other arithmetic: 239 us -> 4.17 us  [sliced_transform(): sent = (strain * STRAIN_SCALE).astype(jnp.float16)]
    add x66 -> x2, other arithmetic: 202 us -> 2.6 us  [the longest x1 2.6 us: on_device(): lag_sin = block_sin * place_cos + block_cos * place_sin]
    while x64 -> x0, local copies, waits for them, and re-layouts: 200 us -> none
    pallas_call x0 -> x6, Pallas kernels: none -> 175 us  [the longest x2 149 us: lag_products(): pl.pallas_call(lag_kernel, grid=(steps,), in_specs=[pl.BlockSpec((segs, 2...]
    all_to_all x3 -> x5, waiting for transfers between devices: 241 us -> 131 us  [the longest x3 81.4 us: sliced_transform(): lax.all_to_all(sent, 'freq', split_axis=0, concat_axis=0, tiled=True)]
  transfers between devices with their start and end apart: 5 -> 10, of which waited for: 5 -> 6; matrix products, arithmetic and copies ran while one was open for 2% -> 28% of each run, Pallas kernels for 0% -> 28%
where the time goes in v1:
time: 583 us; the launch traced here: 580 us
  Pallas kernels  175 us (30%)
  waiting for transfers between devices  163 us (28%)
  local copies, waits for them, and re-layouts  136 us (23%)
  other arithmetic  38.5 us (7%)
  blocking collectives  29 us (5%)
  starting transfers between devices  21.3 us (4%)
  between operations  13.4 us (2%)
    pallas_call x2, Pallas kernels, lag_products(): pl.pallas_call(lag_kernel, grid=(steps,), in_specs=[pl.BlockSpec((segs, 2...  149 us
    all_to_all x3, waiting for transfers between devices, sliced_transform(): lax.all_to_all(sent, 'freq', split_axis=0, concat_axis=0, tiled=True)  81.4 us
    reshape x2, local copies, waits for them, and re-layouts, on_device(): masked.reshape(tmpl_local, 2, quads, per_quad, A).transpose(2, 1, 0, 3, 4)  69.8 us
    reshape x1, local copies, waits for them, and re-layouts, on_device(): laid = laid.reshape(quads, 2 * tmpl_local, per_quad * A)  54 us
    all_to_all x2, waiting for transfers between devices, sliced_transform(): lax.all_to_all(whitened, 'freq', split_axis=0, concat_axis=0, tiled=True)  49.3 us
    reduce_scatter x2, waiting for transfers between devices, on_device(): lax.psum_scatter(sums, 'freq', scatter_dimension=0, tiled=True)  31 us
    all_to_all x1, blocking collectives, sliced_transform(): lax.all_to_all(sent, 'freq', split_axis=0, concat_axis=0, tiled=True)  29 us
    select_n x1, other arithmetic, on_device(): masked = jnp.where(keep[:, None, :, None], templates, jnp.bfloat16(0))  23.6 us
  transfers between devices with their start and end apart: 10, of which 6 were waited for; matrix products, arithmetic and copies ran while one was open for 28% of the time, Pallas kernels for 28%

profile of v1, /device:TPU:0, one launch (start us, length us, event | category | flops | bytes accessed | tf_op | source)
XLA Modules:
  0.0 579.5 jit_solution(8154774897739767917)
XLA Ops:
  6.5 4.2 reshape.176
  10.7 4.2 fusion.3
  14.9 1.1 convert_element_type.60
  16.0 1.3 copy.50
  17.3 6.3 %all-to-all-start.3 = ((f16[8,8,64,128]{3,2,1,0:T(8,128)(2,1)}), f16[8,8,64,128]{3,2,1,0:T(8,128)(2,1)S(1)}, u32[]{:S(2)}, u32[]{:S(2)}) async-start(f16[8,8,64,128]{3,2,1,0:T(8,128)(2,1)} %bitcast.36), calls=%async_computation.4 | async-start | bytes 2097152 | tf_op jit(solution)/shard_map/all_to_all | solution.py:335
  23.7 0.0 copy-start.1
  23.7 0.0 all-gather.6.cloned.1.call-start
  23.7 0.7 all-gather.6.cloned.1.call-update
  24.4 34.3 %all-to-all-done.3 = f16[8,8,64,128]{3,2,1,0:T(8,128)(2,1)S(1)} async-done(((f16[8,8,64,128]{3,2,1,0:T(8,128)(2,1)}), f16[8,8,64,128]{3,2,1,0:T(8,128)(2,1)S(1)}, u32[]{:S(2)}, u32[]{:S(2)}) %all-to-all-start.3) | async-done | bytes 1048608 | tf_op jit(solution)/shard_map/all_to_all | solution.py:335
  58.7 0.3 convert_multiply_fusion.1.x_ref
  58.9 0.0 copy-done
  59.0 0.0 copy-done.1
  59.0 2.6 first_section.3
  61.5 1.2 fusion.7
  62.8 3.6 all-to-all-start.4
  66.3 0.0 copy-start.4
  66.3 0.0 all-gather.6.cloned.1.call-done
  66.4 1.1 slice.17
  67.5 0.2 copy.44
  67.7 0.9 multiply_rsqrt_fusion.wa_ref
  68.6 0.0 copy-done.4
  68.6 2.9 fusion.5.wm_ref
  71.4 21.4 %all-to-all-done.4 = f16[8,1,512,128]{3,2,1,0:T(8,128)(2,1)S(1)} async-done(((f16[8,1,512,128]{3,2,1,0:T(8,128)(2,1)}), f16[8,1,512,128]{3,2,1,0:T(8,128)(2,1)S(1)}, u32[]{:S(2)}, u32[]{:S(2)}) %all-to-all-start.4) | async-done | bytes 1048608 | tf_op jit(solution)/shard_map/all_to_all | solution.py:339
  92.8 1.5 convert_multiply_fusion.y_ref
  94.4 10.5 %second_section.3 = bf16[8,1,2,64,512]{4,3,2,1,0:T(8,128)(2,1)} custom-call(f32[8,1,512,128]{3,2,1,0:T(8,128)} %convert_multiply_fusion.y_ref, f32[256,1024]{1,0:T(8,128)} %constant.86.clone.tc_ref, f32[256,1024]{1,0:T(8,128)} %constant.87.clone.ts_ref, f32[1,1024]{1,0:T(1,128)} %constant.88.clone.ec_ref, f32[1,1024]{1,0:T(1,128)} %constant.89.clone.es_ref, ...), custom_call_target="tpu_custom_call" | custom-call | flops 3321888768 | bytes 3145728 | tf_op jit(solution)/shard_map/second_section/pallas_call | solution.py:177
  104.9 3.6 all-to-all-start.5
  108.5 2.2 convert_element_type.53
  110.7 1.3 copy.51
  112.0 23.0 %all-to-all-done.5 = bf16[8,1,2,64,512]{4,3,2,1,0:T(8,128)(2,1)S(1)} async-done(((bf16[8,1,2,64,512]{4,3,2,1,0:T(8,128)(2,1)}), bf16[8,1,2,64,512]{4,3,2,1,0:T(8,128)(2,1)S(1)}, u32[]{:S(2)}, u32[]{:S(2)}) %all-to-all-start.5) | async-done | bytes 1048608 | tf_op jit(solution)/shard_map/all_to_all | solution.py:342
  135.0 3.6 all-to-all-start
  138.5 0.2 all-gather.10.cloned.1.call-start
  138.8 0.0 copy-done.2
  138.8 0.5 all-gather.10.cloned.1.call-update
  139.3 25.8 %all-to-all-done = f16[8,8,64,128]{3,2,1,0:T(8,128)(2,1)S(1)} async-done(((f16[8,8,64,128]{3,2,1,0:T(8,128)(2,1)}), f16[8,8,64,128]{3,2,1,0:T(8,128)(2,1)S(1)}, u32[]{:S(2)}, u32[]{:S(2)}) %all-to-all-start) | async-done | bytes 1048608 | tf_op jit(solution)/shard_map/all_to_all | solution.py:335
  165.1 0.3 convert_multiply_fusion.3.x_ref
  165.3 2.6 first_section.2
  167.9 0.2 fusion.6
  168.1 29.0 %all_to_all.30 = f16[8,1,512,128]{3,2,1,0:T(8,128)(2,1)S(1)} all-to-all(f16[8,1,512,128]{3,2,1,0:T(8,128)(2,1)S(1)} %fusion.6), channel_id=1, replica_groups=mesh['tmpl'=4,'freq'=8] {'freq'}, dimensions={0} | all-to-all | bytes 2097152 | tf_op jit(solution)/shard_map/all_to_all | solution.py:339
  197.1 1.5 convert_multiply_fusion.2.y_ref
  198.7 10.5 %second_section.2 = bf16[8,1,2,64,512]{4,3,2,1,0:T(8,128)(2,1)} custom-call(f32[8,1,512,128]{3,2,1,0:T(8,128)} %convert_multiply_fusion.2.y_ref, f32[256,1024]{1,0:T(8,128)} %constant.86.clone.tc_ref, f32[256,1024]{1,0:T(8,128)} %constant.87.clone.ts_ref, f32[1,1024]{1,0:T(1,128)} %constant.88.clone.ec_ref, f32[1,1024]{1,0:T(1,128)} %constant.89.clone.es_ref, ...), custom_call_target="tpu_custom_call" | custom-call | flops 3321888768 | bytes 3145728 | tf_op jit(solution)/shard_map/second_section/pallas_call | solution.py:177
  209.2 3.7 all-to-all-start.2
  212.9 0.0 all-gather.8.cloned.1.call-start
  213.0 0.0 copy-done.5
  213.0 0.1 broadcast_compare_fusion
  213.1 26.3 %all-to-all-done.2 = bf16[8,1,2,64,512]{4,3,2,1,0:T(8,128)(2,1)S(1)} async-done(((bf16[8,1,2,64,512]{4,3,2,1,0:T(8,128)(2,1)}), bf16[8,1,2,64,512]{4,3,2,1,0:T(8,128)(2,1)S(1)}, u32[]{:S(2)}, u32[]{:S(2)}) %all-to-all-start.2) | async-done | bytes 1048608 | tf_op jit(solution)/shard_map/all_to_all | solution.py:342
  239.4 1.0 copy-done.3
  240.4 0.0 all-gather.8.cloned.1.call-update
  240.4 0.0 reduce-scatter.5.cloned.1.call-start
  240.5 23.6 %broadcast_select_fusion = bf16[256,2,64,512]{3,2,1,0:T(8,128)(2,1)} fusion(bf16[256,2,64,512]{3,2,1,0:T(8,128)(2,1)} %param.19, pred[256,64]{1,0:T(8,128)(4,1)S(1)} %broadcast_compare_fusion), kind=kLoop, calls=%fused_computation.1 | loop fusion | flops 16777216 | bytes 67125248 | tf_op jit(solution)/shard_map/jit(_where)/select_n | solution.py:359
  264.1 46.1 %reshape.179 = bf16[256,2,16,4,512]{4,3,2,1,0:T(4,128)(2,1)} reshape(bf16[256,2,64,512]{3,2,1,0:T(8,128)(2,1)} %broadcast_select_fusion) | data formatting | bytes 67108864 | tf_op jit(solution)/shard_map/reshape | solution.py:360
  310.2 23.6 %copy.49 = bf16[256,2,16,4,512]{4,3,0,1,2:T(4,128)(2,1)} copy(bf16[256,2,16,4,512]{4,3,2,1,0:T(4,128)(2,1)} %reshape.179) | data formatting | bytes 67108864 | tf_op jit(solution)/shard_map/reshape | solution.py:360
  333.8 54.0 %reshape.180.t_ref = bf16[16,512,2048]{2,1,0:T(8,128)(2,1)} reshape(bf16[16,2,256,4,512]{4,3,2,1,0:T(4,128)(2,1)} %bitcast.38) | data formatting | bytes 67108864 | tf_op jit(solution)/shard_map/reshape | solution.py:361
  387.8 0.2 fusion.19
  388.0 0.2 fusion.21
  388.2 2.6 multiply_add_fusion
  390.8 74.6 %lag_products.3 = f32[32,32,256]{2,1,0:T(8,128)} custom-call(bf16[32,2,64,512]{3,2,1,0:T(8,128)(2,1)} %bitcast.40, bf16[16,512,2048]{2,1,0:T(8,128)(2,1)} %reshape.180.t_ref, f32[64,16,512]{2,1,0:T(8,128)} %get-tuple-element.8.c_ref, f32[64,16,512]{2,1,0:T(8,128)} %get-tuple-element.7.s_ref), custom_call_target="tpu_custom_call" | custom-call | flops 34359738368 | bytes 37748736 | tf_op jit(solution)/shard_map/lag_products/pallas_call | solution.py:257
  465.4 0.0 reduce-scatter.5.cloned.1.call-update
  465.5 0.3 reduce-scatter.3.cloned.1.call-start
  465.7 0.0 all-gather.8.cloned.1.call-done
  465.8 74.6 %lag_products.2 = f32[32,32,256]{2,1,0:T(8,128)} custom-call(bf16[32,2,64,512]{3,2,1,0:T(8,128)(2,1)} %bitcast.41, bf16[16,512,2048]{2,1,0:T(8,128)(2,1)} %reshape.180.t_ref, f32[64,16,512]{2,1,0:T(8,128)} %get-tuple-element.8.c_ref, f32[64,16,512]{2,1,0:T(8,128)} %get-tuple-element.7.s_ref), custom_call_target="tpu_custom_call" | custom-call | flops 34359738368 | bytes 37748736 | tf_op jit(solution)/shard_map/lag_products/pallas_call | solution.py:257
  540.3 0.0 reduce-scatter.3.cloned.1.call-update
  540.3 0.0 reduce-scatter.5.cloned.1.call-done
  540.4 31.0 %reduce-scatter.3.cloned.1.call-done = f32[4,32,256]{2,1,0:T(8,128)} async-done(((f32[32,32,256]{2,1,0:T(8,128)}), f32[4,32,256]{2,1,0:T(8,128)}) %reduce-scatter.3.cloned.1.call-update) | async-done | bytes 131088 | tf_op jit(solution)/shard_map/reduce_scatter | solution.py:396
  571.3 1.7 pad_maximum_fusion
  (9 shorter events, 0.0 us)
Async XLA Ops:
  17.3 41.3 %all-to-all-start.3 = ((f16[8,8,64,128]{3,2,1,0:T(8,128)(2,1)}), f16[8,8,64,128]{3,2,1,0:T(8,128)(2,1)S(1)}, u32[]{:S(2)}, u32[]{:S(2)}) async-start(f16[8,8,64,128]{3,2,1,0:T(8,128)(2,1)} %bitcast.36), calls=%async_computation.4 | async-start | bytes 2097152 | tf_op jit(solution)/shard_map/all_to_all | solution.py:335
  23.7 35.3 %copy-start = (bf16[512,512]{1,0:T(8,128)(2,1)S(1)}, bf16[512,512]{1,0:T(8,128)(2,1)}, u32[]{:S(2)}) copy-start(bf16[512,512]{1,0:T(8,128)(2,1)} %constant.84.clone.high_ref) | copy-start | bytes 1572868
  23.7 35.3 %copy-start.1 = (bf16[512,512]{1,0:T(8,128)(2,1)S(1)}, bf16[512,512]{1,0:T(8,128)(2,1)}, u32[]{:S(2)}) copy-start(bf16[512,512]{1,0:T(8,128)(2,1)} %constant.85.clone.low_ref) | copy-start | bytes 1572868
  23.7 42.7 %all-gather.6.cloned.1.call-start = ((), (), s32[]{:S(2)}) async-start(), calls=%async_computation.8 | async-start | bytes 1179648 | tf_op jit(solution)/shard_map/all_gather | solution.py:380
  62.8 30.1 %all-to-all-start.4 = ((f16[8,1,512,128]{3,2,1,0:T(8,128)(2,1)}), f16[8,1,512,128]{3,2,1,0:T(8,128)(2,1)S(1)}, u32[]{:S(2)}, u32[]{:S(2)}) async-start(f16[8,1,512,128]{3,2,1,0:T(8,128)(2,1)} %fusion.7), calls=%async_computation.5 | async-start | bytes 2097152 | tf_op jit(solution)/shard_map/all_to_all | solution.py:339
  66.3 2.3 copy-start.4
  104.9 30.1 %all-to-all-start.5 = ((bf16[8,1,2,64,512]{4,3,2,1,0:T(8,128)(2,1)}), bf16[8,1,2,64,512]{4,3,2,1,0:T(8,128)(2,1)S(1)}, u32[]{:S(2)}, u32[]{:S(2)}) async-start(bf16[8,1,2,64,512]{4,3,2,1,0:T(8,128)(2,1)} %second_section.3), calls=%async_computation.6 | async-start | bytes 2097152 | tf_op jit(solution)/shard_map/all_to_all | solution.py:342
  135.0 3.8 copy-start.2
  135.0 30.1 %all-to-all-start = ((f16[8,8,64,128]{3,2,1,0:T(8,128)(2,1)}), f16[8,8,64,128]{3,2,1,0:T(8,128)(2,1)S(1)}, u32[]{:S(2)}, u32[]{:S(2)}) async-start(f16[8,8,64,128]{3,2,1,0:T(8,128)(2,1)} %bitcast.39), calls=%async_computation | async-start | bytes 2097152 | tf_op jit(solution)/shard_map/all_to_all | solution.py:335
  138.5 252.3 %all-gather.10.cloned.1.call-start = ((), (), s32[]{:S(2)}) async-start(), calls=%async_computation.12 | async-start | bytes 5242880 | tf_op jit(solution)/shard_map/all_gather | solution.py:394
  209.2 3.8 copy-start.5
  209.2 30.2 %all-to-all-start.2 = ((bf16[8,1,2,64,512]{4,3,2,1,0:T(8,128)(2,1)}), bf16[8,1,2,64,512]{4,3,2,1,0:T(8,128)(2,1)S(1)}, u32[]{:S(2)}, u32[]{:S(2)}) async-start(bf16[8,1,2,64,512]{4,3,2,1,0:T(8,128)(2,1)} %second_section.2), calls=%async_computation.2 | async-start | bytes 2097152 | tf_op jit(solution)/shard_map/all_to_all | solution.py:342
  212.9 252.8 %all-gather.8.cloned.1.call-start = ((), (), s32[]{:S(2)}) async-start(), calls=%async_computation.11 | async-start | bytes 5242880 | tf_op jit(solution)/shard_map/all_gather | solution.py:394
  239.4 1.0 copy-start.3
  240.4 299.9 %reduce-scatter.5.cloned.1.call-start = ((), (), s32[]{:S(2)}) async-start(), calls=%async_computation.10 | async-start | bytes 1179648 | tf_op jit(solution)/shard_map/reduce_scatter | solution.py:396
  333.8 54.0 %copy-start.6 = (s32[16]{0:T(128)S(1)}, s32[16]{0:T(128)}, u32[]{:S(2)}) copy-start(s32[16]{0:T(128)} %param.21) | copy-start | bytes 196
  465.5 105.9 %reduce-scatter.3.cloned.1.call-start = ((), (), s32[]{:S(2)}) async-start(), calls=%async_computation.9 | async-start | bytes 1179648 | tf_op jit(solution)/shard_map/reduce_scatter | solution.py:396
Sparse Core Ops, SparseCore 0:
  26.1 33.2 all-gather.5
  141.2 54.0 all-gather.9
  240.6 51.5 all-gather.7
  465.6 30.8 reduce-scatter.4
  540.5 30.8 reduce-scatter.2

commit v2 on v1

--- a/solution.py
+++ b/solution.py
@@ -189,58 +189,67 @@
     )(received, *fixed)
 
 
-def lag_kernel(w_ref, t_ref, c_ref, s_ref, out_ref, acc_ref, p_ref, wf_ref):
+def lag_kernel(w_ref, t_ref, c_ref, s_ref, out_ref, acc_ref, even_ref, odd_ref, wf_ref):
     segs, _, blocks, _ = w_ref.shape
-    quads = t_ref.shape[0]
-    per_quad = blocks // quads
+    depth = t_ref.shape[2]
+    per_quad = depth // A
     lag_total = c_ref.shape[1]
     tmpl = out_ref.shape[2]
     step = pl.program_id(0)
+    last = pl.num_programs(0) - 1
+    unroll = 8
+
+    def make_rows(rows_ref, quad, jj):
+        block = quad * per_quad + jj
+        for chunk in range(A // 128):
+            lanes = slice(chunk * 128, (chunk + 1) * 128)
+            lag_cos = c_ref[block, :, lanes]
+            lag_sin = s_ref[block, :, lanes]
+            out_lanes = slice(jj * A + chunk * 128, jj * A + (chunk + 1) * 128)
+            for group in range(segs // unroll):
+                some = slice(group * unroll, (group + 1) * unroll)
+                reals = wf_ref[0, block, some, lanes]
+                imags = wf_ref[1, block, some, lanes]
+                for inner in range(unroll):
+                    real = reals[inner : inner + 1]
+                    imag = imags[inner : inner + 1]
+                    first_row = (group * unroll + inner) * lag_total
+                    rows = slice(first_row, first_row + lag_total)
+                    rows_ref[0, rows, out_lanes] = (real * lag_cos - imag * lag_sin).astype(jnp.bfloat16)
+                    rows_ref[1, rows, out_lanes] = (real * lag_sin + imag * lag_cos).astype(jnp.bfloat16)
 
     @pl.when(step == 0)
     def _():
         acc_ref[...] = jnp.zeros_like(acc_ref)
 
-    unroll = 8
-
-    @pl.loop(0, segs // unroll)
-    def _(group):
-        some = pl.ds(pl.multiple_of(group * unroll, unroll), unroll)
+        @pl.loop(0, segs // unroll)
+        def _(group):
+            some = pl.ds(pl.multiple_of(group * unroll, unroll), unroll)
+            for part in range(2):
+                for first in range(0, blocks, 8):
+                    here = slice(first, first + 8)
+                    value = w_ref[some, part, here].astype(jnp.float32)
+                    wf_ref[part, here, some, :] = jnp.swapaxes(value, 0, 1)
+
+        for jj in range(per_quad):
+            make_rows(even_ref, 0, jj)
+
+    def both(now_ref, next_ref):
+        upcoming = jnp.minimum(step + 1, last)
+        for jj in range(per_quad):
+            make_rows(next_ref, upcoming, jj)
         for part in range(2):
-            value = w_ref[some, part].astype(jnp.float32)
-            wf_ref[part, :, some, :] = jnp.swapaxes(value, 0, 1)
-
-    @pl.loop(0, quads)
-    def _(quad):
-        for jj in range(per_quad):
-            block = quad * per_quad + jj
-            for chunk in range(A // 128):
-                lanes = slice(chunk * 128, (chunk + 1) * 128)
-                lag_cos = c_ref[block, :, lanes]
-                lag_sin = s_ref[block, :, lanes]
-                out_lanes = slice(jj * A + chunk * 128, jj * A + (chunk + 1) * 128)
-
-                @pl.loop(0, segs // unroll)
-                def _(group):
-                    some = pl.ds(pl.multiple_of(group * unroll, unroll), unroll)
-                    reals = wf_ref[0, block, some, lanes]
-                    imags = wf_ref[1, block, some, lanes]
-                    for inner in range(unroll):
-                        real = reals[inner : inner + 1]
-                        imag = imags[inner : inner + 1]
-                        first_row = (group * unroll + inner) * lag_total
-                        rows = pl.ds(pl.multiple_of(first_row, lag_total), lag_total)
-                        p_ref[0, rows, out_lanes] = (real * lag_cos - imag * lag_sin).astype(
-                            jnp.bfloat16
-                        )
-                        p_ref[1, rows, out_lanes] = (real * lag_sin + imag * lag_cos).astype(
-                            jnp.bfloat16
-                        )
-
-        for part in range(2):
-            acc_ref[part] += dot_nt(p_ref[part], t_ref[quad])
-
-    @pl.when(step == pl.num_programs(0) - 1)
+            acc_ref[part] += dot_nt(now_ref[part], t_ref[0])
+
+    @pl.when(step % 2 == 0)
+    def _():
+        both(even_ref, odd_ref)
+
+    @pl.when(step % 2 == 1)
+    def _():
+        both(odd_ref, even_ref)
+
+    @pl.when(step == last)
     def _():
         shape = (segs, lag_total, tmpl)
         out_ref[:, :lag_total] = (acc_ref[0, :, :tmpl] + acc_ref[1, :, tmpl:]).reshape(shape)
@@ -250,25 +259,24 @@
 def lag_products(data, laid, lag_cos, lag_sin):
     segs, _, blocks, _ = data.shape
     quads, tmpl2, depth = laid.shape
-    per_quad = depth // A
-    per_step = min(16, blocks)
-    steps = blocks // per_step
     lag_total = lag_cos.shape[1]
+    once = pl.Buffered(1)
     return pl.pallas_call(
         lag_kernel,
-        grid=(steps,),
+        grid=(quads,),
         in_specs=[
-            pl.BlockSpec((segs, 2, per_step, A), lambda i: (0, 0, i, 0)),
-            pl.BlockSpec((per_step // per_quad, tmpl2, depth), lambda i: (i, 0, 0)),
-            pl.BlockSpec((per_step, lag_total, A), lambda i: (i, 0, 0)),
-            pl.BlockSpec((per_step, lag_total, A), lambda i: (i, 0, 0)),
+            pl.BlockSpec(data.shape, lambda i: (0, 0, 0, 0), pipeline_mode=once),
+            pl.BlockSpec((1, tmpl2, depth), lambda i: (i, 0, 0)),
+            pl.BlockSpec(lag_cos.shape, lambda i: (0, 0, 0), pipeline_mode=once),
+            pl.BlockSpec(lag_sin.shape, lambda i: (0, 0, 0), pipeline_mode=once),
         ],
         out_specs=pl.BlockSpec((segs, 2 * lag_total, tmpl2 // 2), lambda i: (0, 0, 0)),
         out_shape=jax.ShapeDtypeStruct((segs, 2 * lag_total, tmpl2 // 2), jnp.float32),
         scratch_shapes=[
             pltpu.VMEM((2, segs * lag_total, tmpl2), jnp.float32),
             pltpu.VMEM((2, segs * lag_total, depth), jnp.bfloat16),
-            pltpu.VMEM((2, per_step, segs, A), jnp.float32),
+            pltpu.VMEM((2, segs * lag_total, depth), jnp.bfloat16),
+            pltpu.VMEM((2, blocks, segs, A), jnp.float32),
         ],
         compiler_params=pltpu.CompilerParams(vmem_limit_bytes=60 * 2**20),
         cost_estimate=pl.CostEstimate(
@@ -280,6 +288,60 @@
     )(data, laid, lag_cos, lag_sin)
 
 
+def layout_kernel(cut_ref, t_ref, *refs):
+    out_ref = refs[-1]
+    tmpl, _, rows, _ = t_ref.shape
+    per_quad = out_ref.shape[3] // A
+    first_row = pl.program_id(0) * rows + cut_ref[cut_ref.shape[0] - 1]
+    first_tmpl = pl.program_id(1) * tmpl
+    row_ids = lax.broadcasted_iota(jnp.int32, (rows, 128), 0) + first_row
+    batch = 16
+
+    @pl.loop(0, tmpl // batch)
+    def _(group):
+        some = pl.ds(pl.multiple_of(group * batch, batch), batch)
+        keeps = [row_ids < cut_ref[first_tmpl + group * batch + n] for n in range(batch)]
+        for part in range(2):
+            for chunk in range(A // 128):
+                lanes = slice(chunk * 128, (chunk + 1) * 128)
+                value = t_ref[some, part, :, lanes].astype(jnp.float32)
+                value = jnp.stack([jnp.where(keeps[n], value[n], 0.0) for n in range(batch)], axis=0)
+                value = jnp.swapaxes(value, 0, 1).astype(jnp.bfloat16)
+                for row in range(rows):
+                    start = row % per_quad * A + chunk * 128
+                    out_ref[row // per_quad, part, some, start : start + 128] = value[row]
+
+
+def lay_out(templates, cuts, per_quad, piece, pieces, laid):
+    tmpl, _, blocks, _ = templates.shape
+    rows = min(16, blocks)
+    steps = blocks // rows // pieces
+    batch = min(64, tmpl)
+    shape = (blocks // per_quad, 2, tmpl, per_quad * A)
+    first = piece * steps
+    info = jnp.concatenate([cuts, jnp.full((1,), first * rows, jnp.int32)])
+    earlier = () if laid is None else (laid,)
+    return pl.pallas_call(
+        layout_kernel,
+        grid=(steps, tmpl // batch),
+        in_specs=[
+            pl.BlockSpec(memory_space=pltpu.SMEM),
+            pl.BlockSpec((batch, 2, rows, A), lambda i, j: (j, 0, i + first, 0)),
+        ]
+        + [pl.BlockSpec(memory_space=pl.ANY)] * len(earlier),
+        out_specs=pl.BlockSpec(
+            (rows // per_quad, 2, batch, per_quad * A), lambda i, j: (i + first, 0, j, 0)
+        ),
+        out_shape=jax.ShapeDtypeStruct(shape, jnp.bfloat16),
+        input_output_aliases={2: 0} if earlier else {},
+        compiler_params=pltpu.CompilerParams(vmem_limit_bytes=40 * 2**20),
+        cost_estimate=pl.CostEstimate(
+            flops=0, bytes_accessed=8 * tmpl * 2 * blocks * A // pieces, transcendentals=0
+        ),
+        name="lay_out",
+    )(info, templates, *earlier)
+
+
 def general_transform(strain, psd):
     freq_count = lax.axis_size("freq")
     freq_index = lax.axis_index("freq")
@@ -325,22 +387,26 @@
     return lax.all_to_all(whitened, "freq", split_axis=2, concat_axis=3, tiled=True)
 
 
-def sliced_transform(strain, tables, white, white_far):
-    freq_count = lax.axis_size("freq")
+def exchange(sent):
+    return lax.all_to_all(sent, "freq", split_axis=0, concat_axis=0, tiled=True)
+
+
+def pack_strain(strain, freq_count):
     seg_local = strain.shape[0]
-    first, second = tables
-    width = B // freq_count
     sent = (strain * STRAIN_SCALE).astype(jnp.float16)
-    sent = sent.reshape(seg_local, A // freq_count, freq_count, width).transpose(2, 0, 1, 3)
-    received = lax.all_to_all(sent, "freq", split_axis=0, concat_axis=0, tiled=True)
-    received = received.astype(jnp.float32) * (1.0 / STRAIN_SCALE)
-    coefs = first_section(received, first)
-    sent = (coefs * COEF_SCALE).astype(jnp.float16).reshape(freq_count, seg_local // freq_count, A, width)
-    received = lax.all_to_all(sent, "freq", split_axis=0, concat_axis=0, tiled=True)
-    received = received.astype(jnp.float32) * (1.0 / COEF_SCALE)
-    whitened = second_section(received, second, white, white_far)
-    local_data = lax.all_to_all(whitened, "freq", split_axis=0, concat_axis=0, tiled=True)
-    return local_data.reshape(seg_local, 2, NB // freq_count, A)
+    sent = sent.reshape(seg_local, A // freq_count, freq_count, B // freq_count)
+    return sent.transpose(2, 0, 1, 3)
+
+
+def pack_coefs(received, table):
+    freq_count, seg_local, _, width = received.shape
+    coefs = first_section(received.astype(jnp.float32) * (1.0 / STRAIN_SCALE), table)
+    sent = (coefs * COEF_SCALE).astype(jnp.float16)
+    return sent.reshape(freq_count, seg_local // freq_count, A, width)
+
+
+def whiten(received, tables, white, white_far):
+    return second_section(received.astype(jnp.float32) * (1.0 / COEF_SCALE), tables, white, white_far)
 
 
 def on_device(strain, psd, templates, cutoffs, lags):
@@ -349,16 +415,12 @@
     seg_local = strain.shape[0]
     tmpl_local = templates.shape[0]
     blocks_here = templates.shape[2]
-    lag_total = lags.shape[0]
     first_block = freq_index * blocks_here
     block_ids = first_block + jnp.arange(blocks_here, dtype=jnp.int32)
-
     per_quad = min(4, blocks_here)
     quads = blocks_here // per_quad
-    keep = block_ids[None, :] < cutoffs[:, None]
-    masked = jnp.where(keep[:, None, :, None], templates, jnp.bfloat16(0))
-    laid = masked.reshape(tmpl_local, 2, quads, per_quad, A).transpose(2, 1, 0, 3, 4)
-    laid = laid.reshape(quads, 2 * tmpl_local, per_quad * A)
+    cuts = cutoffs - first_block
+    tied = lax.optimization_barrier
 
     block_cos, block_sin = cos_sin_table(block_ids, lags % B, B)
     place = lags[:, None] * jnp.arange(A, dtype=jnp.int32)[None, :] % LEN
@@ -370,10 +432,14 @@
     lag_cos = block_cos * place_cos - block_sin * place_sin
     lag_sin = block_sin * place_cos + block_cos * place_sin
 
-    sliced = seg_local % freq_count == 0 and (NB // freq_count) % 16 == 0 and B // freq_count == 128
+    sliced = seg_local == 2 * freq_count and (NB // freq_count) % 32 == 0 and B // freq_count == 128
     if not sliced:
+        laid = lay_out(templates, cuts, per_quad, 0, 1, None)
+        laid = laid.reshape(quads, 2 * tmpl_local, per_quad * A)
         data = lax.all_gather(general_transform(strain, psd), "tmpl", axis=0, tiled=True)
-        sums = lag_products(data, laid, lag_cos, lag_sin)
+        half = data.shape[0] // 2
+        sums = [lag_products(part, laid, lag_cos, lag_sin) for part in (data[:half], data[half:])]
+        sums = jnp.concatenate(sums, axis=0)
         return lax.psum_scatter(sums, "freq", scatter_dimension=0, tiled=True)
 
     order = mirror_table()
@@ -381,17 +447,39 @@
     psd_far = jnp.dot(psd_all[:, HALF:], order.T, precision=lax.Precision.HIGHEST)
     white = lax.rsqrt(LEN * psd_all[:, :HALF])
     white_far = lax.rsqrt(LEN * psd_far)
-    tables = (first_table(), (twist_tables(), second_tables(), order.astype(ml_dtypes.bfloat16)))
-
-    group_total = seg_local // freq_count
+    first = first_table()
+    second = (twist_tables(), second_tables(), order.astype(ml_dtypes.bfloat16))
+
     seg_out = seg_local * lax.axis_size("tmpl") // freq_count
-    owners = seg_local // seg_out
-    by_owner = strain.reshape(owners, group_total, seg_out // group_total, strain.shape[1])
+    by_owner = strain.reshape(seg_local // seg_out, 2, seg_out // 2, strain.shape[1])
+    strain_a, strain_b = (
+        pack_strain(by_owner[:, group].reshape(seg_local // 2, strain.shape[1]), freq_count)
+        for group in range(2)
+    )
+    time_a = exchange(strain_a)
+    laid = lay_out(templates, cuts, per_quad, 0, 2, None)
+    time_a, strain_b, laid = tied((time_a, strain_b, laid))
+    time_b = exchange(strain_b)
+    coefs_a = pack_coefs(time_a, first)
+    laid = lay_out(templates, cuts, per_quad, 1, 2, laid)
+    time_b, coefs_a, laid = tied((time_b, coefs_a, laid))
+    parts_a = exchange(coefs_a)
+    coefs_b = pack_coefs(time_b, first)
+    parts_a, coefs_b, white, white_far, lag_cos, lag_sin = tied(
+        (parts_a, coefs_b, white, white_far, lag_cos, lag_sin)
+    )
+    parts_b = exchange(coefs_b)
+    white_a = whiten(parts_a, second, white, white_far)
+    parts_b, white_a = tied((parts_b, white_a))
+    data_a = exchange(white_a)
+    white_b = whiten(parts_b, second, white, white_far)
+    data_a, white_b = tied((data_a, white_b))
+    data_b = exchange(white_b)
+    laid = laid.reshape(quads, 2 * tmpl_local, per_quad * A)
     outputs = []
-    for group in range(group_total):
-        part = by_owner[:, group].reshape(seg_local // group_total, strain.shape[1])
-        whitened = sliced_transform(part, tables, white, white_far)
-        data = lax.all_gather(whitened, "tmpl", axis=0, tiled=True)
+    for data in (data_a, data_b):
+        data = data.reshape(seg_local // 2, 2, blocks_here, A)
+        data = lax.all_gather(data, "tmpl", axis=0, tiled=True)
         sums = lag_products(data, laid, lag_cos, lag_sin)
         outputs.append(lax.psum_scatter(sums, "freq", scatter_dimension=0, tiled=True))
     return jnp.concatenate(outputs, axis=0)

time: 583 us -> 408 us (0.70)
  local copies, waits for them, and re-layouts: 136 us -> 15 us
  waiting for transfers between devices: 163 us -> 112 us
  other arithmetic: 38.5 us -> 15.6 us
  Pallas kernels: 175 us -> 196 us
    reshape x4 -> x1, local copies, waits for them, and re-layouts: 128 us -> 4.16 us  [on_device(): strain.reshape(seg_local // seg_out, 2, seg_out // 2, strain.shape[1])]
    all_to_all x5, waiting for transfers between devices: 131 us -> 58.4 us  [exchange(): return lax.all_to_all(sent, 'freq', split_axis=0, concat_axis=0, tiled=True)]
    select_n x1 -> x0, other arithmetic: 23.6 us -> none  [on_device(): masked = jnp.where(keep[:, None, :, None], templates, jnp.bfloat16(0))]
    pallas_call x2 -> x4, Pallas kernels: 149 us -> 170 us  [the longest x2 136 us: lag_products(): pl.pallas_call(lag_kernel, grid=(quads,), in_specs=[pl.BlockSpec(data.sha...]
    all_gather x2, waiting for transfers between devices: 0.02 us -> 20.6 us  [on_device(): data = lax.all_gather(data, 'tmpl', axis=0, tiled=True)]
  transfers between devices with their start and end apart: 10 -> 10, of which waited for: 6 -> 7; matrix products, arithmetic and copies ran while one was open for 28% -> 5% of each run, Pallas kernels for 28% -> 48%
where the time goes in v2:
time: 408 us; the launch traced here: 407 us
  Pallas kernels  196 us (48%)
  waiting for transfers between devices  112 us (27%)
  blocking collectives  30.8 us (8%)
  starting transfers between devices  21.4 us (5%)
  other arithmetic  15.6 us (4%)
  local copies, waits for them, and re-layouts  15 us (4%)
  between operations  13.3 us (3%)
    pallas_call x2, Pallas kernels, lag_products(): pl.pallas_call(lag_kernel, grid=(quads,), in_specs=[pl.BlockSpec(data.sha...  136 us
    all_to_all x5, waiting for transfers between devices, exchange(): return lax.all_to_all(sent, 'freq', split_axis=0, concat_axis=0, tiled=True)  58.4 us
    pallas_call x2, Pallas kernels, lay_out(): pl.pallas_call(layout_kernel, grid=(steps, tmpl // batch), in_specs=[pl.B...  34.4 us
    reduce_scatter x2, waiting for transfers between devices, on_device(): lax.psum_scatter(sums, 'freq', scatter_dimension=0, tiled=True)  32.5 us
    all_to_all x1, blocking collectives, exchange(): return lax.all_to_all(sent, 'freq', split_axis=0, concat_axis=0, tiled=True)  30.8 us
    pallas_call x2, Pallas kernels, second_section(): pl.pallas_call(second_kernel, grid=(segs,), in_specs=[pl.BlockSpec((parts...  21.1 us
    all_to_all x5, starting transfers between devices, exchange(): return lax.all_to_all(sent, 'freq', split_axis=0, concat_axis=0, tiled=True)  20.7 us
    all_gather x2, waiting for transfers between devices, on_device(): data = lax.all_gather(data, 'tmpl', axis=0, tiled=True)  20.6 us
  transfers between devices with their start and end apart: 10, of which 7 were waited for; matrix products, arithmetic and copies ran while one was open for 5% of the time, Pallas kernels for 48%

profile of v2, /device:TPU:0, one launch (start us, length us, event | category | flops | bytes accessed | tf_op | source)
XLA Modules:
  0.0 407.4 jit_solution(16925386366993161898)
XLA Ops:
  6.5 4.2 %reshape.143 = f32[2,2,4,65536]{3,2,1,0:T(4,128)} reshape(f32[16,65536]{1,0:T(8,128)} %param.17) | data formatting | bytes 8388608 | tf_op jit(solution)/shard_map/reshape | solution.py:454
  10.7 3.2 fusion.1
  13.9 1.2 convert_element_type.53
  15.0 1.3 copy.47
  16.4 6.3 %all-to-all-start = ((f16[8,8,64,128]{3,2,1,0:T(8,128)(2,1)}), f16[8,8,64,128]{3,2,1,0:T(8,128)(2,1)S(1)}, u32[]{:S(2)}, u32[]{:S(2)}) async-start(f16[8,8,64,128]{3,2,1,0:T(8,128)(2,1)} %bitcast.32), calls=%async_computation | async-start | bytes 2097152 | tf_op jit(solution)/shard_map/all_to_all | solution.py:391
  22.7 0.0 copy-start.4
  22.7 1.2 convert_element_type.55
  23.9 1.3 copy.46
  25.2 0.0 copy-done.4
  25.2 17.2 %lay_out.2.refs_0_ = bf16[16,2,256,2048]{3,2,1,0:T(8,128)(2,1)} custom-call(s32[257]{0:T(512)S(1)} %get-tuple-element.44.cut_ref, bf16[256,2,64,512]{3,2,1,0:T(8,128)(2,1)} %t_ref.3), custom_call_target="tpu_custom_call" | custom-call | bytes 67108864 | tf_op jit(solution)/shard_map/lay_out/pallas_call | solution.py:324
  42.4 0.0 copy-start.5
  42.4 6.9 %all-to-all-done = f16[8,8,64,128]{3,2,1,0:T(8,128)(2,1)S(1)} async-done(((f16[8,8,64,128]{3,2,1,0:T(8,128)(2,1)}), f16[8,8,64,128]{3,2,1,0:T(8,128)(2,1)S(1)}, u32[]{:S(2)}, u32[]{:S(2)}) %all-to-all-start) | async-done | bytes 1048608 | tf_op jit(solution)/shard_map/all_to_all | solution.py:391
  49.3 3.6 all-to-all-start.1
  52.8 0.0 all-gather.6.cloned.1.call-start
  52.9 0.7 all-gather.6.cloned.1.call-update
  53.6 0.0 copy-done.5
  53.6 0.2 fusion.19
  53.8 17.2 %lay_out.3 = bf16[16,2,256,2048]{3,2,1,0:T(8,128)(2,1)} custom-call(s32[257]{0:T(512)S(1)} %get-tuple-element.43.cut_ref, bf16[256,2,64,512]{3,2,1,0:T(8,128)(2,1)} %t_ref.3, bf16[16,2,256,2048]{3,2,1,0:T(8,128)(2,1)} %lay_out.2.refs_0_), custom_call_target="tpu_custom_call", output_to_operand_aliasing={{}: (2, {})} | custom-call | bytes 67108864 | tf_op jit(solution)/shard_map/lay_out/pallas_call | solution.py:324
  71.1 0.0 copy-start.1
  71.1 0.3 convert_multiply_fusion.3.x_ref
  71.3 0.8 copy-done
  72.1 0.2 copy-done.1
  72.3 2.5 first_section.2
  74.8 1.2 fusion.6
  76.0 11.8 %all-to-all-done.1 = f16[8,8,64,128]{3,2,1,0:T(8,128)(2,1)S(1)} async-done(((f16[8,8,64,128]{3,2,1,0:T(8,128)(2,1)}), f16[8,8,64,128]{3,2,1,0:T(8,128)(2,1)S(1)}, u32[]{:S(2)}, u32[]{:S(2)}) %all-to-all-start.1) | async-done | bytes 1048608 | tf_op jit(solution)/shard_map/all_to_all | solution.py:391
  87.8 3.6 all-to-all-start.2
  91.4 0.2 fusion.21
  91.6 2.5 multiply_add_fusion
  94.1 0.0 copy-start.3
  94.1 0.0 all-gather.6.cloned.1.call-done
  94.1 1.9 slice.18
  96.0 2.0 copy.43
  98.0 1.9 multiply_rsqrt_fusion.wa_ref
  99.9 0.0 copy-done.3
  99.9 2.8 fusion.5.wm_ref
  102.8 0.3 convert_multiply_fusion.2.x_ref
  103.1 2.6 first_section.3
  105.6 1.2 fusion.7
  106.9 11.0 %all-to-all-done.2 = f16[8,1,512,128]{3,2,1,0:T(8,128)(2,1)S(1)} async-done(((f16[8,1,512,128]{3,2,1,0:T(8,128)(2,1)}), f16[8,1,512,128]{3,2,1,0:T(8,128)(2,1)S(1)}, u32[]{:S(2)}, u32[]{:S(2)}) %all-to-all-start.2) | async-done | bytes 1048608 | tf_op jit(solution)/shard_map/all_to_all | solution.py:391
  117.9 3.7 all-to-all-start.3
  121.6 1.5 convert_multiply_fusion.1.y_ref
  123.1 10.5 %second_section.2 = bf16[8,1,2,64,512]{4,3,2,1,0:T(8,128)(2,1)} custom-call(f32[8,1,512,128]{3,2,1,0:T(8,128)} %convert_multiply_fusion.1.y_ref, f32[256,1024]{1,0:T(8,128)} %constant.88.clone.tc_ref, f32[256,1024]{1,0:T(8,128)} %constant.89.clone.ts_ref, f32[1,1024]{1,0:T(1,128)} %constant.90.clone.ec_ref, f32[1,1024]{1,0:T(1,128)} %constant.91.clone.es_ref, ...), custom_call_target="tpu_custom_call" | custom-call | flops 3321888768 | bytes 3145728 | tf_op jit(solution)/shard_map/second_section/pallas_call | solution.py:177
  133.6 14.3 %all-to-all-done.3 = f16[8,1,512,128]{3,2,1,0:T(8,128)(2,1)S(1)} async-done(((f16[8,1,512,128]{3,2,1,0:T(8,128)(2,1)}), f16[8,1,512,128]{3,2,1,0:T(8,128)(2,1)S(1)}, u32[]{:S(2)}, u32[]{:S(2)}) %all-to-all-start.3) | async-done | bytes 1048608 | tf_op jit(solution)/shard_map/all_to_all | solution.py:391
  147.9 3.6 all-to-all-start.4
  151.5 0.0 all-gather.8.cloned.1.call-start
  151.6 1.5 convert_multiply_fusion.y_ref
  153.0 10.5 %second_section.3 = bf16[8,1,2,64,512]{4,3,2,1,0:T(8,128)(2,1)} custom-call(f32[8,1,512,128]{3,2,1,0:T(8,128)} %convert_multiply_fusion.y_ref, f32[256,1024]{1,0:T(8,128)} %constant.88.clone.tc_ref, f32[256,1024]{1,0:T(8,128)} %constant.89.clone.ts_ref, f32[1,1024]{1,0:T(1,128)} %constant.90.clone.ec_ref, f32[1,1024]{1,0:T(1,128)} %constant.91.clone.es_ref, ...), custom_call_target="tpu_custom_call" | custom-call | flops 3321888768 | bytes 3145728 | tf_op jit(solution)/shard_map/second_section/pallas_call | solution.py:177
  163.6 14.4 %all-to-all-done.4 = bf16[8,1,2,64,512]{4,3,2,1,0:T(8,128)(2,1)S(1)} async-done(((bf16[8,1,2,64,512]{4,3,2,1,0:T(8,128)(2,1)}), bf16[8,1,2,64,512]{4,3,2,1,0:T(8,128)(2,1)S(1)}, u32[]{:S(2)}, u32[]{:S(2)}) %all-to-all-start.4) | async-done | bytes 1048608 | tf_op jit(solution)/shard_map/all_to_all | solution.py:391
  178.0 1.0 copy-done.2
  179.0 0.0 all-gather.8.cloned.1.call-update
  179.0 0.0 all-gather.10.cloned.1.call-start
  179.1 30.8 %all_to_all.30 = bf16[8,1,2,64,512]{4,3,2,1,0:T(8,128)(2,1)} all-to-all(bf16[8,1,2,64,512]{4,3,2,1,0:T(8,128)(2,1)} %second_section.3), channel_id=1, replica_groups=mesh['tmpl'=4,'freq'=8] {'freq'}, dimensions={0} | all-to-all | bytes 2097152 | tf_op jit(solution)/shard_map/all_to_all | solution.py:391
  209.9 0.0 all-gather.10.cloned.1.call-update
  210.0 0.3 reduce-scatter.3.cloned.1.call-start
  210.2 20.6 %all-gather.8.cloned.1.call-done = bf16[32,1,2,64,512]{4,3,2,1,0:T(8,128)(2,1)} async-done(((bf16[8,1,2,64,512]{4,3,2,1,0:T(8,128)(2,1)}), bf16[32,1,2,64,512]{4,3,2,1,0:T(8,128)(2,1)}) %all-gather.8.cloned.1.call-update) | async-done | bytes 4194320 | tf_op jit(solution)/shard_map/all_gather | solution.py:482
  230.8 67.8 %lag_products.2 = f32[32,32,256]{2,1,0:T(8,128)} custom-call(bf16[32,2,64,512]{3,2,1,0:T(8,128)(2,1)} %bitcast.36, bf16[16,512,2048]{2,1,0:T(8,128)(2,1)} %bitcast.33, f32[64,16,512]{2,1,0:T(8,128)} %get-tuple-element.34.c_ref, f32[64,16,512]{2,1,0:T(8,128)} %get-tuple-element.35.s_ref), custom_call_target="tpu_custom_call" | custom-call | flops 34359738368 | bytes 37748736 | tf_op jit(solution)/shard_map/lag_products/pallas_call | solution.py:264
  298.6 0.0 reduce-scatter.3.cloned.1.call-update
  298.6 0.3 reduce-scatter.5.cloned.1.call-start
  298.9 0.0 all-gather.10.cloned.1.call-done
  298.9 67.8 %lag_products.3 = f32[32,32,256]{2,1,0:T(8,128)} custom-call(bf16[32,2,64,512]{3,2,1,0:T(8,128)(2,1)} %bitcast.35, bf16[16,512,2048]{2,1,0:T(8,128)(2,1)} %bitcast.34, f32[64,16,512]{2,1,0:T(8,128)} %get-tuple-element.34.c_ref, f32[64,16,512]{2,1,0:T(8,128)} %get-tuple-element.35.s_ref), custom_call_target="tpu_custom_call" | custom-call | flops 34359738368 | bytes 37748736 | tf_op jit(solution)/shard_map/lag_products/pallas_call | solution.py:264
  366.7 0.0 reduce-scatter.5.cloned.1.call-update
  366.7 0.0 reduce-scatter.3.cloned.1.call-done
  366.7 32.5 %reduce-scatter.5.cloned.1.call-done = f32[4,32,256]{2,1,0:T(8,128)} async-done(((f32[32,32,256]{2,1,0:T(8,128)}), f32[4,32,256]{2,1,0:T(8,128)}) %reduce-scatter.5.cloned.1.call-update) | async-done | bytes 131088 | tf_op jit(solution)/shard_map/reduce_scatter | solution.py:484
  399.2 1.7 pad_maximum_fusion
  (6 shorter events, 0.0 us)
Async XLA Ops:
  16.4 32.9 %all-to-all-start = ((f16[8,8,64,128]{3,2,1,0:T(8,128)(2,1)}), f16[8,8,64,128]{3,2,1,0:T(8,128)(2,1)S(1)}, u32[]{:S(2)}, u32[]{:S(2)}) async-start(f16[8,8,64,128]{3,2,1,0:T(8,128)(2,1)} %bitcast.32), calls=%async_computation | async-start | bytes 2097152 | tf_op jit(solution)/shard_map/all_to_all | solution.py:391
  22.7 2.5 copy-start.4
  42.4 11.2 %copy-start.5 = (s32[16]{0:T(128)S(1)}, s32[16]{0:T(128)}, u32[]{:S(2)}) copy-start(s32[16]{0:T(128)} %param.21) | copy-start | bytes 196
  49.3 38.5 %all-to-all-start.1 = ((f16[8,8,64,128]{3,2,1,0:T(8,128)(2,1)}), f16[8,8,64,128]{3,2,1,0:T(8,128)(2,1)S(1)}, u32[]{:S(2)}, u32[]{:S(2)}) async-start(f16[8,8,64,128]{3,2,1,0:T(8,128)(2,1)} %bitcast.31), calls=%async_computation.1 | async-start | bytes 2097152 | tf_op jit(solution)/shard_map/all_to_all | solution.py:391
  52.8 41.2 %all-gather.6.cloned.1.call-start = ((), (), s32[]{:S(2)}) async-start(), calls=%async_computation.8 | async-start | bytes 1179648 | tf_op jit(solution)/shard_map/all_gather | solution.py:446
  71.1 1.0 copy-start
  71.1 1.2 copy-start.1
  87.8 30.1 %all-to-all-start.2 = ((f16[8,1,512,128]{3,2,1,0:T(8,128)(2,1)}), f16[8,1,512,128]{3,2,1,0:T(8,128)(2,1)S(1)}, u32[]{:S(2)}, u32[]{:S(2)}) async-start(f16[8,1,512,128]{3,2,1,0:T(8,128)(2,1)} %fusion.6), calls=%async_computation.2 | async-start | bytes 2097152 | tf_op jit(solution)/shard_map/all_to_all | solution.py:391
  94.1 5.9 %copy-start.3 = (f32[256,256]{1,0:T(8,128)S(1)}, f32[256,256]{1,0:T(8,128)}, u32[]{:S(2)}) copy-start(f32[256,256]{1,0:T(8,128)} %constant.85.clone) | copy-start | bytes 786436
  117.9 30.1 %all-to-all-start.3 = ((f16[8,1,512,128]{3,2,1,0:T(8,128)(2,1)}), f16[8,1,512,128]{3,2,1,0:T(8,128)(2,1)S(1)}, u32[]{:S(2)}, u32[]{:S(2)}) async-start(f16[8,1,512,128]{3,2,1,0:T(8,128)(2,1)} %bitcast.5), calls=%async_computation.3 | async-start | bytes 2097152 | tf_op jit(solution)/shard_map/all_to_all | solution.py:391
  147.9 30.1 %all-to-all-start.4 = ((bf16[8,1,2,64,512]{4,3,2,1,0:T(8,128)(2,1)}), bf16[8,1,2,64,512]{4,3,2,1,0:T(8,128)(2,1)S(1)}, u32[]{:S(2)}, u32[]{:S(2)}) async-start(bf16[8,1,2,64,512]{4,3,2,1,0:T(8,128)(2,1)} %second_section.2), calls=%async_computation.4 | async-start | bytes 2097152 | tf_op jit(solution)/shard_map/all_to_all | solution.py:391
  151.5 79.3 %all-gather.8.cloned.1.call-start = ((), (), s32[]{:S(2)}) async-start(), calls=%async_computation.11 | async-start | bytes 5242880 | tf_op jit(solution)/shard_map/all_gather | solution.py:482
  178.0 1.0 copy-start.2
  179.0 119.9 %all-gather.10.cloned.1.call-start = ((), (), s32[]{:S(2)}) async-start(), calls=%async_computation.12 | async-start | bytes 5242880 | tf_op jit(solution)/shard_map/all_gather | solution.py:482
  210.0 156.8 %reduce-scatter.3.cloned.1.call-start = ((), (), s32[]{:S(2)}) async-start(), calls=%async_computation.9 | async-start | bytes 1179648 | tf_op jit(solution)/shard_map/reduce_scatter | solution.py:484
  298.6 100.6 %reduce-scatter.5.cloned.1.call-start = ((), (), s32[]{:S(2)}) async-start(), calls=%async_computation.10 | async-start | bytes 1179648 | tf_op jit(solution)/shard_map/reduce_scatter | solution.py:484
Sparse Core Ops, SparseCore 0:
  55.3 33.2 all-gather.5
  179.2 51.5 all-gather.7
  232.6 52.6 all-gather.9
  298.7 32.3 reduce-scatter.2
  366.8 32.3 reduce-scatter.4

commit v3 on v2

--- a/solution.py
+++ b/solution.py
@@ -197,6 +197,7 @@
     tmpl = out_ref.shape[2]
     step = pl.program_id(0)
     last = pl.num_programs(0) - 1
+    half = segs * lag_total
     unroll = 8
 
     def make_rows(rows_ref, quad, jj):
@@ -215,8 +216,9 @@
                     imag = imags[inner : inner + 1]
                     first_row = (group * unroll + inner) * lag_total
                     rows = slice(first_row, first_row + lag_total)
-                    rows_ref[0, rows, out_lanes] = (real * lag_cos - imag * lag_sin).astype(jnp.bfloat16)
-                    rows_ref[1, rows, out_lanes] = (real * lag_sin + imag * lag_cos).astype(jnp.bfloat16)
+                    rows_ref[rows, out_lanes] = (real * lag_cos - imag * lag_sin).astype(jnp.bfloat16)
+                    rows = slice(half + first_row, half + first_row + lag_total)
+                    rows_ref[rows, out_lanes] = (real * lag_sin + imag * lag_cos).astype(jnp.bfloat16)
 
     @pl.when(step == 0)
     def _():
@@ -236,10 +238,15 @@
 
     def both(now_ref, next_ref):
         upcoming = jnp.minimum(step + 1, last)
-        for jj in range(per_quad):
-            make_rows(next_ref, upcoming, jj)
-        for part in range(2):
-            acc_ref[part] += dot_nt(now_ref[part], t_ref[0])
+        cut = max(1, per_quad // 2)
+        pieces = [(k, n) for k in range(per_quad // cut) for n in range(2)]
+        for index, (k, n) in enumerate(pieces):
+            for jj in range(per_quad):
+                if jj * len(pieces) // per_quad == index:
+                    make_rows(next_ref, upcoming, jj)
+            deep = slice(k * cut * A, (k + 1) * cut * A)
+            cols = slice(n * tmpl, (n + 1) * tmpl)
+            acc_ref[:, cols] += dot_nt(now_ref[:, deep], t_ref[0, cols, deep])
 
     @pl.when(step % 2 == 0)
     def _():
@@ -252,8 +259,8 @@
     @pl.when(step == last)
     def _():
         shape = (segs, lag_total, tmpl)
-        out_ref[:, :lag_total] = (acc_ref[0, :, :tmpl] + acc_ref[1, :, tmpl:]).reshape(shape)
-        out_ref[:, lag_total:] = (acc_ref[1, :, :tmpl] - acc_ref[0, :, tmpl:]).reshape(shape)
+        out_ref[:, :lag_total] = (acc_ref[:half, :tmpl] + acc_ref[half:, tmpl:]).reshape(shape)
+        out_ref[:, lag_total:] = (acc_ref[half:, :tmpl] - acc_ref[:half, tmpl:]).reshape(shape)
 
 
 def lag_products(data, laid, lag_cos, lag_sin):
@@ -273,9 +280,9 @@
         out_specs=pl.BlockSpec((segs, 2 * lag_total, tmpl2 // 2), lambda i: (0, 0, 0)),
         out_shape=jax.ShapeDtypeStruct((segs, 2 * lag_total, tmpl2 // 2), jnp.float32),
         scratch_shapes=[
-            pltpu.VMEM((2, segs * lag_total, tmpl2), jnp.float32),
-            pltpu.VMEM((2, segs * lag_total, depth), jnp.bfloat16),
-            pltpu.VMEM((2, segs * lag_total, depth), jnp.bfloat16),
+            pltpu.VMEM((2 * segs * lag_total, tmpl2), jnp.float32),
+            pltpu.VMEM((2 * segs * lag_total, depth), jnp.bfloat16),
+            pltpu.VMEM((2 * segs * lag_total, depth), jnp.bfloat16),
             pltpu.VMEM((2, blocks, segs, A), jnp.float32),
         ],
         compiler_params=pltpu.CompilerParams(vmem_limit_bytes=60 * 2**20),
@@ -458,28 +465,29 @@
     )
     time_a = exchange(strain_a)
     laid = lay_out(templates, cuts, per_quad, 0, 2, None)
-    time_a, strain_b, laid = tied((time_a, strain_b, laid))
+    time_a, laid = tied((time_a, laid))
+    coefs_a = pack_coefs(time_a, first)
+    parts_a = exchange(coefs_a)
+    laid = lay_out(templates, cuts, per_quad, 1, 2, laid)
+    parts_a, strain_b, laid, white, white_far, lag_cos, lag_sin = tied(
+        (parts_a, strain_b, laid, white, white_far, lag_cos, lag_sin)
+    )
     time_b = exchange(strain_b)
-    coefs_a = pack_coefs(time_a, first)
-    laid = lay_out(templates, cuts, per_quad, 1, 2, laid)
-    time_b, coefs_a, laid = tied((time_b, coefs_a, laid))
-    parts_a = exchange(coefs_a)
+    white_a = whiten(parts_a, second, white, white_far)
+    time_b, white_a = tied((time_b, white_a))
+    data_a = exchange(white_a)
     coefs_b = pack_coefs(time_b, first)
-    parts_a, coefs_b, white, white_far, lag_cos, lag_sin = tied(
-        (parts_a, coefs_b, white, white_far, lag_cos, lag_sin)
-    )
+    data_a, coefs_b = tied((data_a, coefs_b))
     parts_b = exchange(coefs_b)
-    white_a = whiten(parts_a, second, white, white_far)
-    parts_b, white_a = tied((parts_b, white_a))
-    data_a = exchange(white_a)
+    data_a = data_a.reshape(seg_local // 2, 2, blocks_here, A)
+    data_a = lax.all_gather(data_a, "tmpl", axis=0, tiled=True)
     white_b = whiten(parts_b, second, white, white_far)
-    data_a, white_b = tied((data_a, white_b))
-    data_b = exchange(white_b)
+    data_a = tied((data_a, white_b))[0]
+    data_b = exchange(white_b).reshape(seg_local // 2, 2, blocks_here, A)
+    data_b = lax.all_gather(data_b, "tmpl", axis=0, tiled=True)
     laid = laid.reshape(quads, 2 * tmpl_local, per_quad * A)
     outputs = []
     for data in (data_a, data_b):
-        data = data.reshape(seg_local // 2, 2, blocks_here, A)
-        data = lax.all_gather(data, "tmpl", axis=0, tiled=True)
         sums = lag_products(data, laid, lag_cos, lag_sin)
         outputs.append(lax.psum_scatter(sums, "freq", scatter_dimension=0, tiled=True))
     return jnp.concatenate(outputs, axis=0)

time: 408 us -> 402 us (0.985)
  blocking collectives: 30.8 us -> 59.8 us
  waiting for transfers between devices: 112 us -> 87.2 us
    all_to_all x1 -> x2, blocking collectives: 30.8 us -> 59.8 us  [exchange(): return lax.all_to_all(sent, 'freq', split_axis=0, concat_axis=0, tiled=True)]
    all_gather x2, waiting for transfers between devices: 20.6 us -> 0.04 us  [the longest x1 0.02 us: on_device(): data_a = lax.all_gather(data_a, 'tmpl', axis=0, tiled=True)]
    all_to_all x5 -> x4, waiting for transfers between devices: 58.4 us -> 55 us  [exchange(): return lax.all_to_all(sent, 'freq', split_axis=0, concat_axis=0, tiled=True)]
    all_to_all x5 -> x4, starting transfers between devices: 20.7 us -> 18.5 us  [exchange(): return lax.all_to_all(sent, 'freq', split_axis=0, concat_axis=0, tiled=True)]
  transfers between devices with their start and end apart: 10 -> 9, of which waited for: 7 -> 4; matrix products, arithmetic and copies ran while one was open for 5% -> 4% of each run, Pallas kernels for 48% -> 48%
where the time goes in v3:
time: 402 us; the launch traced here: 401 us
  Pallas kernels  192 us (48%)
  waiting for transfers between devices  87.2 us (22%)
  blocking collectives  59.8 us (15%)
  starting transfers between devices  19.1 us (5%)
  other arithmetic  14.6 us (4%)
  between operations  13.4 us (3%)
  local copies, waits for them, and re-layouts  12.4 us (3%)
    pallas_call x2, Pallas kernels, lag_products(): pl.pallas_call(lag_kernel, grid=(quads,), in_specs=[pl.BlockSpec(data.sha...  132 us
    all_to_all x2, blocking collectives, exchange(): return lax.all_to_all(sent, 'freq', split_axis=0, concat_axis=0, tiled=True)  59.8 us
    all_to_all x4, waiting for transfers between devices, exchange(): return lax.all_to_all(sent, 'freq', split_axis=0, concat_axis=0, tiled=True)  55 us
    pallas_call x2, Pallas kernels, lay_out(): pl.pallas_call(layout_kernel, grid=(steps, tmpl // batch), in_specs=[pl.B...  34.5 us
    reduce_scatter x2, waiting for transfers between devices, on_device(): lax.psum_scatter(sums, 'freq', scatter_dimension=0, tiled=True)  31.4 us
    pallas_call x2, Pallas kernels, second_section(): pl.pallas_call(second_kernel, grid=(segs,), in_specs=[pl.BlockSpec((parts...  21.1 us
    all_to_all x4, starting transfers between devices, exchange(): return lax.all_to_all(sent, 'freq', split_axis=0, concat_axis=0, tiled=True)  18.5 us
  transfers between devices with their start and end apart: 9, of which 4 were waited for; matrix products, arithmetic and copies ran while one was open for 4% of the time, Pallas kernels for 48%

profile of v3, /device:TPU:0, one launch (start us, length us, event | category | flops | bytes accessed | tf_op | source)
XLA Modules:
  0.0 400.9 jit_solution(9831712356558576483)
XLA Ops:
  6.5 4.2 %reshape.143 = f32[2,2,4,65536]{3,2,1,0:T(4,128)} reshape(f32[16,65536]{1,0:T(8,128)} %param.17) | data formatting | bytes 8388608 | tf_op jit(solution)/shard_map/reshape | solution.py:461
  10.7 4.2 %fusion.1 = (f16[2,1,4,65536]{3,2,0,1:T(4,128)(2,1)}, f16[2,1,4,65536]{3,2,0,1:T(4,128)(2,1)S(1)}) fusion(f32[2,2,4,65536]{3,2,1,0:T(4,128)} %reshape.143), kind=kLoop, calls=%fused_computation.2 | loop fusion | flops 2097152 | bytes 6291456 | tf_op jit(solution)/shard_map/convert_element_type | solution.py:403
  14.9 1.1 convert_element_type.53
  16.0 0.0 copy-start.5
  16.0 1.3 copy.47
  17.3 6.3 %all-to-all-start = ((f16[8,8,64,128]{3,2,1,0:T(8,128)(2,1)}), f16[8,8,64,128]{3,2,1,0:T(8,128)(2,1)S(1)}, u32[]{:S(2)}, u32[]{:S(2)}) async-start(f16[8,8,64,128]{3,2,1,0:T(8,128)(2,1)} %bitcast.32), calls=%async_computation | async-start | bytes 2097152 | tf_op jit(solution)/shard_map/all_to_all | solution.py:398
  23.7 0.0 all-gather.6.cloned.1.call-start
  23.7 0.7 all-gather.6.cloned.1.call-update
  24.4 0.0 copy-done.5
  24.4 17.2 %lay_out.2.refs_0_ = bf16[16,2,256,2048]{3,2,1,0:T(8,128)(2,1)} custom-call(s32[257]{0:T(512)S(1)} %get-tuple-element.40.cut_ref, bf16[256,2,64,512]{3,2,1,0:T(8,128)(2,1)} %t_ref.3), custom_call_target="tpu_custom_call" | custom-call | bytes 67108864 | tf_op jit(solution)/shard_map/lay_out/pallas_call | solution.py:331
  41.6 0.0 copy-start
  41.6 17.1 %all-to-all-done = f16[8,8,64,128]{3,2,1,0:T(8,128)(2,1)S(1)} async-done(((f16[8,8,64,128]{3,2,1,0:T(8,128)(2,1)}), f16[8,8,64,128]{3,2,1,0:T(8,128)(2,1)S(1)}, u32[]{:S(2)}, u32[]{:S(2)}) %all-to-all-start) | async-done | bytes 1048608 | tf_op jit(solution)/shard_map/all_to_all | solution.py:398
  58.7 0.3 convert_multiply_fusion.3.x_ref
  59.0 0.0 copy-done
  59.0 0.0 copy-done.1
  59.0 2.6 first_section.2
  61.5 1.2 fusion.6
  62.8 3.6 all-to-all-start.1
  66.3 0.0 copy-start.6
  66.3 2.2 convert_element_type.57
  68.5 1.3 copy.46
  69.9 0.0 copy-done.6
  69.9 0.2 fusion.19
  70.1 0.2 fusion.21
  70.3 2.5 multiply_add_fusion
  72.8 1.1 slice.18
  73.9 0.2 copy.43
  74.1 0.0 copy-start.3
  74.1 0.0 copy-start.4
  74.1 17.3 %lay_out.3 = bf16[16,2,256,2048]{3,2,1,0:T(8,128)(2,1)} custom-call(s32[257]{0:T(512)S(1)} %get-tuple-element.39.cut_ref, bf16[256,2,64,512]{3,2,1,0:T(8,128)(2,1)} %t_ref.3, bf16[16,2,256,2048]{3,2,1,0:T(8,128)(2,1)} %lay_out.2.refs_0_), custom_call_target="tpu_custom_call", output_to_operand_aliasing={{}: (2, {})} | custom-call | bytes 67108864 | tf_op jit(solution)/shard_map/lay_out/pallas_call | solution.py:331
  91.4 0.9 multiply_rsqrt_fusion.wa_ref
  92.3 0.0 copy-done.3
  92.3 0.0 copy-done.4
  92.3 1.8 fusion.5.wm_ref
  94.1 0.0 all-to-all-done.1
  94.1 5.0 %all-to-all-start.2 = ((f16[8,8,64,128]{3,2,1,0:T(8,128)(2,1)}), f16[8,8,64,128]{3,2,1,0:T(8,128)(2,1)S(1)}, u32[]{:S(2)}, u32[]{:S(2)}) async-start(f16[8,8,64,128]{3,2,1,0:T(8,128)(2,1)} %bitcast.36), calls=%async_computation.2 | async-start | bytes 2097152 | tf_op jit(solution)/shard_map/all_to_all | solution.py:398
  99.2 1.5 convert_multiply_fusion.2.y_ref
  100.6 10.6 %second_section.2 = bf16[8,1,2,64,512]{4,3,2,1,0:T(8,128)(2,1)} custom-call(f32[8,1,512,128]{3,2,1,0:T(8,128)} %convert_multiply_fusion.2.y_ref, f32[256,1024]{1,0:T(8,128)} %constant.88.clone.tc_ref, f32[256,1024]{1,0:T(8,128)} %constant.89.clone.ts_ref, f32[1,1024]{1,0:T(1,128)} %constant.90.clone.ec_ref, f32[1,1024]{1,0:T(1,128)} %constant.91.clone.es_ref, ...), custom_call_target="tpu_custom_call" | custom-call | flops 3321888768 | bytes 3145728 | tf_op jit(solution)/shard_map/second_section/pallas_call | solution.py:177
  111.2 14.6 %all-to-all-done.2 = f16[8,8,64,128]{3,2,1,0:T(8,128)(2,1)S(1)} async-done(((f16[8,8,64,128]{3,2,1,0:T(8,128)(2,1)}), f16[8,8,64,128]{3,2,1,0:T(8,128)(2,1)S(1)}, u32[]{:S(2)}, u32[]{:S(2)}) %all-to-all-start.2) | async-done | bytes 1048608 | tf_op jit(solution)/shard_map/all_to_all | solution.py:398
  125.7 3.6 all-to-all-start.3
  129.3 0.0 all-gather.8.cloned.1.call-start
  129.4 0.3 convert_multiply_fusion.1.x_ref
  129.6 2.6 first_section.3
  132.2 0.2 fusion.7
  132.4 23.4 %all-to-all-done.3 = bf16[8,1,2,64,512]{4,3,2,1,0:T(8,128)(2,1)S(1)} async-done(((bf16[8,1,2,64,512]{4,3,2,1,0:T(8,128)(2,1)}), bf16[8,1,2,64,512]{4,3,2,1,0:T(8,128)(2,1)S(1)}, u32[]{:S(2)}, u32[]{:S(2)}) %all-to-all-start.3) | async-done | bytes 1048608 | tf_op jit(solution)/shard_map/all_to_all | solution.py:398
  155.8 1.0 copy-done.2
  156.8 0.0 all-gather.8.cloned.1.call-update
  156.8 0.0 all-gather.10.cloned.1.call-start
  156.9 29.0 %all_to_all.30 = f16[8,1,512,128]{3,2,1,0:T(8,128)(2,1)S(1)} all-to-all(f16[8,1,512,128]{3,2,1,0:T(8,128)(2,1)S(1)} %bitcast.35), channel_id=1, replica_groups=mesh['tmpl'=4,'freq'=8] {'freq'}, dimensions={0} | all-to-all | bytes 2097152 | tf_op jit(solution)/shard_map/all_to_all | solution.py:398
  185.9 1.5 convert_multiply_fusion.y_ref
  187.4 10.5 %second_section.3 = bf16[8,1,2,64,512]{4,3,2,1,0:T(8,128)(2,1)} custom-call(f32[8,1,512,128]{3,2,1,0:T(8,128)} %convert_multiply_fusion.y_ref, f32[256,1024]{1,0:T(8,128)} %constant.88.clone.tc_ref, f32[256,1024]{1,0:T(8,128)} %constant.89.clone.ts_ref, f32[1,1024]{1,0:T(1,128)} %constant.90.clone.ec_ref, f32[1,1024]{1,0:T(1,128)} %constant.91.clone.es_ref, ...), custom_call_target="tpu_custom_call" | custom-call | flops 3321888768 | bytes 3145728 | tf_op jit(solution)/shard_map/second_section/pallas_call | solution.py:177
  197.9 30.8 %all_to_all.31 = bf16[8,1,2,64,512]{4,3,2,1,0:T(8,128)(2,1)} all-to-all(bf16[8,1,2,64,512]{4,3,2,1,0:T(8,128)(2,1)} %second_section.3), channel_id=1, replica_groups=mesh['tmpl'=4,'freq'=8] {'freq'}, dimensions={0} | all-to-all | bytes 2097152 | tf_op jit(solution)/shard_map/all_to_all | solution.py:398
  228.7 0.0 all-gather.10.cloned.1.call-update
  228.8 0.3 reduce-scatter.3.cloned.1.call-start
  229.0 0.0 all-gather.8.cloned.1.call-done
  229.0 65.9 %lag_products.2 = f32[32,32,256]{2,1,0:T(8,128)} custom-call(bf16[32,2,64,512]{3,2,1,0:T(8,128)(2,1)} %bitcast.37, bf16[16,512,2048]{2,1,0:T(8,128)(2,1)} %bitcast.33, f32[64,16,512]{2,1,0:T(8,128)} %get-tuple-element.31.c_ref, f32[64,16,512]{2,1,0:T(8,128)} %get-tuple-element.32.s_ref), custom_call_target="tpu_custom_call" | custom-call | flops 34359738368 | bytes 37748736 | tf_op jit(solution)/shard_map/lag_products/pallas_call | solution.py:271
  294.9 0.0 reduce-scatter.3.cloned.1.call-update
  295.0 0.3 reduce-scatter.5.cloned.1.call-start
  295.3 0.0 all-gather.10.cloned.1.call-done
  295.3 65.9 %lag_products.3 = f32[32,32,256]{2,1,0:T(8,128)} custom-call(bf16[32,2,64,512]{3,2,1,0:T(8,128)(2,1)} %bitcast.38, bf16[16,512,2048]{2,1,0:T(8,128)(2,1)} %bitcast.34, f32[64,16,512]{2,1,0:T(8,128)} %get-tuple-element.31.c_ref, f32[64,16,512]{2,1,0:T(8,128)} %get-tuple-element.32.s_ref), custom_call_target="tpu_custom_call" | custom-call | flops 34359738368 | bytes 37748736 | tf_op jit(solution)/shard_map/lag_products/pallas_call | solution.py:271
  361.2 0.0 reduce-scatter.5.cloned.1.call-update
  361.2 0.0 reduce-scatter.3.cloned.1.call-done
  361.2 31.4 %reduce-scatter.5.cloned.1.call-done = f32[4,32,256]{2,1,0:T(8,128)} async-done(((f32[32,32,256]{2,1,0:T(8,128)}), f32[4,32,256]{2,1,0:T(8,128)}) %reduce-scatter.5.cloned.1.call-update) | async-done | bytes 131088 | tf_op jit(solution)/shard_map/reduce_scatter | solution.py:492
  392.7 1.7 pad_maximum_fusion
  (7 shorter events, 0.0 us)
Async XLA Ops:
  16.0 8.4 %copy-start.5 = (s32[256]{0:T(256)S(1)}, s32[256]{0:T(256)}, u32[]{:S(2)}) copy-start(s32[256]{0:T(256)} %param.20) | copy-start | bytes 3076
  17.3 41.3 %all-to-all-start = ((f16[8,8,64,128]{3,2,1,0:T(8,128)(2,1)}), f16[8,8,64,128]{3,2,1,0:T(8,128)(2,1)S(1)}, u32[]{:S(2)}, u32[]{:S(2)}) async-start(f16[8,8,64,128]{3,2,1,0:T(8,128)(2,1)} %bitcast.32), calls=%async_computation | async-start | bytes 2097152 | tf_op jit(solution)/shard_map/all_to_all | solution.py:398
  23.7 49.1 %all-gather.6.cloned.1.call-start = ((), (), s32[]{:S(2)}) async-start(), calls=%async_computation.8 | async-start | bytes 1179648 | tf_op jit(solution)/shard_map/all_gather | solution.py:453
  41.6 17.3 %copy-start = (bf16[512,512]{1,0:T(8,128)(2,1)S(1)}, bf16[512,512]{1,0:T(8,128)(2,1)}, u32[]{:S(2)}) copy-start(bf16[512,512]{1,0:T(8,128)(2,1)} %constant.86.clone.high_ref) | copy-start | bytes 1572868
  41.6 17.4 %copy-start.1 = (bf16[512,512]{1,0:T(8,128)(2,1)S(1)}, bf16[512,512]{1,0:T(8,128)(2,1)}, u32[]{:S(2)}) copy-start(bf16[512,512]{1,0:T(8,128)(2,1)} %constant.87.clone.low_ref) | copy-start | bytes 1572868
  62.8 31.4 %all-to-all-start.1 = ((f16[8,1,512,128]{3,2,1,0:T(8,128)(2,1)}), f16[8,1,512,128]{3,2,1,0:T(8,128)(2,1)S(1)}, u32[]{:S(2)}, u32[]{:S(2)}) async-start(f16[8,1,512,128]{3,2,1,0:T(8,128)(2,1)} %fusion.6), calls=%async_computation.1 | async-start | bytes 2097152 | tf_op jit(solution)/shard_map/all_to_all | solution.py:398
  66.3 3.6 copy-start.6
  74.1 18.2 %copy-start.3 = (f32[512,512]{0,1:T(8,128)S(1)}, f32[512,512]{0,1:T(8,128)}, u32[]{:S(2)}) copy-start(f32[512,512]{0,1:T(8,128)} %all-gather.6.cloned.1.call-done) | copy-start | bytes 3145732
  74.1 18.2 %copy-start.4 = (f32[256,256]{1,0:T(8,128)S(1)}, f32[256,256]{1,0:T(8,128)}, u32[]{:S(2)}) copy-start(f32[256,256]{1,0:T(8,128)} %constant.85.clone) | copy-start | bytes 786436
  94.1 31.6 %all-to-all-start.2 = ((f16[8,8,64,128]{3,2,1,0:T(8,128)(2,1)}), f16[8,8,64,128]{3,2,1,0:T(8,128)(2,1)S(1)}, u32[]{:S(2)}, u32[]{:S(2)}) async-start(f16[8,8,64,128]{3,2,1,0:T(8,128)(2,1)} %bitcast.36), calls=%async_computation.2 | async-start | bytes 2097152 | tf_op jit(solution)/shard_map/all_to_all | solution.py:398
  125.7 30.1 %all-to-all-start.3 = ((bf16[8,1,2,64,512]{4,3,2,1,0:T(8,128)(2,1)}), bf16[8,1,2,64,512]{4,3,2,1,0:T(8,128)(2,1)S(1)}, u32[]{:S(2)}, u32[]{:S(2)}) async-start(bf16[8,1,2,64,512]{4,3,2,1,0:T(8,128)(2,1)} %second_section.2), calls=%async_computation.3 | async-start | bytes 2097152 | tf_op jit(solution)/shard_map/all_to_all | solution.py:398
  129.3 99.7 %all-gather.8.cloned.1.call-start = ((), (), s32[]{:S(2)}) async-start(), calls=%async_computation.11 | async-start | bytes 5242880 | tf_op jit(solution)/shard_map/all_gather | solution.py:483
  155.8 1.0 copy-start.2
  156.8 138.5 %all-gather.10.cloned.1.call-start = ((), (), s32[]{:S(2)}) async-start(), calls=%async_computation.12 | async-start | bytes 5242880 | tf_op jit(solution)/shard_map/all_gather | solution.py:487
  228.8 132.5 %reduce-scatter.3.cloned.1.call-start = ((), (), s32[]{:S(2)}) async-start(), calls=%async_computation.9 | async-start | bytes 1179648 | tf_op jit(solution)/shard_map/reduce_scatter | solution.py:492
  295.0 97.7 %reduce-scatter.5.cloned.1.call-start = ((), (), s32[]{:S(2)}) async-start(), calls=%async_computation.10 | async-start | bytes 1179648 | tf_op jit(solution)/shard_map/reduce_scatter | solution.py:492
Sparse Core Ops, SparseCore 0:
  26.1 33.3 all-gather.5
  157.0 51.5 all-gather.7
  228.9 51.6 all-gather.9
  295.1 31.2 reduce-scatter.2
  361.3 31.2 reduce-scatter.4

commit v4 on v3

--- a/solution.py
+++ b/solution.py
@@ -189,93 +189,91 @@
     )(received, *fixed)
 
 
-def lag_kernel(w_ref, t_ref, c_ref, s_ref, out_ref, acc_ref, even_ref, odd_ref, wf_ref):
-    segs, _, blocks, _ = w_ref.shape
+def lag_kernel(place_ref, a_ref, b_ref, x_ref, y_ref, t_ref, c_ref, s_ref, out_ref, acc_ref, even_ref, odd_ref):
+    sources = (a_ref, b_ref, x_ref, y_ref)
+    segs = a_ref.shape[1] // 2
     depth = t_ref.shape[2]
     per_quad = depth // A
     lag_total = c_ref.shape[1]
     tmpl = out_ref.shape[2]
     step = pl.program_id(0)
     last = pl.num_programs(0) - 1
-    half = segs * lag_total
-    unroll = 8
-
-    def make_rows(rows_ref, quad, jj):
-        block = quad * per_quad + jj
+    half = len(sources) * segs * lag_total
+
+    def make_rows(rows_ref, jj):
         for chunk in range(A // 128):
             lanes = slice(chunk * 128, (chunk + 1) * 128)
-            lag_cos = c_ref[block, :, lanes]
-            lag_sin = s_ref[block, :, lanes]
+            lag_cos = c_ref[jj, :, lanes]
+            lag_sin = s_ref[jj, :, lanes]
             out_lanes = slice(jj * A + chunk * 128, jj * A + (chunk + 1) * 128)
-            for group in range(segs // unroll):
-                some = slice(group * unroll, (group + 1) * unroll)
-                reals = wf_ref[0, block, some, lanes]
-                imags = wf_ref[1, block, some, lanes]
-                for inner in range(unroll):
-                    real = reals[inner : inner + 1]
-                    imag = imags[inner : inner + 1]
-                    first_row = (group * unroll + inner) * lag_total
+            for index, source in enumerate(sources):
+                value = source[jj, :, lanes].astype(jnp.float32)
+                for s in range(segs):
+                    real = value[s : s + 1]
+                    imag = value[segs + s : segs + s + 1]
+                    first_row = (index * segs + s) * lag_total
                     rows = slice(first_row, first_row + lag_total)
                     rows_ref[rows, out_lanes] = (real * lag_cos - imag * lag_sin).astype(jnp.bfloat16)
                     rows = slice(half + first_row, half + first_row + lag_total)
                     rows_ref[rows, out_lanes] = (real * lag_sin + imag * lag_cos).astype(jnp.bfloat16)
 
+    def multiply(now_ref, next_ref):
+        cut = max(1, per_quad // 2)
+        pieces = [(k, n) for k in range(per_quad // cut) for n in range(2)]
+        for index, (k, n) in enumerate(pieces):
+            if next_ref is not None:
+                for jj in range(per_quad):
+                    if jj * len(pieces) // per_quad == index:
+                        make_rows(next_ref, jj)
+            deep = slice(k * cut * A, (k + 1) * cut * A)
+            cols = slice(n * tmpl, (n + 1) * tmpl)
+            acc_ref[:, cols] += dot_nt(now_ref[:, deep], t_ref[0, cols, deep])
+
     @pl.when(step == 0)
     def _():
         acc_ref[...] = jnp.zeros_like(acc_ref)
-
-        @pl.loop(0, segs // unroll)
-        def _(group):
-            some = pl.ds(pl.multiple_of(group * unroll, unroll), unroll)
-            for part in range(2):
-                for first in range(0, blocks, 8):
-                    here = slice(first, first + 8)
-                    value = w_ref[some, part, here].astype(jnp.float32)
-                    wf_ref[part, here, some, :] = jnp.swapaxes(value, 0, 1)
-
         for jj in range(per_quad):
-            make_rows(even_ref, 0, jj)
-
-    def both(now_ref, next_ref):
-        upcoming = jnp.minimum(step + 1, last)
-        cut = max(1, per_quad // 2)
-        pieces = [(k, n) for k in range(per_quad // cut) for n in range(2)]
-        for index, (k, n) in enumerate(pieces):
-            for jj in range(per_quad):
-                if jj * len(pieces) // per_quad == index:
-                    make_rows(next_ref, upcoming, jj)
-            deep = slice(k * cut * A, (k + 1) * cut * A)
-            cols = slice(n * tmpl, (n + 1) * tmpl)
-            acc_ref[:, cols] += dot_nt(now_ref[:, deep], t_ref[0, cols, deep])
-
-    @pl.when(step % 2 == 0)
+            make_rows(even_ref, jj)
+
+    @pl.when((step % 2 == 1) & (step < last))
     def _():
-        both(even_ref, odd_ref)
-
-    @pl.when(step % 2 == 1)
+        multiply(even_ref, odd_ref)
+
+    @pl.when((step % 2 == 0) & (step > 0) & (step < last))
     def _():
-        both(odd_ref, even_ref)
+        multiply(odd_ref, even_ref)
 
     @pl.when(step == last)
     def _():
+        multiply(odd_ref, None)
         shape = (segs, lag_total, tmpl)
-        out_ref[:, :lag_total] = (acc_ref[:half, :tmpl] + acc_ref[half:, tmpl:]).reshape(shape)
-        out_ref[:, lag_total:] = (acc_ref[half:, :tmpl] - acc_ref[:half, tmpl:]).reshape(shape)
-
-
-def lag_products(data, laid, lag_cos, lag_sin):
-    segs, _, blocks, _ = data.shape
+        for index in range(len(sources)):
+            low = slice(index * segs * lag_total, (index + 1) * segs * lag_total)
+            high = slice(half + low.start, half + low.stop)
+            place = pl.ds((place_ref[0] ^ index) * segs, segs)
+            out_ref[place, :lag_total] = (acc_ref[low, :tmpl] + acc_ref[high, tmpl:]).reshape(shape)
+            out_ref[place, lag_total:] = (acc_ref[high, :tmpl] - acc_ref[low, tmpl:]).reshape(shape)
+
+
+def lag_products(sources, place, laid, lag_cos, lag_sin):
+    blocks, rows, _ = sources[0].shape
     quads, tmpl2, depth = laid.shape
+    per_quad = depth // A
     lag_total = lag_cos.shape[1]
-    once = pl.Buffered(1)
+    segs = len(sources) * rows // 2
+
+    def ahead(i):
+        return (jnp.minimum(i, quads - 1), 0, 0)
+
     return pl.pallas_call(
         lag_kernel,
-        grid=(quads,),
-        in_specs=[
-            pl.BlockSpec(data.shape, lambda i: (0, 0, 0, 0), pipeline_mode=once),
-            pl.BlockSpec((1, tmpl2, depth), lambda i: (i, 0, 0)),
-            pl.BlockSpec(lag_cos.shape, lambda i: (0, 0, 0), pipeline_mode=once),
-            pl.BlockSpec(lag_sin.shape, lambda i: (0, 0, 0), pipeline_mode=once),
+        grid=(quads + 1,),
+        in_specs=[pl.BlockSpec(memory_space=pltpu.SMEM)]
+        + [pl.BlockSpec((per_quad, rows, A), ahead)] * len(sources)
+        + [
+            pl.BlockSpec((1, tmpl2, depth), lambda i: (jnp.maximum(i - 1, 0), 0, 0)),
+            pl.BlockSpec((per_quad, lag_total, A), ahead),
+            pl.BlockSpec((per_quad, lag_total, A), ahead),
         ],
         out_specs=pl.BlockSpec((segs, 2 * lag_total, tmpl2 // 2), lambda i: (0, 0, 0)),
         out_shape=jax.ShapeDtypeStruct((segs, 2 * lag_total, tmpl2 // 2), jnp.float32),
@@ -283,7 +281,6 @@
             pltpu.VMEM((2 * segs * lag_total, tmpl2), jnp.float32),
             pltpu.VMEM((2 * segs * lag_total, depth), jnp.bfloat16),
             pltpu.VMEM((2 * segs * lag_total, depth), jnp.bfloat16),
-            pltpu.VMEM((2, blocks, segs, A), jnp.float32),
         ],
         compiler_params=pltpu.CompilerParams(vmem_limit_bytes=60 * 2**20),
         cost_estimate=pl.CostEstimate(
@@ -292,7 +289,23 @@
             transcendentals=0,
         ),
         name="lag_products",
-    )(data, laid, lag_cos, lag_sin)
+    )(place, *sources, laid, lag_cos, lag_sin)
+
+
+def block_rows(data):
+    segs, parts, blocks, _ = data.shape
+    return data.transpose(2, 1, 0, 3).reshape(blocks, parts * segs, A)
+
+
+def spread(data):
+    def swap(value, bit):
+        return lax.ppermute(value, "tmpl", [(n, n ^ bit) for n in range(4)])
+
+    middle = data.shape[0] // 2
+    first = swap(data, 1)
+    second = swap(data, 2)
+    corner = jnp.concatenate([swap(first[:middle], 2), swap(second[middle:], 1)], axis=0)
+    return data, first, second, corner
 
 
 def layout_kernel(cut_ref, t_ref, *refs):
@@ -439,13 +452,21 @@
     lag_cos = block_cos * place_cos - block_sin * place_sin
     lag_sin = block_sin * place_cos + block_cos * place_sin
 
-    sliced = seg_local == 2 * freq_count and (NB // freq_count) % 32 == 0 and B // freq_count == 128
+    sliced = (
+        lax.axis_size("tmpl") == 4
+        and seg_local == 2 * freq_count == 16
+        and (NB // freq_count) % 32 == 0
+        and B // freq_count == 128
+    )
     if not sliced:
         laid = lay_out(templates, cuts, per_quad, 0, 1, None)
         laid = laid.reshape(quads, 2 * tmpl_local, per_quad * A)
         data = lax.all_gather(general_transform(strain, psd), "tmpl", axis=0, tiled=True)
-        half = data.shape[0] // 2
-        sums = [lag_products(part, laid, lag_cos, lag_sin) for part in (data[:half], data[half:])]
+        origin = jnp.zeros((1,), jnp.int32)
+        sums = []
+        for start in range(0, data.shape[0], 16):
+            sources = [block_rows(data[n : n + 4]) for n in range(start, start + 16, 4)]
+            sums.append(lag_products(sources, origin, laid, lag_cos, lag_sin))
         sums = jnp.concatenate(sums, axis=0)
         return lax.psum_scatter(sums, "freq", scatter_dimension=0, tiled=True)
 
@@ -479,17 +500,29 @@
     coefs_b = pack_coefs(time_b, first)
     data_a, coefs_b = tied((data_a, coefs_b))
     parts_b = exchange(coefs_b)
-    data_a = data_a.reshape(seg_local // 2, 2, blocks_here, A)
-    data_a = lax.all_gather(data_a, "tmpl", axis=0, tiled=True)
+    laid = laid.reshape(quads, 2 * tmpl_local, per_quad * A)
+    place = lax.axis_index("tmpl").astype(jnp.int32).reshape(1)
+
+    def halves(data):
+        data = data.reshape(2, 2, 2, 2, blocks_here, A)
+        return [spread(block_rows(data[:, n].reshape(4, 2, blocks_here, A))) for n in range(2)]
+
+    def collect(sums):
+        return lax.psum_scatter(sums, "freq", scatter_dimension=0, tiled=True)
+
+    first_a, second_a = halves(data_a)
     white_b = whiten(parts_b, second, white, white_far)
-    data_a = tied((data_a, white_b))[0]
-    data_b = exchange(white_b).reshape(seg_local // 2, 2, blocks_here, A)
-    data_b = lax.all_gather(data_b, "tmpl", axis=0, tiled=True)
-    laid = laid.reshape(quads, 2 * tmpl_local, per_quad * A)
-    outputs = []
-    for data in (data_a, data_b):
-        sums = lag_products(data, laid, lag_cos, lag_sin)
-        outputs.append(lax.psum_scatter(sums, "freq", scatter_dimension=0, tiled=True))
+    first_a = tied((first_a, white_b))[0]
+    data_b = exchange(white_b)
+    sums_a = lag_products(first_a, place, laid, lag_cos, lag_sin)
+    data_b, sums_a = tied((data_b, sums_a))
+    first_b, second_b = halves(data_b)
+    sums = [sums_a] + [
+        lag_products(part, place, laid, lag_cos, lag_sin) for part in (second_a, first_b, second_b)
+    ]
+    outputs = [collect(part) for part in sums[:3]]
+    shares = exchange(sums[3].reshape(freq_count, 2, 2 * lags.shape[0], tmpl_local))
+    outputs.append(jnp.sum(shares, axis=0))
     return jnp.concatenate(outputs, axis=0)
 
 

time: 402 us -> 422 us (1.050); the launches traced: 401 us -> 415 us
  blocking collectives: 59.8 us -> 20.4 us
  starting transfers between devices: 19.1 us -> 47.5 us
  local copies, waits for them, and re-layouts: 12.4 us -> 20.4 us
  other arithmetic: 14.6 us -> 21.1 us
  waiting for transfers between devices: 87.2 us -> 93.2 us
  Pallas kernels: 192 us -> 197 us
    all_to_all x2 -> x1, blocking collectives: 59.8 us -> 20.4 us  [exchange(): return lax.all_to_all(sent, 'freq', split_axis=0, concat_axis=0, tiled=True)]
    ppermute x0 -> x16, waiting for transfers between devices: none -> 38.4 us  [swap(): return lax.ppermute(value, 'tmpl', [(n, n ^ bit) for n in range(4)])]
    reduce_scatter x2 -> x3, waiting for transfers between devices: 31.4 us -> 0.06 us  [collect(): return lax.psum_scatter(sums, 'freq', scatter_dimension=0, tiled=True)]
    ppermute x0 -> x16, starting transfers between devices: none -> 19 us  [swap(): return lax.ppermute(value, 'tmpl', [(n, n ^ bit) for n in range(4)])]
    all_to_all x4 -> x6, starting transfers between devices: 18.5 us -> 27.8 us  [exchange(): return lax.all_to_all(sent, 'freq', split_axis=0, concat_axis=0, tiled=True)]
    slice x0 -> x10, local copies, waits for them, and re-layouts: none -> 6.02 us  [the longest x4 3.87 us: spread(): first[:middle]]
    concatenate x0 -> x4, other arithmetic: none -> 5.38 us  [spread(): jnp.concatenate([swap(first[:middle], 2), swap(second[middle:], 1)], axis=0)]
    pallas_call x2 -> x4, Pallas kernels: 132 us -> 136 us  [lag_products(): pl.pallas_call(lag_kernel, grid=(quads + 1,), in_specs=[pl.BlockSpec(memo...]
  transfers between devices with their start and end apart: 9 -> 26, of which waited for: 4 -> 9; matrix products, arithmetic and copies ran while one was open for 4% -> 7% of each run, Pallas kernels for 48% -> 47%
where the time goes in v4:
time: 422 us; the launch traced here: 415 us
  Pallas kernels  197 us (47%)
  waiting for transfers between devices  93.2 us (22%)
  starting transfers between devices  47.5 us (11%)
  other arithmetic  21.1 us (5%)
  local copies, waits for them, and re-layouts  20.4 us (5%)
  blocking collectives  20.4 us (5%)
  between operations  13.8 us (3%)
    pallas_call x4, Pallas kernels, lag_products(): pl.pallas_call(lag_kernel, grid=(quads + 1,), in_specs=[pl.BlockSpec(memo...  136 us
    all_to_all x6, waiting for transfers between devices, exchange(): return lax.all_to_all(sent, 'freq', split_axis=0, concat_axis=0, tiled=True)  54 us
    ppermute x16, waiting for transfers between devices, swap(): return lax.ppermute(value, 'tmpl', [(n, n ^ bit) for n in range(4)])  38.4 us
    pallas_call x2, Pallas kernels, lay_out(): pl.pallas_call(layout_kernel, grid=(steps, tmpl // batch), in_specs=[pl.B...  34.4 us
    all_to_all x6, starting transfers between devices, exchange(): return lax.all_to_all(sent, 'freq', split_axis=0, concat_axis=0, tiled=True)  27.8 us
    pallas_call x2, Pallas kernels, second_section(): pl.pallas_call(second_kernel, grid=(segs,), in_specs=[pl.BlockSpec((parts...  21.1 us
    all_to_all x1, blocking collectives, exchange(): return lax.all_to_all(sent, 'freq', split_axis=0, concat_axis=0, tiled=True)  20.4 us
    ppermute x16, starting transfers between devices, swap(): return lax.ppermute(value, 'tmpl', [(n, n ^ bit) for n in range(4)])  19 us
  transfers between devices with their start and end apart: 26, of which 9 were waited for; matrix products, arithmetic and copies ran while one was open for 7% of the time, Pallas kernels for 47%

profile of v4, /device:TPU:0, one launch (start us, length us, event | category | flops | bytes accessed | tf_op | source)
XLA Modules:
  0.0 415.1 jit_solution(12450256441680977865)
XLA Ops:
  6.5 4.2 %reshape.161 = f32[2,2,4,65536]{3,2,1,0:T(4,128)} reshape(f32[16,65536]{1,0:T(8,128)} %param.17) | data formatting | bytes 8388608 | tf_op jit(solution)/shard_map/reshape | solution.py:482
  10.7 4.1 fusion.1
  14.9 1.1 convert_element_type.53
  16.0 1.3 copy.63
  17.3 6.3 %all-to-all-start = ((f16[8,8,64,128]{3,2,1,0:T(8,128)(2,1)}), f16[8,8,64,128]{3,2,1,0:T(8,128)(2,1)S(1)}, u32[]{:S(2)}, u32[]{:S(2)}) async-start(f16[8,8,64,128]{3,2,1,0:T(8,128)(2,1)} %bitcast.46), calls=%async_computation | async-start | bytes 2097152 | tf_op jit(solution)/shard_map/all_to_all | solution.py:411
  23.7 0.7 all-gather.2.cloned.1.call-update
  24.4 17.2 %lay_out.2.refs_0_ = bf16[16,2,256,2048]{3,2,1,0:T(8,128)(2,1)} custom-call(s32[257]{0:T(512)S(1)} %get-tuple-element.54.cut_ref, bf16[256,2,64,512]{3,2,1,0:T(8,128)(2,1)} %t_ref.3), custom_call_target="tpu_custom_call" | custom-call | bytes 67108864 | tf_op jit(solution)/shard_map/lay_out/pallas_call | solution.py:344
  41.6 17.1 %all-to-all-done = f16[8,8,64,128]{3,2,1,0:T(8,128)(2,1)S(1)} async-done(((f16[8,8,64,128]{3,2,1,0:T(8,128)(2,1)}), f16[8,8,64,128]{3,2,1,0:T(8,128)(2,1)S(1)}, u32[]{:S(2)}, u32[]{:S(2)}) %all-to-all-start) | async-done | bytes 1048608 | tf_op jit(solution)/shard_map/all_to_all | solution.py:411
  59.0 2.6 first_section.2
  61.5 1.3 fusion.6
  62.8 3.6 all-to-all-start.1
  66.4 2.2 convert_element_type.57
  68.6 1.3 copy.62
  70.3 2.6 multiply_add_fusion
  72.9 1.1 slice.66
  74.2 17.3 %lay_out.3 = bf16[16,2,256,2048]{3,2,1,0:T(8,128)(2,1)} custom-call(s32[257]{0:T(512)S(1)} %get-tuple-element.53.cut_ref, bf16[256,2,64,512]{3,2,1,0:T(8,128)(2,1)} %t_ref.3, bf16[16,2,256,2048]{3,2,1,0:T(8,128)(2,1)} %lay_out.2.refs_0_), custom_call_target="tpu_custom_call", output_to_operand_aliasing={{}: (2, {})} | custom-call | bytes 67108864 | tf_op jit(solution)/shard_map/lay_out/pallas_call | solution.py:344
  91.5 0.9 multiply_rsqrt_fusion.wa_ref
  92.4 1.8 fusion.5.wm_ref
  94.2 5.6 %all-to-all-start.2 = ((f16[8,8,64,128]{3,2,1,0:T(8,128)(2,1)}), f16[8,8,64,128]{3,2,1,0:T(8,128)(2,1)S(1)}, u32[]{:S(2)}, u32[]{:S(2)}) async-start(f16[8,8,64,128]{3,2,1,0:T(8,128)(2,1)} %bitcast.55), calls=%async_computation.2 | async-start | bytes 2097152 | tf_op jit(solution)/shard_map/all_to_all | solution.py:411
  99.8 1.5 convert_multiply_fusion.2.y_ref
  101.3 10.6 %second_section.2 = bf16[8,1,2,64,512]{4,3,2,1,0:T(8,128)(2,1)} custom-call(f32[8,1,512,128]{3,2,1,0:T(8,128)} %convert_multiply_fusion.2.y_ref, f32[256,1024]{1,0:T(8,128)} %constant.94.clone.tc_ref, f32[256,1024]{1,0:T(8,128)} %constant.95.clone.ts_ref, f32[1,1024]{1,0:T(1,128)} %constant.96.clone.ec_ref, f32[1,1024]{1,0:T(1,128)} %constant.97.clone.es_ref, ...), custom_call_target="tpu_custom_call" | custom-call | flops 3321888768 | bytes 3145728 | tf_op jit(solution)/shard_map/second_section/pallas_call | solution.py:177
  111.9 14.5 %all-to-all-done.2 = f16[8,8,64,128]{3,2,1,0:T(8,128)(2,1)S(1)} async-done(((f16[8,8,64,128]{3,2,1,0:T(8,128)(2,1)}), f16[8,8,64,128]{3,2,1,0:T(8,128)(2,1)S(1)}, u32[]{:S(2)}, u32[]{:S(2)}) %all-to-all-start.2) | async-done | bytes 1048608 | tf_op jit(solution)/shard_map/all_to_all | solution.py:411
  126.4 3.6 all-to-all-start.3
  130.2 2.6 first_section.3
  132.8 1.2 fusion.7
  134.0 22.4 %all-to-all-done.3 = bf16[8,1,2,64,512]{4,3,2,1,0:T(8,128)(2,1)S(1)} async-done(((bf16[8,1,2,64,512]{4,3,2,1,0:T(8,128)(2,1)}), bf16[8,1,2,64,512]{4,3,2,1,0:T(8,128)(2,1)S(1)}, u32[]{:S(2)}, u32[]{:S(2)}) %all-to-all-start.3) | async-done | bytes 1048608 | tf_op jit(solution)/shard_map/all_to_all | solution.py:411
  156.4 3.7 all-to-all-start.4
  160.8 1.6 collective-permute-start.5
  162.4 1.5 collective-permute-start.4
  165.6 10.2 %collective-permute-done.5.x_ref = bf16[64,8,512]{2,1,0:T(8,128)(2,1)} collective-permute-done((bf16[64,8,512]{2,1,0:T(8,128)(2,1)S(1)}, bf16[64,8,512]{2,1,0:T(8,128)(2,1)}, u32[]{:S(2)}, u32[]{:S(2)}) %collective-permute-start.5) | collective-permute-done | bytes 524320 | tf_op jit(solution)/shard_map/ppermute | solution.py:302
  175.7 1.0 slice.73
  176.7 1.6 collective-permute-start.7
  178.3 1.0 slice.72
  179.2 1.6 collective-permute-start.6
  180.8 6.1 %collective-permute-done.1.x_ref = bf16[64,8,512]{2,1,0:T(8,128)(2,1)} collective-permute-done((bf16[64,8,512]{2,1,0:T(8,128)(2,1)S(1)}, bf16[64,8,512]{2,1,0:T(8,128)(2,1)}, u32[]{:S(2)}, u32[]{:S(2)}) %collective-permute-start.1) | collective-permute-done | bytes 524320 | tf_op jit(solution)/shard_map/ppermute | solution.py:302
  187.0 1.0 slice.70
  187.9 1.6 collective-permute-start.3
  189.5 1.0 slice.69
  190.5 1.6 collective-permute-start.2
  192.1 2.1 collective-permute-done.7
  194.2 1.9 pad_maximum_fusion.1.y_ref
  196.0 1.5 convert_multiply_fusion.y_ref
  197.5 10.5 %second_section.3 = bf16[8,1,2,64,512]{4,3,2,1,0:T(8,128)(2,1)} custom-call(f32[8,1,512,128]{3,2,1,0:T(8,128)} %convert_multiply_fusion.y_ref, f32[256,1024]{1,0:T(8,128)} %constant.94.clone.tc_ref, f32[256,1024]{1,0:T(8,128)} %constant.95.clone.ts_ref, f32[1,1024]{1,0:T(1,128)} %constant.96.clone.ec_ref, f32[1,1024]{1,0:T(1,128)} %constant.97.clone.es_ref, ...), custom_call_target="tpu_custom_call" | custom-call | flops 3321888768 | bytes 3145728 | tf_op jit(solution)/shard_map/second_section/pallas_call | solution.py:177
  208.0 5.1 %all-to-all-start.5 = ((bf16[8,1,2,64,512]{4,3,2,1,0:T(8,128)(2,1)}), bf16[8,1,2,64,512]{4,3,2,1,0:T(8,128)(2,1)S(1)}, u32[]{:S(2)}, u32[]{:S(2)}) async-start(bf16[8,1,2,64,512]{4,3,2,1,0:T(8,128)(2,1)} %second_section.3), calls=%async_computation.5 | async-start | bytes 2097152 | tf_op jit(solution)/shard_map/all_to_all | solution.py:411
  213.2 34.1 %lag_products.5 = f32[16,32,256]{2,1,0:T(8,128)} custom-call(s32[1]{0:T(128)} %bitcast.6.place_ref, bf16[64,8,512]{2,1,0:T(8,128)(2,1)} %copy-done.4, bf16[64,8,512]{2,1,0:T(8,128)(2,1)} %collective-permute-done.4.b_ref, bf16[64,8,512]{2,1,0:T(8,128)(2,1)} %collective-permute-done.5.x_ref, bf16[64,8,512]{2,1,0:T(8,128)(2,1)} %pad_maximum_fusion.1.y_ref, ...), custom_call_target="tpu_custom_call" | custom-call | flops 17179869184 | bytes 35651584 | tf_op jit(solution)/shard_map/lag_products/pallas_call | solution.py:268
  247.6 1.8 pad_maximum_fusion.y_ref
  249.4 34.0 %lag_products.4 = f32[16,32,256]{2,1,0:T(8,128)} custom-call(s32[1]{0:T(128)} %bitcast.6.place_ref, bf16[64,8,512]{2,1,0:T(8,128)(2,1)} %copy-done.3, bf16[64,8,512]{2,1,0:T(8,128)(2,1)} %collective-permute-done.b_ref, bf16[64,8,512]{2,1,0:T(8,128)(2,1)} %collective-permute-done.1.x_ref, bf16[64,8,512]{2,1,0:T(8,128)(2,1)} %pad_maximum_fusion.y_ref, ...), custom_call_target="tpu_custom_call" | custom-call | flops 17179869184 | bytes 35651584 | tf_op jit(solution)/shard_map/lag_products/pallas_call | solution.py:268
  284.6 1.5 collective-permute-start.8
  286.7 1.6 collective-permute-start.13
  288.8 10.1 %collective-permute-done.9.x_ref = bf16[64,8,512]{2,1,0:T(8,128)(2,1)S(1)} collective-permute-done((bf16[64,8,512]{2,1,0:T(8,128)(2,1)S(1)}, bf16[64,8,512]{2,1,0:T(8,128)(2,1)S(1)}, u32[]{:S(2)}, u32[]{:S(2)}) %collective-permute-start.9) | collective-permute-done | bytes 524320 | tf_op jit(solution)/shard_map/ppermute | solution.py:302
  298.9 0.8 copy-done.9
  299.7 1.6 collective-permute-start.11
  301.2 1.0 slice.75
  303.1 7.0 %collective-permute-done.13.x_ref = bf16[64,8,512]{2,1,0:T(8,128)(2,1)S(1)} collective-permute-done((bf16[64,8,512]{2,1,0:T(8,128)(2,1)S(1)}, bf16[64,8,512]{2,1,0:T(8,128)(2,1)S(1)}, u32[]{:S(2)}, u32[]{:S(2)}) %collective-permute-start.13) | collective-permute-done | bytes 524320 | tf_op jit(solution)/shard_map/ppermute | solution.py:302
  310.1 1.6 collective-permute-start.15
  311.7 1.0 slice.78
  312.7 0.6 collective-permute-start.14
  313.3 3.0 collective-permute-done.11
  316.3 0.9 pad_maximum_fusion.2.y_ref
  317.1 34.0 %lag_products.6 = f32[16,32,256]{2,1,0:T(8,128)} custom-call(s32[1]{0:T(128)} %bitcast.6.place_ref, bf16[64,8,512]{2,1,0:T(8,128)(2,1)} %copy-done.6, bf16[64,8,512]{2,1,0:T(8,128)(2,1)} %collective-permute-done.8.b_ref, bf16[64,8,512]{2,1,0:T(8,128)(2,1)} %copy-done.9, bf16[64,8,512]{2,1,0:T(8,128)(2,1)} %pad_maximum_fusion.2.y_ref, ...), custom_call_target="tpu_custom_call" | custom-call | flops 17179869184 | bytes 35651584 | tf_op jit(solution)/shard_map/lag_products/pallas_call | solution.py:268
  351.2 0.9 pad_maximum_fusion.3.y_ref
  352.1 34.1 %lag_products.7 = f32[16,32,256]{2,1,0:T(8,128)} custom-call(s32[1]{0:T(128)} %bitcast.6.place_ref, bf16[64,8,512]{2,1,0:T(8,128)(2,1)} %copy-done.5, bf16[64,8,512]{2,1,0:T(8,128)(2,1)} %collective-permute-done.12.b_ref, bf16[64,8,512]{2,1,0:T(8,128)(2,1)} %copy-done.8, bf16[64,8,512]{2,1,0:T(8,128)(2,1)} %pad_maximum_fusion.3.y_ref, ...), custom_call_target="tpu_custom_call" | custom-call | flops 17179869184 | bytes 35651584 | tf_op jit(solution)/shard_map/lag_products/pallas_call | solution.py:268
  386.1 20.4 %all_to_all.35 = f32[8,2,32,256]{3,2,1,0:T(8,128)S(1)} all-to-all(f32[8,2,32,256]{3,2,1,0:T(8,128)} %bitcast.66), channel_id=1, replica_groups=mesh['tmpl'=4,'freq'=8] {'freq'}, dimensions={0} | all-to-all | bytes 1048576 | tf_op jit(solution)/shard_map/all_to_all | solution.py:411
  406.7 1.6 pad_maximum_fusion.4
  (74 shorter events, 7.1 us)
Async XLA Ops:
  16.0 8.4 %copy-start.10 = (s32[256]{0:T(256)S(1)}, s32[256]{0:T(256)}, u32[]{:S(2)}) copy-start(s32[256]{0:T(256)} %param.20) | copy-start | bytes 3076
  17.3 41.3 %all-to-all-start = ((f16[8,8,64,128]{3,2,1,0:T(8,128)(2,1)}), f16[8,8,64,128]{3,2,1,0:T(8,128)(2,1)S(1)}, u32[]{:S(2)}, u32[]{:S(2)}) async-start(f16[8,8,64,128]{3,2,1,0:T(8,128)(2,1)} %bitcast.46), calls=%async_computation | async-start | bytes 2097152 | tf_op jit(solution)/shard_map/all_to_all | solution.py:411
  23.7 49.3 %all-gather.2.cloned.1.call-start = ((), (), s32[]{:S(2)}) async-start(), calls=%async_computation.10 | async-start | bytes 1179648 | tf_op jit(solution)/shard_map/all_gather | solution.py:474
  41.6 17.4 %copy-start = (bf16[512,512]{1,0:T(8,128)(2,1)S(1)}, bf16[512,512]{1,0:T(8,128)(2,1)}, u32[]{:S(2)}) copy-start(bf16[512,512]{1,0:T(8,128)(2,1)} %constant.92.clone.high_ref) | copy-start | bytes 1572868
  41.6 17.4 %copy-start.1 = (bf16[512,512]{1,0:T(8,128)(2,1)S(1)}, bf16[512,512]{1,0:T(8,128)(2,1)}, u32[]{:S(2)}) copy-start(bf16[512,512]{1,0:T(8,128)(2,1)} %constant.93.clone.low_ref) | copy-start | bytes 1572868
  62.8 31.4 %all-to-all-start.1 = ((f16[8,1,512,128]{3,2,1,0:T(8,128)(2,1)}), f16[8,1,512,128]{3,2,1,0:T(8,128)(2,1)S(1)}, u32[]{:S(2)}, u32[]{:S(2)}) async-start(f16[8,1,512,128]{3,2,1,0:T(8,128)(2,1)} %fusion.6), calls=%async_computation.1 | async-start | bytes 2097152 | tf_op jit(solution)/shard_map/all_to_all | solution.py:411
  66.4 3.5 copy-start.11
  74.2 18.2 %copy-start.2 = (f32[512,512]{0,1:T(8,128)S(1)}, f32[512,512]{0,1:T(8,128)}, u32[]{:S(2)}) copy-start(f32[512,512]{0,1:T(8,128)} %all-gather.2.cloned.1.call-done) | copy-start | bytes 3145732
  74.2 18.2 %copy-start.7 = (f32[256,256]{1,0:T(8,128)S(1)}, f32[256,256]{1,0:T(8,128)}, u32[]{:S(2)}) copy-start(f32[256,256]{1,0:T(8,128)} %constant.91.clone) | copy-start | bytes 786436
  94.2 32.1 %all-to-all-start.2 = ((f16[8,8,64,128]{3,2,1,0:T(8,128)(2,1)}), f16[8,8,64,128]{3,2,1,0:T(8,128)(2,1)S(1)}, u32[]{:S(2)}, u32[]{:S(2)}) async-start(f16[8,8,64,128]{3,2,1,0:T(8,128)(2,1)} %bitcast.55), calls=%async_computation.2 | async-start | bytes 2097152 | tf_op jit(solution)/shard_map/all_to_all | solution.py:411
  126.4 30.1 %all-to-all-start.3 = ((bf16[8,1,2,64,512]{4,3,2,1,0:T(8,128)(2,1)}), bf16[8,1,2,64,512]{4,3,2,1,0:T(8,128)(2,1)S(1)}, u32[]{:S(2)}, u32[]{:S(2)}) async-start(bf16[8,1,2,64,512]{4,3,2,1,0:T(8,128)(2,1)} %second_section.2), calls=%async_computation.3 | async-start | bytes 2097152 | tf_op jit(solution)/shard_map/all_to_all | solution.py:411
  156.4 39.6 %all-to-all-start.4 = ((f16[8,1,512,128]{3,2,1,0:T(8,128)(2,1)}), f16[8,1,512,128]{3,2,1,0:T(8,128)(2,1)S(1)}, u32[]{:S(2)}, u32[]{:S(2)}) async-start(f16[8,1,512,128]{3,2,1,0:T(8,128)(2,1)} %bitcast.5), calls=%async_computation.4 | async-start | bytes 2097152 | tf_op jit(solution)/shard_map/all_to_all | solution.py:411
  160.8 29.7 %copy-start.4 = (bf16[64,8,512]{2,1,0:T(8,128)(2,1)}, bf16[64,8,512]{2,1,0:T(8,128)(2,1)S(1)}, u32[]{:S(2)}) copy-start(bf16[64,8,512]{2,1,0:T(8,128)(2,1)S(1)} %reshape.168.a_ref) | copy-start | bytes 1572868
  160.8 14.9 %collective-permute-start.5 = (bf16[64,8,512]{2,1,0:T(8,128)(2,1)S(1)}, bf16[64,8,512]{2,1,0:T(8,128)(2,1)}, u32[]{:S(2)}, u32[]{:S(2)}) collective-permute-start(bf16[64,8,512]{2,1,0:T(8,128)(2,1)S(1)} %reshape.168.a_ref), channel_id=1, source_target_pairs={{0,16},{8,24},{16,0},{24,8},{1,17},{9,25},{17,1},{25,9},{2,18},{10... | collective-permute-start | bytes 1572872 | tf_op jit(solution)/shard_map/ppermute | solution.py:302
  162.4 15.8 %collective-permute-start.4 = (bf16[64,8,512]{2,1,0:T(8,128)(2,1)S(1)}, bf16[64,8,512]{2,1,0:T(8,128)(2,1)}, u32[]{:S(2)}, u32[]{:S(2)}) collective-permute-start(bf16[64,8,512]{2,1,0:T(8,128)(2,1)S(1)} %reshape.168.a_ref), channel_id=1, source_target_pairs={{0,8},{8,0},{16,24},{24,16},{1,9},{9,1},{17,25},{25,17},{2,10},{10... | collective-permute-start | bytes 1572872 | tf_op jit(solution)/shard_map/ppermute | solution.py:302
  164.5 33.1 %copy-start.3 = (bf16[64,8,512]{2,1,0:T(8,128)(2,1)}, bf16[64,8,512]{2,1,0:T(8,128)(2,1)S(1)}, u32[]{:S(2)}) copy-start(bf16[64,8,512]{2,1,0:T(8,128)(2,1)S(1)} %reshape.166.a_ref) | copy-start | bytes 1572868
  164.5 22.5 %collective-permute-start.1 = (bf16[64,8,512]{2,1,0:T(8,128)(2,1)S(1)}, bf16[64,8,512]{2,1,0:T(8,128)(2,1)}, u32[]{:S(2)}, u32[]{:S(2)}) collective-permute-start(bf16[64,8,512]{2,1,0:T(8,128)(2,1)S(1)} %reshape.166.a_ref), channel_id=1, source_target_pairs={{0,16},{8,24},{16,0},{24,8},{1,17},{9,25},{17,1},{25,9},{2,18},{10... | collective-permute-start | bytes 1572872 | tf_op jit(solution)/shard_map/ppermute | solution.py:302
  165.0 24.5 %collective-permute-start = (bf16[64,8,512]{2,1,0:T(8,128)(2,1)S(1)}, bf16[64,8,512]{2,1,0:T(8,128)(2,1)}, u32[]{:S(2)}, u32[]{:S(2)}) collective-permute-start(bf16[64,8,512]{2,1,0:T(8,128)(2,1)S(1)} %reshape.166.a_ref), channel_id=1, source_target_pairs={{0,8},{8,0},{16,24},{24,16},{1,9},{9,1},{17,25},{25,17},{2,10},{10... | collective-permute-start | bytes 1572872 | tf_op jit(solution)/shard_map/ppermute | solution.py:302
  176.7 17.4 %collective-permute-start.7 = (bf16[32,8,512]{2,1,0:T(8,128)(2,1)S(1)}, bf16[32,8,512]{2,1,0:T(8,128)(2,1)}, u32[]{:S(2)}, u32[]{:S(2)}) collective-permute-start(bf16[32,8,512]{2,1,0:T(8,128)(2,1)S(1)} %slice.73), channel_id=1, source_target_pairs={{0,8},{8,0},{16,24},{24,16},{1,9},{9,1},{17,25},{25,17},{2,10},{10... | collective-permute-start | bytes 786440 | tf_op jit(solution)/shard_map/ppermute | solution.py:302
  179.2 14.9 %collective-permute-start.6 = (bf16[32,8,512]{2,1,0:T(8,128)(2,1)S(1)}, bf16[32,8,512]{2,1,0:T(8,128)(2,1)}, u32[]{:S(2)}, u32[]{:S(2)}) collective-permute-start(bf16[32,8,512]{2,1,0:T(8,128)(2,1)S(1)} %slice.72), channel_id=1, source_target_pairs={{0,16},{8,24},{16,0},{24,8},{1,17},{9,25},{17,1},{25,9},{2,18},{10... | collective-permute-start | bytes 786440 | tf_op jit(solution)/shard_map/ppermute | solution.py:302
  187.9 59.6 %collective-permute-start.3 = (bf16[32,8,512]{2,1,0:T(8,128)(2,1)S(1)}, bf16[32,8,512]{2,1,0:T(8,128)(2,1)S(1)}, u32[]{:S(2)}, u32[]{:S(2)}) collective-permute-start(bf16[32,8,512]{2,1,0:T(8,128)(2,1)S(1)} %slice.70), channel_id=1, source_target_pairs={{0,8},{8,0},{16,24},{24,16},{1,9},{9,1},{17,25},{25,17},{2,10},{10... | collective-permute-start | bytes 786440 | tf_op jit(solution)/shard_map/ppermute | solution.py:302
  190.5 57.1 %collective-permute-start.2 = (bf16[32,8,512]{2,1,0:T(8,128)(2,1)S(1)}, bf16[32,8,512]{2,1,0:T(8,128)(2,1)}, u32[]{:S(2)}, u32[]{:S(2)}) collective-permute-start(bf16[32,8,512]{2,1,0:T(8,128)(2,1)S(1)} %slice.69), channel_id=1, source_target_pairs={{0,16},{8,24},{16,0},{24,8},{1,17},{9,25},{17,1},{25,9},{2,18},{10... | collective-permute-start | bytes 786440 | tf_op jit(solution)/shard_map/ppermute | solution.py:302
  208.0 75.4 %all-to-all-start.5 = ((bf16[8,1,2,64,512]{4,3,2,1,0:T(8,128)(2,1)}), bf16[8,1,2,64,512]{4,3,2,1,0:T(8,128)(2,1)S(1)}, u32[]{:S(2)}, u32[]{:S(2)}) async-start(bf16[8,1,2,64,512]{4,3,2,1,0:T(8,128)(2,1)} %second_section.3), calls=%async_computation.5 | async-start | bytes 2097152 | tf_op jit(solution)/shard_map/all_to_all | solution.py:411
  213.1 193.5 %reduce-scatter.6.cloned.1.call-start = ((), (), s32[]{:S(2)}) async-start(), calls=%async_computation.12 | async-start | bytes 589824 | tf_op jit(solution)/shard_map/reduce_scatter | solution.py:511
  247.3 159.3 %reduce-scatter.4.cloned.1.call-start = ((), (), s32[]{:S(2)}) async-start(), calls=%async_computation.11 | async-start | bytes 589824 | tf_op jit(solution)/shard_map/reduce_scatter | solution.py:511
  284.1 26.1 %copy-start.6 = (bf16[64,8,512]{2,1,0:T(8,128)(2,1)}, bf16[64,8,512]{2,1,0:T(8,128)(2,1)S(1)}, u32[]{:S(2)}) copy-start(bf16[64,8,512]{2,1,0:T(8,128)(2,1)S(1)} %reshape.170.a_ref) | copy-start | bytes 1572868
  284.1 14.8 %collective-permute-start.9 = (bf16[64,8,512]{2,1,0:T(8,128)(2,1)S(1)}, bf16[64,8,512]{2,1,0:T(8,128)(2,1)S(1)}, u32[]{:S(2)}, u32[]{:S(2)}) collective-permute-start(bf16[64,8,512]{2,1,0:T(8,128)(2,1)S(1)} %reshape.170.a_ref), channel_id=1, source_target_pairs={{0,16},{8,24},{16,0},{24,8},{1,17},{9,25},{17,1},{25,9},{2,18},{10... | collective-permute-start | bytes 1572872 | tf_op jit(solution)/shard_map/ppermute | solution.py:302
  284.6 16.6 %collective-permute-start.8 = (bf16[64,8,512]{2,1,0:T(8,128)(2,1)S(1)}, bf16[64,8,512]{2,1,0:T(8,128)(2,1)}, u32[]{:S(2)}, u32[]{:S(2)}) collective-permute-start(bf16[64,8,512]{2,1,0:T(8,128)(2,1)S(1)} %reshape.170.a_ref), channel_id=1, source_target_pairs={{0,8},{8,0},{16,24},{24,16},{1,9},{9,1},{17,25},{25,17},{2,10},{10... | collective-permute-start | bytes 1572872 | tf_op jit(solution)/shard_map/ppermute | solution.py:302
  286.7 64.5 %copy-start.5 = (bf16[64,8,512]{2,1,0:T(8,128)(2,1)}, bf16[64,8,512]{2,1,0:T(8,128)(2,1)S(1)}, u32[]{:S(2)}) copy-start(bf16[64,8,512]{2,1,0:T(8,128)(2,1)S(1)} %reshape.171.a_ref) | copy-start | bytes 1572868
  286.7 23.4 %collective-permute-start.13 = (bf16[64,8,512]{2,1,0:T(8,128)(2,1)S(1)}, bf16[64,8,512]{2,1,0:T(8,128)(2,1)S(1)}, u32[]{:S(2)}, u32[]{:S(2)}) collective-permute-start(bf16[64,8,512]{2,1,0:T(8,128)(2,1)S(1)} %reshape.171.a_ref), channel_id=1, source_target_pairs={{0,16},{8,24},{16,0},{24,8},{1,17},{9,25},{17,1},{25,9},{2,18},{10... | collective-permute-start | bytes 1572872 | tf_op jit(solution)/shard_map/ppermute | solution.py:302
  288.3 23.4 %collective-permute-start.12 = (bf16[64,8,512]{2,1,0:T(8,128)(2,1)S(1)}, bf16[64,8,512]{2,1,0:T(8,128)(2,1)}, u32[]{:S(2)}, u32[]{:S(2)}) collective-permute-start(bf16[64,8,512]{2,1,0:T(8,128)(2,1)S(1)} %reshape.171.a_ref), channel_id=1, source_target_pairs={{0,8},{8,0},{16,24},{24,16},{1,9},{9,1},{17,25},{25,17},{2,10},{10... | collective-permute-start | bytes 1572872 | tf_op jit(solution)/shard_map/ppermute | solution.py:302
  298.9 0.8 copy-start.9
  299.7 16.6 %collective-permute-start.11 = (bf16[32,8,512]{2,1,0:T(8,128)(2,1)S(1)}, bf16[32,8,512]{2,1,0:T(8,128)(2,1)S(1)}, u32[]{:S(2)}, u32[]{:S(2)}) collective-permute-start(bf16[32,8,512]{2,1,0:T(8,128)(2,1)S(1)} %slice.76), channel_id=1, source_target_pairs={{0,8},{8,0},{16,24},{24,16},{1,9},{9,1},{17,25},{25,17},{2,10},{10... | collective-permute-start | bytes 786440 | tf_op jit(solution)/shard_map/ppermute | solution.py:302
  302.2 14.0 %collective-permute-start.10 = (bf16[32,8,512]{2,1,0:T(8,128)(2,1)S(1)}, bf16[32,8,512]{2,1,0:T(8,128)(2,1)S(1)}, u32[]{:S(2)}, u32[]{:S(2)}) collective-permute-start(bf16[32,8,512]{2,1,0:T(8,128)(2,1)S(1)} %slice.75), channel_id=1, source_target_pairs={{0,16},{8,24},{16,0},{24,8},{1,17},{9,25},{17,1},{25,9},{2,18},{10... | collective-permute-start | bytes 786440 | tf_op jit(solution)/shard_map/ppermute | solution.py:302
  302.8 103.9 %reduce-scatter.8.cloned.1.call-start = ((), (), s32[]{:S(2)}) async-start(), calls=%async_computation.13 | async-start | bytes 589824 | tf_op jit(solution)/shard_map/reduce_scatter | solution.py:511
  310.1 41.1 %copy-start.8 = (bf16[64,8,512]{2,1,0:T(8,128)(2,1)}, bf16[64,8,512]{2,1,0:T(8,128)(2,1)S(1)}, u32[]{:S(2)}) copy-start(bf16[64,8,512]{2,1,0:T(8,128)(2,1)S(1)} %collective-permute-done.13.x_ref) | copy-start | bytes 1572868
  310.1 41.1 %collective-permute-start.15 = (bf16[32,8,512]{2,1,0:T(8,128)(2,1)S(1)}, bf16[32,8,512]{2,1,0:T(8,128)(2,1)S(1)}, u32[]{:S(2)}, u32[]{:S(2)}) collective-permute-start(bf16[32,8,512]{2,1,0:T(8,128)(2,1)S(1)} %slice.79), channel_id=1, source_target_pairs={{0,8},{8,0},{16,24},{24,16},{1,9},{9,1},{17,25},{25,17},{2,10},{10... | collective-permute-start | bytes 786440 | tf_op jit(solution)/shard_map/ppermute | solution.py:302
  312.7 38.5 %collective-permute-start.14 = (bf16[32,8,512]{2,1,0:T(8,128)(2,1)S(1)}, bf16[32,8,512]{2,1,0:T(8,128)(2,1)S(1)}, u32[]{:S(2)}, u32[]{:S(2)}) collective-permute-start(bf16[32,8,512]{2,1,0:T(8,128)(2,1)S(1)} %slice.78), channel_id=1, source_target_pairs={{0,16},{8,24},{16,0},{24,8},{1,17},{9,25},{17,1},{25,9},{2,18},{10... | collective-permute-start | bytes 786440 | tf_op jit(solution)/shard_map/ppermute | solution.py:302
Sparse Core Ops, SparseCore 0:
  26.1 33.3 all-gather.1
  247.4 31.3 reduce-scatter.5
  302.9 31.4 reduce-scatter.3
  351.3 32.4 reduce-scatter.7

commit v5 on v4

--- a/solution.py
+++ b/solution.py
@@ -198,7 +198,6 @@
     tmpl = out_ref.shape[2]
     step = pl.program_id(0)
     last = pl.num_programs(0) - 1
-    half = len(sources) * segs * lag_total
 
     def make_rows(rows_ref, jj):
         for chunk in range(A // 128):
@@ -213,21 +212,26 @@
                     imag = value[segs + s : segs + s + 1]
                     first_row = (index * segs + s) * lag_total
                     rows = slice(first_row, first_row + lag_total)
-                    rows_ref[rows, out_lanes] = (real * lag_cos - imag * lag_sin).astype(jnp.bfloat16)
-                    rows = slice(half + first_row, half + first_row + lag_total)
-                    rows_ref[rows, out_lanes] = (real * lag_sin + imag * lag_cos).astype(jnp.bfloat16)
+                    real_q = (real * lag_cos - imag * lag_sin).astype(jnp.bfloat16)
+                    imag_q = (real * lag_sin + imag * lag_cos).astype(jnp.bfloat16)
+                    rows_ref[0, rows, out_lanes] = real_q
+                    rows_ref[1, rows, out_lanes] = imag_q - real_q
+                    rows_ref[2, rows, out_lanes] = imag_q + real_q
 
     def multiply(now_ref, next_ref):
         cut = max(1, per_quad // 2)
-        pieces = [(k, n) for k in range(per_quad // cut) for n in range(2)]
+        pieces = [(k, n) for k in range(per_quad // cut) for n in range(3)]
         for index, (k, n) in enumerate(pieces):
             if next_ref is not None:
                 for jj in range(per_quad):
                     if jj * len(pieces) // per_quad == index:
                         make_rows(next_ref, jj)
             deep = slice(k * cut * A, (k + 1) * cut * A)
-            cols = slice(n * tmpl, (n + 1) * tmpl)
-            acc_ref[:, cols] += dot_nt(now_ref[:, deep], t_ref[0, cols, deep])
+            if n == 0:
+                columns = t_ref[0, :tmpl, deep] - t_ref[0, tmpl:, deep]
+            else:
+                columns = t_ref[0, (n - 1) * tmpl : n * tmpl, deep]
+            acc_ref[n] += dot_nt(now_ref[n, :, deep], columns)
 
     @pl.when(step == 0)
     def _():
@@ -248,11 +252,10 @@
         multiply(odd_ref, None)
         shape = (segs, lag_total, tmpl)
         for index in range(len(sources)):
-            low = slice(index * segs * lag_total, (index + 1) * segs * lag_total)
-            high = slice(half + low.start, half + low.stop)
+            rows = slice(index * segs * lag_total, (index + 1) * segs * lag_total)
             place = pl.ds((place_ref[0] ^ index) * segs, segs)
-            out_ref[place, :lag_total] = (acc_ref[low, :tmpl] + acc_ref[high, tmpl:]).reshape(shape)
-            out_ref[place, lag_total:] = (acc_ref[high, :tmpl] - acc_ref[low, tmpl:]).reshape(shape)
+            out_ref[place, :lag_total] = (acc_ref[0, rows] + acc_ref[2, rows]).reshape(shape)
+            out_ref[place, lag_total:] = (acc_ref[0, rows] + acc_ref[1, rows]).reshape(shape)
 
 
 def lag_products(sources, place, laid, lag_cos, lag_sin):
@@ -278,13 +281,13 @@
         out_specs=pl.BlockSpec((segs, 2 * lag_total, tmpl2 // 2), lambda i: (0, 0, 0)),
         out_shape=jax.ShapeDtypeStruct((segs, 2 * lag_total, tmpl2 // 2), jnp.float32),
         scratch_shapes=[
-            pltpu.VMEM((2 * segs * lag_total, tmpl2), jnp.float32),
-            pltpu.VMEM((2 * segs * lag_total, depth), jnp.bfloat16),
-            pltpu.VMEM((2 * segs * lag_total, depth), jnp.bfloat16),
+            pltpu.VMEM((3, segs * lag_total, tmpl2 // 2), jnp.float32),
+            pltpu.VMEM((3, segs * lag_total, depth), jnp.bfloat16),
+            pltpu.VMEM((3, segs * lag_total, depth), jnp.bfloat16),
         ],
         compiler_params=pltpu.CompilerParams(vmem_limit_bytes=60 * 2**20),
         cost_estimate=pl.CostEstimate(
-            flops=4 * segs * lag_total * tmpl2 * blocks * A,
+            flops=3 * segs * lag_total * tmpl2 * blocks * A,
             bytes_accessed=blocks * A * (tmpl2 * 2 + segs * 4),
             transcendentals=0,
         ),
@@ -301,11 +304,7 @@
     def swap(value, bit):
         return lax.ppermute(value, "tmpl", [(n, n ^ bit) for n in range(4)])
 
-    middle = data.shape[0] // 2
-    first = swap(data, 1)
-    second = swap(data, 2)
-    corner = jnp.concatenate([swap(first[:middle], 2), swap(second[middle:], 1)], axis=0)
-    return data, first, second, corner
+    return (data,) + tuple(swap(data, bit) for bit in (1, 2, 3))
 
 
 def layout_kernel(cut_ref, t_ref, *refs):
@@ -516,6 +515,7 @@
     data_b = exchange(white_b)
     sums_a = lag_products(first_a, place, laid, lag_cos, lag_sin)
     data_b, sums_a = tied((data_b, sums_a))
+    second_a = tied((second_a, data_b))[0]
     first_b, second_b = halves(data_b)
     sums = [sums_a] + [
         lag_products(part, place, laid, lag_cos, lag_sin) for part in (second_a, first_b, second_b)

time: 422 us -> 439 us (1.040)
  blocking collectives: 20.4 us -> 49.4 us
  starting transfers between devices: 47.5 us -> 38.9 us
  Pallas kernels: 197 us -> 204 us
  other arithmetic: 21.1 us -> 14.8 us
    all_to_all x1 -> x2, blocking collectives: 20.4 us -> 49.4 us  [exchange(): return lax.all_to_all(sent, 'freq', split_axis=0, concat_axis=0, tiled=True)]
    pallas_call x4, Pallas kernels: 136 us -> 144 us  [lag_products(): pl.pallas_call(lag_kernel, grid=(quads + 1,), in_specs=[pl.BlockSpec(memo...]
    slice x8 -> x0, local copies, waits for them, and re-layouts: 5.84 us -> none  [the longest x4 3.87 us: spread(): first[:middle]]
    all_to_all x6 -> x5, starting transfers between devices: 27.8 us -> 22.2 us  [exchange(): return lax.all_to_all(sent, 'freq', split_axis=0, concat_axis=0, tiled=True)]
    concatenate x4 -> x0, other arithmetic: 5.38 us -> none  [spread(): jnp.concatenate([swap(first[:middle], 2), swap(second[middle:], 1)], axis=0)]
    ppermute x16 -> x12, starting transfers between devices: 19 us -> 16.3 us  [swap(): return lax.ppermute(value, 'tmpl', [(n, n ^ bit) for n in range(4)])]
    ppermute x16 -> x12, waiting for transfers between devices: 38.4 us -> 37.3 us  [swap(): return lax.ppermute(value, 'tmpl', [(n, n ^ bit) for n in range(4)])]
    all_to_all x6 -> x5, waiting for transfers between devices: 54 us -> 55 us  [exchange(): return lax.all_to_all(sent, 'freq', split_axis=0, concat_axis=0, tiled=True)]
  transfers between devices with their start and end apart: 26 -> 21, of which waited for: 9 -> 8; matrix products, arithmetic and copies ran while one was open for 7% -> 4% of each run, Pallas kernels for 47% -> 37%
where the time goes in v5:
time: 439 us; the launch traced here: 432 us
  Pallas kernels  204 us (46%)
  waiting for transfers between devices  93 us (21%)
  blocking collectives  49.4 us (11%)
  starting transfers between devices  38.9 us (9%)
  local copies, waits for them, and re-layouts  16.1 us (4%)
  other arithmetic  14.8 us (3%)
  between operations  14 us (3%)
    pallas_call x4, Pallas kernels, lag_products(): pl.pallas_call(lag_kernel, grid=(quads + 1,), in_specs=[pl.BlockSpec(memo...  144 us
    all_to_all x5, waiting for transfers between devices, exchange(): return lax.all_to_all(sent, 'freq', split_axis=0, concat_axis=0, tiled=True)  55 us
    all_to_all x2, blocking collectives, exchange(): return lax.all_to_all(sent, 'freq', split_axis=0, concat_axis=0, tiled=True)  49.4 us
    ppermute x12, waiting for transfers between devices, swap(): return lax.ppermute(value, 'tmpl', [(n, n ^ bit) for n in range(4)])  37.3 us
    pallas_call x2, Pallas kernels, lay_out(): pl.pallas_call(layout_kernel, grid=(steps, tmpl // batch), in_specs=[pl.B...  34.5 us
    all_to_all x5, starting transfers between devices, exchange(): return lax.all_to_all(sent, 'freq', split_axis=0, concat_axis=0, tiled=True)  22.2 us
    pallas_call x2, Pallas kernels, second_section(): pl.pallas_call(second_kernel, grid=(segs,), in_specs=[pl.BlockSpec((parts...  21.1 us
    ppermute x12, starting transfers between devices, swap(): return lax.ppermute(value, 'tmpl', [(n, n ^ bit) for n in range(4)])  16.3 us
  transfers between devices with their start and end apart: 21, of which 8 were waited for; matrix products, arithmetic and copies ran while one was open for 4% of the time, Pallas kernels for 37%

profile of v5, /device:TPU:0, one launch (start us, length us, event | category | flops | bytes accessed | tf_op | source)
XLA Modules:
  0.0 432.4 jit_solution(2048830660646807777)
XLA Ops:
  6.5 4.2 reshape.161
  10.7 4.1 fusion.1
  14.9 1.1 convert_element_type.53
  16.0 1.3 copy.63
  17.3 6.3 %all-to-all-start = ((f16[8,8,64,128]{3,2,1,0:T(8,128)(2,1)}), f16[8,8,64,128]{3,2,1,0:T(8,128)(2,1)S(1)}, u32[]{:S(2)}, u32[]{:S(2)}) async-start(f16[8,8,64,128]{3,2,1,0:T(8,128)(2,1)} %bitcast.46), calls=%async_computation | async-start | bytes 2097152 | tf_op jit(solution)/shard_map/all_to_all | solution.py:410
  23.7 0.7 all-gather.2.cloned.1.call-update
  24.4 17.2 %lay_out.2.refs_0_ = bf16[16,2,256,2048]{3,2,1,0:T(8,128)(2,1)} custom-call(s32[257]{0:T(512)S(1)} %get-tuple-element.62.cut_ref, bf16[256,2,64,512]{3,2,1,0:T(8,128)(2,1)} %t_ref.3), custom_call_target="tpu_custom_call" | custom-call | bytes 67108864 | tf_op jit(solution)/shard_map/lay_out/pallas_call | solution.py:343
  41.6 17.1 %all-to-all-done = f16[8,8,64,128]{3,2,1,0:T(8,128)(2,1)S(1)} async-done(((f16[8,8,64,128]{3,2,1,0:T(8,128)(2,1)}), f16[8,8,64,128]{3,2,1,0:T(8,128)(2,1)S(1)}, u32[]{:S(2)}, u32[]{:S(2)}) %all-to-all-start) | async-done | bytes 1048608 | tf_op jit(solution)/shard_map/all_to_all | solution.py:410
  58.7 0.3 convert_multiply_fusion.3.x_ref
  59.0 2.6 first_section.2
  61.5 1.3 fusion.6
  62.8 3.6 all-to-all-start.1
  66.4 2.2 convert_element_type.57
  68.6 1.3 copy.62
  69.9 0.2 fusion.19
  70.1 0.2 fusion.21
  70.4 2.6 multiply_add_fusion
  73.0 1.1 slice.34
  74.3 17.3 %lay_out.3 = bf16[16,2,256,2048]{3,2,1,0:T(8,128)(2,1)} custom-call(s32[257]{0:T(512)S(1)} %get-tuple-element.61.cut_ref, bf16[256,2,64,512]{3,2,1,0:T(8,128)(2,1)} %t_ref.3, bf16[16,2,256,2048]{3,2,1,0:T(8,128)(2,1)} %lay_out.2.refs_0_), custom_call_target="tpu_custom_call", output_to_operand_aliasing={{}: (2, {})} | custom-call | bytes 67108864 | tf_op jit(solution)/shard_map/lay_out/pallas_call | solution.py:343
  91.6 0.9 multiply_rsqrt_fusion.wa_ref
  92.5 1.8 fusion.5.wm_ref
  94.3 5.2 %all-to-all-start.2 = ((f16[8,8,64,128]{3,2,1,0:T(8,128)(2,1)}), f16[8,8,64,128]{3,2,1,0:T(8,128)(2,1)S(1)}, u32[]{:S(2)}, u32[]{:S(2)}) async-start(f16[8,8,64,128]{3,2,1,0:T(8,128)(2,1)} %bitcast.57), calls=%async_computation.2 | async-start | bytes 2097152 | tf_op jit(solution)/shard_map/all_to_all | solution.py:410
  99.5 1.5 convert_multiply_fusion.2.y_ref
  101.0 10.6 %second_section.2 = bf16[8,1,2,64,512]{4,3,2,1,0:T(8,128)(2,1)} custom-call(f32[8,1,512,128]{3,2,1,0:T(8,128)} %convert_multiply_fusion.2.y_ref, f32[256,1024]{1,0:T(8,128)} %constant.94.clone.tc_ref, f32[256,1024]{1,0:T(8,128)} %constant.95.clone.ts_ref, f32[1,1024]{1,0:T(1,128)} %constant.96.clone.ec_ref, f32[1,1024]{1,0:T(1,128)} %constant.97.clone.es_ref, ...), custom_call_target="tpu_custom_call" | custom-call | flops 3321888768 | bytes 3145728 | tf_op jit(solution)/shard_map/second_section/pallas_call | solution.py:177
  111.6 14.5 %all-to-all-done.2 = f16[8,8,64,128]{3,2,1,0:T(8,128)(2,1)S(1)} async-done(((f16[8,8,64,128]{3,2,1,0:T(8,128)(2,1)}), f16[8,8,64,128]{3,2,1,0:T(8,128)(2,1)S(1)}, u32[]{:S(2)}, u32[]{:S(2)}) %all-to-all-start.2) | async-done | bytes 1048608 | tf_op jit(solution)/shard_map/all_to_all | solution.py:410
  126.1 3.6 all-to-all-start.3
  129.7 0.3 convert_multiply_fusion.1.x_ref
  129.9 2.6 first_section.3
  132.5 0.2 fusion.7
  132.7 23.4 %all-to-all-done.3 = bf16[8,1,2,64,512]{4,3,2,1,0:T(8,128)(2,1)S(1)} async-done(((bf16[8,1,2,64,512]{4,3,2,1,0:T(8,128)(2,1)}), bf16[8,1,2,64,512]{4,3,2,1,0:T(8,128)(2,1)S(1)}, u32[]{:S(2)}, u32[]{:S(2)}) %all-to-all-start.3) | async-done | bytes 1048608 | tf_op jit(solution)/shard_map/all_to_all | solution.py:410
  156.2 29.0 %all_to_all.35 = f16[8,1,512,128]{3,2,1,0:T(8,128)(2,1)S(1)} all-to-all(f16[8,1,512,128]{3,2,1,0:T(8,128)(2,1)S(1)} %bitcast.55), channel_id=1, replica_groups=mesh['tmpl'=4,'freq'=8] {'freq'}, dimensions={0} | all-to-all | bytes 2097152 | tf_op jit(solution)/shard_map/all_to_all | solution.py:410
  185.2 1.5 convert_multiply_fusion.y_ref
  186.7 10.5 %second_section.3 = bf16[8,1,2,64,512]{4,3,2,1,0:T(8,128)(2,1)} custom-call(f32[8,1,512,128]{3,2,1,0:T(8,128)} %convert_multiply_fusion.y_ref, f32[256,1024]{1,0:T(8,128)} %constant.94.clone.tc_ref, f32[256,1024]{1,0:T(8,128)} %constant.95.clone.ts_ref, f32[1,1024]{1,0:T(1,128)} %constant.96.clone.ec_ref, f32[1,1024]{1,0:T(1,128)} %constant.97.clone.es_ref, ...), custom_call_target="tpu_custom_call" | custom-call | flops 3321888768 | bytes 3145728 | tf_op jit(solution)/shard_map/second_section/pallas_call | solution.py:177
  197.2 3.6 all-to-all-start.5
  200.9 0.4 copy.67
  201.5 1.6 collective-permute-start
  203.0 1.5 collective-permute-start.1
  204.6 0.5 collective-permute-start.2
  205.0 0.4 copy.66
  205.6 1.6 collective-permute-start.3
  207.1 1.5 collective-permute-start.4
  208.7 7.6 %collective-permute-done.b_ref = bf16[64,8,512]{2,1,0:T(8,128)(2,1)S(1)} collective-permute-done((bf16[64,8,512]{2,1,0:T(8,128)(2,1)S(1)}, bf16[64,8,512]{2,1,0:T(8,128)(2,1)S(1)}, u32[]{:S(2)}, u32[]{:S(2)}) %collective-permute-start) | collective-permute-done | bytes 524320 | tf_op jit(solution)/shard_map/ppermute | solution.py:305
  216.3 2.5 collective-permute-start.5
  218.7 10.4 %collective-permute-done.1.x_ref = bf16[64,8,512]{2,1,0:T(8,128)(2,1)} collective-permute-done((bf16[64,8,512]{2,1,0:T(8,128)(2,1)S(1)}, bf16[64,8,512]{2,1,0:T(8,128)(2,1)}, u32[]{:S(2)}, u32[]{:S(2)}) %collective-permute-start.1) | collective-permute-done | bytes 524320 | tf_op jit(solution)/shard_map/ppermute | solution.py:305
  229.2 36.1 %lag_products.4 = f32[16,32,256]{2,1,0:T(8,128)} custom-call(s32[1]{0:T(128)} %bitcast.6.place_ref, bf16[64,8,512]{2,1,0:T(8,128)(2,1)} %copy-done.5, bf16[64,8,512]{2,1,0:T(8,128)(2,1)} %copy-done.13, bf16[64,8,512]{2,1,0:T(8,128)(2,1)} %collective-permute-done.1.x_ref, bf16[64,8,512]{2,1,0:T(8,128)(2,1)} %collective-permute-done.2.y_ref, ...), custom_call_target="tpu_custom_call" | custom-call | flops 12884901888 | bytes 35651584 | tf_op jit(solution)/shard_map/lag_products/pallas_call | solution.py:271
  265.3 0.8 copy-done.15
  266.1 35.9 %lag_products.5 = f32[16,32,256]{2,1,0:T(8,128)} custom-call(s32[1]{0:T(128)} %bitcast.6.place_ref, bf16[64,8,512]{2,1,0:T(8,128)(2,1)} %copy-done.6, bf16[64,8,512]{2,1,0:T(8,128)(2,1)} %copy-done.15, bf16[64,8,512]{2,1,0:T(8,128)(2,1)} %collective-permute-done.4.x_ref, bf16[64,8,512]{2,1,0:T(8,128)(2,1)} %collective-permute-done.5.y_ref, ...), custom_call_target="tpu_custom_call" | custom-call | flops 12884901888 | bytes 35651584 | tf_op jit(solution)/shard_map/lag_products/pallas_call | solution.py:271
  302.1 0.4 copy.65
  302.7 1.0 collective-permute-start.6
  303.7 1.1 collective-permute-start.7
  304.8 1.4 collective-permute-start.8
  306.2 0.4 copy.64
  306.8 1.0 collective-permute-start.9
  307.8 1.1 collective-permute-start.10
  308.9 0.3 reduce-scatter.8.cloned.1.call-start
  309.2 8.4 %collective-permute-done.6.b_ref = bf16[64,8,512]{2,1,0:T(8,128)(2,1)S(1)} collective-permute-done((bf16[64,8,512]{2,1,0:T(8,128)(2,1)S(1)}, bf16[64,8,512]{2,1,0:T(8,128)(2,1)S(1)}, u32[]{:S(2)}, u32[]{:S(2)}) %collective-permute-start.6) | collective-permute-done | bytes 524320 | tf_op jit(solution)/shard_map/ppermute | solution.py:305
  317.6 1.5 collective-permute-start.11
  319.1 10.6 %collective-permute-done.7.x_ref = bf16[64,8,512]{2,1,0:T(8,128)(2,1)S(1)} collective-permute-done((bf16[64,8,512]{2,1,0:T(8,128)(2,1)S(1)}, bf16[64,8,512]{2,1,0:T(8,128)(2,1)S(1)}, u32[]{:S(2)}, u32[]{:S(2)}) %collective-permute-start.7) | collective-permute-done | bytes 524320 | tf_op jit(solution)/shard_map/ppermute | solution.py:305
  330.0 0.6 copy-done.14
  330.6 35.9 %lag_products.6 = f32[16,32,256]{2,1,0:T(8,128)} custom-call(s32[1]{0:T(128)} %bitcast.6.place_ref, bf16[64,8,512]{2,1,0:T(8,128)(2,1)} %copy-done.4, bf16[64,8,512]{2,1,0:T(8,128)(2,1)} %copy-done.12, bf16[64,8,512]{2,1,0:T(8,128)(2,1)} %copy-done.14, bf16[64,8,512]{2,1,0:T(8,128)(2,1)} %collective-permute-done.8.y_ref, bf16[16,512,2048]{2,1,0:T(8,128)(2,1)} %bitcast.53, ...), custom_call_target="tpu_custom_call" | custom-call | flops 12884901888 | bytes 35651584 | tf_op jit(solution)/shard_map/lag_products/pallas_call | solution.py:271
  366.5 0.8 copy-done.10
  367.5 35.9 %lag_products.7 = f32[16,32,256]{2,1,0:T(8,128)} custom-call(s32[1]{0:T(128)} %bitcast.6.place_ref, bf16[64,8,512]{2,1,0:T(8,128)(2,1)} %copy-done.3, bf16[64,8,512]{2,1,0:T(8,128)(2,1)} %copy-done.10, bf16[64,8,512]{2,1,0:T(8,128)(2,1)} %copy-done.11, bf16[64,8,512]{2,1,0:T(8,128)(2,1)} %collective-permute-done.11.y_ref, bf16[16,512,2048]{2,1,0:T(8,128)(2,1)} %bitcast.54, ...), custom_call_target="tpu_custom_call" | custom-call | flops 12884901888 | bytes 35651584 | tf_op jit(solution)/shard_map/lag_products/pallas_call | solution.py:271
  403.3 20.4 %all_to_all.36 = f32[8,2,32,256]{3,2,1,0:T(8,128)S(1)} all-to-all(f32[8,2,32,256]{3,2,1,0:T(8,128)} %bitcast.67), channel_id=1, replica_groups=mesh['tmpl'=4,'freq'=8] {'freq'}, dimensions={0} | all-to-all | bytes 1048576 | tf_op jit(solution)/shard_map/all_to_all | solution.py:410
  423.8 1.6 pad_maximum_fusion
  (61 shorter events, 1.7 us)
Async XLA Ops:
  16.0 8.4 %copy-start.8 = (s32[256]{0:T(256)S(1)}, s32[256]{0:T(256)}, u32[]{:S(2)}) copy-start(s32[256]{0:T(256)} %param.20) | copy-start | bytes 3076
  17.3 41.3 %all-to-all-start = ((f16[8,8,64,128]{3,2,1,0:T(8,128)(2,1)}), f16[8,8,64,128]{3,2,1,0:T(8,128)(2,1)S(1)}, u32[]{:S(2)}, u32[]{:S(2)}) async-start(f16[8,8,64,128]{3,2,1,0:T(8,128)(2,1)} %bitcast.46), calls=%async_computation | async-start | bytes 2097152 | tf_op jit(solution)/shard_map/all_to_all | solution.py:410
  23.7 49.3 %all-gather.2.cloned.1.call-start = ((), (), s32[]{:S(2)}) async-start(), calls=%async_computation.10 | async-start | bytes 1179648 | tf_op jit(solution)/shard_map/all_gather | solution.py:473
  41.6 17.3 %copy-start = (bf16[512,512]{1,0:T(8,128)(2,1)S(1)}, bf16[512,512]{1,0:T(8,128)(2,1)}, u32[]{:S(2)}) copy-start(bf16[512,512]{1,0:T(8,128)(2,1)} %constant.92.clone.high_ref) | copy-start | bytes 1572868
  41.6 17.3 %copy-start.1 = (bf16[512,512]{1,0:T(8,128)(2,1)S(1)}, bf16[512,512]{1,0:T(8,128)(2,1)}, u32[]{:S(2)}) copy-start(bf16[512,512]{1,0:T(8,128)(2,1)} %constant.93.clone.low_ref) | copy-start | bytes 1572868
  62.8 31.5 %all-to-all-start.1 = ((f16[8,1,512,128]{3,2,1,0:T(8,128)(2,1)}), f16[8,1,512,128]{3,2,1,0:T(8,128)(2,1)S(1)}, u32[]{:S(2)}, u32[]{:S(2)}) async-start(f16[8,1,512,128]{3,2,1,0:T(8,128)(2,1)} %fusion.6), calls=%async_computation.1 | async-start | bytes 2097152 | tf_op jit(solution)/shard_map/all_to_all | solution.py:410
  66.4 3.5 copy-start.9
  74.2 18.2 %copy-start.2 = (f32[512,512]{0,1:T(8,128)S(1)}, f32[512,512]{0,1:T(8,128)}, u32[]{:S(2)}) copy-start(f32[512,512]{0,1:T(8,128)} %all-gather.2.cloned.1.call-done) | copy-start | bytes 3145732
  74.2 18.2 %copy-start.7 = (f32[256,256]{1,0:T(8,128)S(1)}, f32[256,256]{1,0:T(8,128)}, u32[]{:S(2)}) copy-start(f32[256,256]{1,0:T(8,128)} %constant.91.clone) | copy-start | bytes 786436
  94.3 31.8 %all-to-all-start.2 = ((f16[8,8,64,128]{3,2,1,0:T(8,128)(2,1)}), f16[8,8,64,128]{3,2,1,0:T(8,128)(2,1)S(1)}, u32[]{:S(2)}, u32[]{:S(2)}) async-start(f16[8,8,64,128]{3,2,1,0:T(8,128)(2,1)} %bitcast.57), calls=%async_computation.2 | async-start | bytes 2097152 | tf_op jit(solution)/shard_map/all_to_all | solution.py:410
  126.1 30.1 %all-to-all-start.3 = ((bf16[8,1,2,64,512]{4,3,2,1,0:T(8,128)(2,1)}), bf16[8,1,2,64,512]{4,3,2,1,0:T(8,128)(2,1)S(1)}, u32[]{:S(2)}, u32[]{:S(2)}) async-start(bf16[8,1,2,64,512]{4,3,2,1,0:T(8,128)(2,1)} %second_section.2), calls=%async_computation.3 | async-start | bytes 2097152 | tf_op jit(solution)/shard_map/all_to_all | solution.py:410
  197.2 68.1 %all-to-all-start.5 = ((bf16[8,1,2,64,512]{4,3,2,1,0:T(8,128)(2,1)}), bf16[8,1,2,64,512]{4,3,2,1,0:T(8,128)(2,1)S(1)}, u32[]{:S(2)}, u32[]{:S(2)}) async-start(bf16[8,1,2,64,512]{4,3,2,1,0:T(8,128)(2,1)} %second_section.3), calls=%async_computation.5 | async-start | bytes 2097152 | tf_op jit(solution)/shard_map/all_to_all | solution.py:410
  200.8 223.0 %reduce-scatter.6.cloned.1.call-start = ((), (), s32[]{:S(2)}) async-start(), calls=%async_computation.12 | async-start | bytes 589824 | tf_op jit(solution)/shard_map/reduce_scatter | solution.py:510
  201.5 27.7 %copy-start.5 = (bf16[64,8,512]{2,1,0:T(8,128)(2,1)}, bf16[64,8,512]{2,1,0:T(8,128)(2,1)S(1)}, u32[]{:S(2)}) copy-start(bf16[64,8,512]{2,1,0:T(8,128)(2,1)S(1)} %reshape.166.a_ref) | copy-start | bytes 1572868
  201.5 14.8 %collective-permute-start = (bf16[64,8,512]{2,1,0:T(8,128)(2,1)S(1)}, bf16[64,8,512]{2,1,0:T(8,128)(2,1)S(1)}, u32[]{:S(2)}, u32[]{:S(2)}) collective-permute-start(bf16[64,8,512]{2,1,0:T(8,128)(2,1)S(1)} %reshape.166.a_ref), channel_id=1, source_target_pairs={{0,8},{8,0},{16,24},{24,16},{1,9},{9,1},{17,25},{25,17},{2,10},{10... | collective-permute-start | bytes 1572872 | tf_op jit(solution)/shard_map/ppermute | solution.py:305
  203.0 26.1 %collective-permute-start.1 = (bf16[64,8,512]{2,1,0:T(8,128)(2,1)S(1)}, bf16[64,8,512]{2,1,0:T(8,128)(2,1)}, u32[]{:S(2)}, u32[]{:S(2)}) collective-permute-start(bf16[64,8,512]{2,1,0:T(8,128)(2,1)S(1)} %reshape.166.a_ref), channel_id=1, source_target_pairs={{0,16},{8,24},{16,0},{24,8},{1,17},{9,25},{17,1},{25,9},{2,18},{10... | collective-permute-start | bytes 1572872 | tf_op jit(solution)/shard_map/ppermute | solution.py:305
  204.6 24.6 %collective-permute-start.2 = (bf16[64,8,512]{2,1,0:T(8,128)(2,1)S(1)}, bf16[64,8,512]{2,1,0:T(8,128)(2,1)}, u32[]{:S(2)}, u32[]{:S(2)}) collective-permute-start(bf16[64,8,512]{2,1,0:T(8,128)(2,1)S(1)} %reshape.166.a_ref), channel_id=1, source_target_pairs={{0,24},{8,16},{16,8},{24,0},{1,25},{9,17},{17,9},{25,1},{2,26},{10... | collective-permute-start | bytes 1572872 | tf_op jit(solution)/shard_map/ppermute | solution.py:305
  205.6 59.7 %copy-start.6 = (bf16[64,8,512]{2,1,0:T(8,128)(2,1)}, bf16[64,8,512]{2,1,0:T(8,128)(2,1)S(1)}, u32[]{:S(2)}) copy-start(bf16[64,8,512]{2,1,0:T(8,128)(2,1)S(1)} %reshape.168.a_ref) | copy-start | bytes 1572868
  205.6 59.7 %collective-permute-start.3 = (bf16[64,8,512]{2,1,0:T(8,128)(2,1)S(1)}, bf16[64,8,512]{2,1,0:T(8,128)(2,1)S(1)}, u32[]{:S(2)}, u32[]{:S(2)}) collective-permute-start(bf16[64,8,512]{2,1,0:T(8,128)(2,1)S(1)} %reshape.168.a_ref), channel_id=1, source_target_pairs={{0,8},{8,0},{16,24},{24,16},{1,9},{9,1},{17,25},{25,17},{2,10},{10... | collective-permute-start | bytes 1572872 | tf_op jit(solution)/shard_map/ppermute | solution.py:305
  207.1 58.2 %collective-permute-start.4 = (bf16[64,8,512]{2,1,0:T(8,128)(2,1)S(1)}, bf16[64,8,512]{2,1,0:T(8,128)(2,1)}, u32[]{:S(2)}, u32[]{:S(2)}) collective-permute-start(bf16[64,8,512]{2,1,0:T(8,128)(2,1)S(1)} %reshape.168.a_ref), channel_id=1, source_target_pairs={{0,16},{8,24},{16,0},{24,8},{1,17},{9,25},{17,1},{25,9},{2,18},{10... | collective-permute-start | bytes 1572872 | tf_op jit(solution)/shard_map/ppermute | solution.py:305
  216.3 12.9 %copy-start.13 = (bf16[64,8,512]{2,1,0:T(8,128)(2,1)}, bf16[64,8,512]{2,1,0:T(8,128)(2,1)S(1)}, u32[]{:S(2)}) copy-start(bf16[64,8,512]{2,1,0:T(8,128)(2,1)S(1)} %collective-permute-done.b_ref) | copy-start | bytes 1572868
  216.3 49.1 %collective-permute-start.5 = (bf16[64,8,512]{2,1,0:T(8,128)(2,1)S(1)}, bf16[64,8,512]{2,1,0:T(8,128)(2,1)}, u32[]{:S(2)}, u32[]{:S(2)}) collective-permute-start(bf16[64,8,512]{2,1,0:T(8,128)(2,1)S(1)} %reshape.168.a_ref), channel_id=1, source_target_pairs={{0,24},{8,16},{16,8},{24,0},{1,25},{9,17},{17,9},{25,1},{2,26},{10... | collective-permute-start | bytes 1572872 | tf_op jit(solution)/shard_map/ppermute | solution.py:305
  265.3 0.8 copy-start.15
  302.0 121.8 %reduce-scatter.4.cloned.1.call-start = ((), (), s32[]{:S(2)}) async-start(), calls=%async_computation.11 | async-start | bytes 589824 | tf_op jit(solution)/shard_map/reduce_scatter | solution.py:510
  302.7 27.3 %copy-start.4 = (bf16[64,8,512]{2,1,0:T(8,128)(2,1)}, bf16[64,8,512]{2,1,0:T(8,128)(2,1)S(1)}, u32[]{:S(2)}) copy-start(bf16[64,8,512]{2,1,0:T(8,128)(2,1)S(1)} %reshape.170.a_ref) | copy-start | bytes 1572868
  302.7 14.9 %collective-permute-start.6 = (bf16[64,8,512]{2,1,0:T(8,128)(2,1)S(1)}, bf16[64,8,512]{2,1,0:T(8,128)(2,1)S(1)}, u32[]{:S(2)}, u32[]{:S(2)}) collective-permute-start(bf16[64,8,512]{2,1,0:T(8,128)(2,1)S(1)} %reshape.170.a_ref), channel_id=1, source_target_pairs={{0,8},{8,0},{16,24},{24,16},{1,9},{9,1},{17,25},{25,17},{2,10},{10... | collective-permute-start | bytes 1572872 | tf_op jit(solution)/shard_map/ppermute | solution.py:305
  303.7 26.0 %collective-permute-start.7 = (bf16[64,8,512]{2,1,0:T(8,128)(2,1)S(1)}, bf16[64,8,512]{2,1,0:T(8,128)(2,1)S(1)}, u32[]{:S(2)}, u32[]{:S(2)}) collective-permute-start(bf16[64,8,512]{2,1,0:T(8,128)(2,1)S(1)} %reshape.170.a_ref), channel_id=1, source_target_pairs={{0,16},{8,24},{16,0},{24,8},{1,17},{9,25},{17,1},{25,9},{2,18},{10... | collective-permute-start | bytes 1572872 | tf_op jit(solution)/shard_map/ppermute | solution.py:305
  304.8 25.1 %collective-permute-start.8 = (bf16[64,8,512]{2,1,0:T(8,128)(2,1)S(1)}, bf16[64,8,512]{2,1,0:T(8,128)(2,1)}, u32[]{:S(2)}, u32[]{:S(2)}) collective-permute-start(bf16[64,8,512]{2,1,0:T(8,128)(2,1)S(1)} %reshape.170.a_ref), channel_id=1, source_target_pairs={{0,24},{8,16},{16,8},{24,0},{1,25},{9,17},{17,9},{25,1},{2,26},{10... | collective-permute-start | bytes 1572872 | tf_op jit(solution)/shard_map/ppermute | solution.py:305
  306.8 59.6 %copy-start.3 = (bf16[64,8,512]{2,1,0:T(8,128)(2,1)}, bf16[64,8,512]{2,1,0:T(8,128)(2,1)S(1)}, u32[]{:S(2)}) copy-start(bf16[64,8,512]{2,1,0:T(8,128)(2,1)S(1)} %reshape.171.a_ref) | copy-start | bytes 1572868
  306.8 59.6 %collective-permute-start.9 = (bf16[64,8,512]{2,1,0:T(8,128)(2,1)S(1)}, bf16[64,8,512]{2,1,0:T(8,128)(2,1)S(1)}, u32[]{:S(2)}, u32[]{:S(2)}) collective-permute-start(bf16[64,8,512]{2,1,0:T(8,128)(2,1)S(1)} %reshape.171.a_ref), channel_id=1, source_target_pairs={{0,8},{8,0},{16,24},{24,16},{1,9},{9,1},{17,25},{25,17},{2,10},{10... | collective-permute-start | bytes 1572872 | tf_op jit(solution)/shard_map/ppermute | solution.py:305
  307.8 58.7 %collective-permute-start.10 = (bf16[64,8,512]{2,1,0:T(8,128)(2,1)S(1)}, bf16[64,8,512]{2,1,0:T(8,128)(2,1)S(1)}, u32[]{:S(2)}, u32[]{:S(2)}) collective-permute-start(bf16[64,8,512]{2,1,0:T(8,128)(2,1)S(1)} %reshape.171.a_ref), channel_id=1, source_target_pairs={{0,16},{8,24},{16,0},{24,8},{1,17},{9,25},{17,1},{25,9},{2,18},{10... | collective-permute-start | bytes 1572872 | tf_op jit(solution)/shard_map/ppermute | solution.py:305
  308.9 114.9 %reduce-scatter.8.cloned.1.call-start = ((), (), s32[]{:S(2)}) async-start(), calls=%async_computation.13 | async-start | bytes 589824 | tf_op jit(solution)/shard_map/reduce_scatter | solution.py:510
  317.6 12.3 %copy-start.12 = (bf16[64,8,512]{2,1,0:T(8,128)(2,1)}, bf16[64,8,512]{2,1,0:T(8,128)(2,1)S(1)}, u32[]{:S(2)}) copy-start(bf16[64,8,512]{2,1,0:T(8,128)(2,1)S(1)} %collective-permute-done.6.b_ref) | copy-start | bytes 1572868
  317.6 48.9 %collective-permute-start.11 = (bf16[64,8,512]{2,1,0:T(8,128)(2,1)S(1)}, bf16[64,8,512]{2,1,0:T(8,128)(2,1)}, u32[]{:S(2)}, u32[]{:S(2)}) collective-permute-start(bf16[64,8,512]{2,1,0:T(8,128)(2,1)S(1)} %reshape.171.a_ref), channel_id=1, source_target_pairs={{0,24},{8,16},{16,8},{24,0},{1,25},{9,17},{17,9},{25,1},{2,26},{10... | collective-permute-start | bytes 1572872 | tf_op jit(solution)/shard_map/ppermute | solution.py:305
  329.7 0.8 copy-start.14
  366.4 0.8 copy-start.10
  366.5 1.0 copy-start.11
Sparse Core Ops, SparseCore 0:
  26.1 33.3 all-gather.1
  302.1 31.3 reduce-scatter.5
  335.9 29.0 reduce-scatter.3
  367.1 31.4 reduce-scatter.7

commit v6 on v4

--- a/solution.py
+++ b/solution.py
@@ -192,8 +192,7 @@
 def lag_kernel(place_ref, a_ref, b_ref, x_ref, y_ref, t_ref, c_ref, s_ref, out_ref, acc_ref, even_ref, odd_ref):
     sources = (a_ref, b_ref, x_ref, y_ref)
     segs = a_ref.shape[1] // 2
-    depth = t_ref.shape[2]
-    per_quad = depth // A
+    per_quad = t_ref.shape[0]
     lag_total = c_ref.shape[1]
     tmpl = out_ref.shape[2]
     step = pl.program_id(0)
@@ -205,7 +204,6 @@
             lanes = slice(chunk * 128, (chunk + 1) * 128)
             lag_cos = c_ref[jj, :, lanes]
             lag_sin = s_ref[jj, :, lanes]
-            out_lanes = slice(jj * A + chunk * 128, jj * A + (chunk + 1) * 128)
             for index, source in enumerate(sources):
                 value = source[jj, :, lanes].astype(jnp.float32)
                 for s in range(segs):
@@ -213,39 +211,41 @@
                     imag = value[segs + s : segs + s + 1]
                     first_row = (index * segs + s) * lag_total
                     rows = slice(first_row, first_row + lag_total)
-                    rows_ref[rows, out_lanes] = (real * lag_cos - imag * lag_sin).astype(jnp.bfloat16)
+                    rows_ref[jj, rows, lanes] = (real * lag_cos - imag * lag_sin).astype(jnp.bfloat16)
                     rows = slice(half + first_row, half + first_row + lag_total)
-                    rows_ref[rows, out_lanes] = (real * lag_sin + imag * lag_cos).astype(jnp.bfloat16)
-
-    def multiply(now_ref, next_ref):
-        cut = max(1, per_quad // 2)
-        pieces = [(k, n) for k in range(per_quad // cut) for n in range(2)]
-        for index, (k, n) in enumerate(pieces):
-            if next_ref is not None:
-                for jj in range(per_quad):
-                    if jj * len(pieces) // per_quad == index:
-                        make_rows(next_ref, jj)
-            deep = slice(k * cut * A, (k + 1) * cut * A)
-            cols = slice(n * tmpl, (n + 1) * tmpl)
-            acc_ref[:, cols] += dot_nt(now_ref[:, deep], t_ref[0, cols, deep])
+                    rows_ref[jj, rows, lanes] = (real * lag_sin + imag * lag_cos).astype(jnp.bfloat16)
+
+    def multiply(now_ref, jj):
+        acc_ref[...] += dot_nt(now_ref[jj], t_ref[jj])
 
     @pl.when(step == 0)
     def _():
         acc_ref[...] = jnp.zeros_like(acc_ref)
-        for jj in range(per_quad):
+
+        @pl.loop(0, per_quad)
+        def _(jj):
             make_rows(even_ref, jj)
 
     @pl.when((step % 2 == 1) & (step < last))
     def _():
-        multiply(even_ref, odd_ref)
+        @pl.loop(0, per_quad)
+        def _(jj):
+            make_rows(odd_ref, jj)
+            multiply(even_ref, jj)
 
     @pl.when((step % 2 == 0) & (step > 0) & (step < last))
     def _():
-        multiply(odd_ref, even_ref)
+        @pl.loop(0, per_quad)
+        def _(jj):
+            make_rows(even_ref, jj)
+            multiply(odd_ref, jj)
 
     @pl.when(step == last)
     def _():
-        multiply(odd_ref, None)
+        @pl.loop(0, per_quad)
+        def _(jj):
+            multiply(odd_ref, jj)
+
         shape = (segs, lag_total, tmpl)
         for index in range(len(sources)):
             low = slice(index * segs * lag_total, (index + 1) * segs * lag_total)
@@ -257,8 +257,9 @@
 
 def lag_products(sources, place, laid, lag_cos, lag_sin):
     blocks, rows, _ = sources[0].shape
-    quads, tmpl2, depth = laid.shape
-    per_quad = depth // A
+    tmpl2 = laid.shape[1]
+    per_quad = min(4, blocks)
+    quads = blocks // per_quad
     lag_total = lag_cos.shape[1]
     segs = len(sources) * rows // 2
 
@@ -271,7 +272,7 @@
         in_specs=[pl.BlockSpec(memory_space=pltpu.SMEM)]
         + [pl.BlockSpec((per_quad, rows, A), ahead)] * len(sources)
         + [
-            pl.BlockSpec((1, tmpl2, depth), lambda i: (jnp.maximum(i - 1, 0), 0, 0)),
+            pl.BlockSpec((per_quad, tmpl2, A), lambda i: (jnp.maximum(i - 1, 0), 0, 0)),
             pl.BlockSpec((per_quad, lag_total, A), ahead),
             pl.BlockSpec((per_quad, lag_total, A), ahead),
         ],
@@ -279,8 +280,8 @@
         out_shape=jax.ShapeDtypeStruct((segs, 2 * lag_total, tmpl2 // 2), jnp.float32),
         scratch_shapes=[
             pltpu.VMEM((2 * segs * lag_total, tmpl2), jnp.float32),
-            pltpu.VMEM((2 * segs * lag_total, depth), jnp.bfloat16),
-            pltpu.VMEM((2 * segs * lag_total, depth), jnp.bfloat16),
+            pltpu.VMEM((per_quad, 2 * segs * lag_total, A), jnp.bfloat16),
+            pltpu.VMEM((per_quad, 2 * segs * lag_total, A), jnp.bfloat16),
         ],
         compiler_params=pltpu.CompilerParams(vmem_limit_bytes=60 * 2**20),
         cost_estimate=pl.CostEstimate(
@@ -298,20 +299,13 @@
 
 
 def spread(data):
-    def swap(value, bit):
-        return lax.ppermute(value, "tmpl", [(n, n ^ bit) for n in range(4)])
-
-    middle = data.shape[0] // 2
-    first = swap(data, 1)
-    second = swap(data, 2)
-    corner = jnp.concatenate([swap(first[:middle], 2), swap(second[middle:], 1)], axis=0)
-    return data, first, second, corner
+    moved = [lax.ppermute(data, "tmpl", [(n, n ^ bit) for n in range(4)]) for bit in (1, 2, 3)]
+    return (data, *moved)
 
 
 def layout_kernel(cut_ref, t_ref, *refs):
     out_ref = refs[-1]
     tmpl, _, rows, _ = t_ref.shape
-    per_quad = out_ref.shape[3] // A
     first_row = pl.program_id(0) * rows + cut_ref[cut_ref.shape[0] - 1]
     first_tmpl = pl.program_id(1) * tmpl
     row_ids = lax.broadcasted_iota(jnp.int32, (rows, 128), 0) + first_row
@@ -328,16 +322,15 @@
                 value = jnp.stack([jnp.where(keeps[n], value[n], 0.0) for n in range(batch)], axis=0)
                 value = jnp.swapaxes(value, 0, 1).astype(jnp.bfloat16)
                 for row in range(rows):
-                    start = row % per_quad * A + chunk * 128
-                    out_ref[row // per_quad, part, some, start : start + 128] = value[row]
-
-
-def lay_out(templates, cuts, per_quad, piece, pieces, laid):
+                    out_ref[row, part, some, lanes] = value[row]
+
+
+def lay_out(templates, cuts, piece, pieces, laid):
     tmpl, _, blocks, _ = templates.shape
     rows = min(16, blocks)
     steps = blocks // rows // pieces
     batch = min(64, tmpl)
-    shape = (blocks // per_quad, 2, tmpl, per_quad * A)
+    shape = (blocks, 2, tmpl, A)
     first = piece * steps
     info = jnp.concatenate([cuts, jnp.full((1,), first * rows, jnp.int32)])
     earlier = () if laid is None else (laid,)
@@ -349,9 +342,7 @@
             pl.BlockSpec((batch, 2, rows, A), lambda i, j: (j, 0, i + first, 0)),
         ]
         + [pl.BlockSpec(memory_space=pl.ANY)] * len(earlier),
-        out_specs=pl.BlockSpec(
-            (rows // per_quad, 2, batch, per_quad * A), lambda i, j: (i + first, 0, j, 0)
-        ),
+        out_specs=pl.BlockSpec((rows, 2, batch, A), lambda i, j: (i + first, 0, j, 0)),
         out_shape=jax.ShapeDtypeStruct(shape, jnp.bfloat16),
         input_output_aliases={2: 0} if earlier else {},
         compiler_params=pltpu.CompilerParams(vmem_limit_bytes=40 * 2**20),
@@ -437,8 +428,6 @@
     blocks_here = templates.shape[2]
     first_block = freq_index * blocks_here
     block_ids = first_block + jnp.arange(blocks_here, dtype=jnp.int32)
-    per_quad = min(4, blocks_here)
-    quads = blocks_here // per_quad
     cuts = cutoffs - first_block
     tied = lax.optimization_barrier
 
@@ -459,8 +448,8 @@
         and B // freq_count == 128
     )
     if not sliced:
-        laid = lay_out(templates, cuts, per_quad, 0, 1, None)
-        laid = laid.reshape(quads, 2 * tmpl_local, per_quad * A)
+        laid = lay_out(templates, cuts, 0, 1, None)
+        laid = laid.reshape(blocks_here, 2 * tmpl_local, A)
         data = lax.all_gather(general_transform(strain, psd), "tmpl", axis=0, tiled=True)
         origin = jnp.zeros((1,), jnp.int32)
         sums = []
@@ -485,11 +474,11 @@
         for group in range(2)
     )
     time_a = exchange(strain_a)
-    laid = lay_out(templates, cuts, per_quad, 0, 2, None)
+    laid = lay_out(templates, cuts, 0, 2, None)
     time_a, laid = tied((time_a, laid))
     coefs_a = pack_coefs(time_a, first)
     parts_a = exchange(coefs_a)
-    laid = lay_out(templates, cuts, per_quad, 1, 2, laid)
+    laid = lay_out(templates, cuts, 1, 2, laid)
     parts_a, strain_b, laid, white, white_far, lag_cos, lag_sin = tied(
         (parts_a, strain_b, laid, white, white_far, lag_cos, lag_sin)
     )
@@ -500,30 +489,42 @@
     coefs_b = pack_coefs(time_b, first)
     data_a, coefs_b = tied((data_a, coefs_b))
     parts_b = exchange(coefs_b)
-    laid = laid.reshape(quads, 2 * tmpl_local, per_quad * A)
+    laid = laid.reshape(blocks_here, 2 * tmpl_local, A)
     place = lax.axis_index("tmpl").astype(jnp.int32).reshape(1)
 
     def halves(data):
         data = data.reshape(2, 2, 2, 2, blocks_here, A)
-        return [spread(block_rows(data[:, n].reshape(4, 2, blocks_here, A))) for n in range(2)]
+        return [block_rows(data[:, n].reshape(4, 2, blocks_here, A)) for n in range(2)]
+
+    def products(part):
+        return lag_products(part, place, laid, lag_cos, lag_sin)
 
     def collect(sums):
         return lax.psum_scatter(sums, "freq", scatter_dimension=0, tiled=True)
 
+    def collect_late(sums):
+        shares = exchange(sums.reshape(freq_count, 2, 2 * lags.shape[0], tmpl_local))
+        return jnp.sum(shares, axis=0)
+
     first_a, second_a = halves(data_a)
-    white_b = whiten(parts_b, second, white, white_far)
-    first_a = tied((first_a, white_b))[0]
-    data_b = exchange(white_b)
-    sums_a = lag_products(first_a, place, laid, lag_cos, lag_sin)
-    data_b, sums_a = tied((data_b, sums_a))
+    first_a = spread(first_a)
+    parts_b, first_a, second_a = tied((parts_b, first_a, second_a))
+    second_a = spread(second_a)
+    data_b = exchange(whiten(parts_b, second, white, white_far))
+    sums_a1 = products(first_a)
+    data_b, second_a, sums_a1 = tied((data_b, second_a, sums_a1))
     first_b, second_b = halves(data_b)
-    sums = [sums_a] + [
-        lag_products(part, place, laid, lag_cos, lag_sin) for part in (second_a, first_b, second_b)
-    ]
-    outputs = [collect(part) for part in sums[:3]]
-    shares = exchange(sums[3].reshape(freq_count, 2, 2 * lags.shape[0], tmpl_local))
-    outputs.append(jnp.sum(shares, axis=0))
-    return jnp.concatenate(outputs, axis=0)
+    first_b = spread(first_b)
+    out_a1 = collect(sums_a1)
+    sums_a2 = products(second_a)
+    first_b, second_b, sums_a2 = tied((first_b, second_b, sums_a2))
+    second_b = spread(second_b)
+    out_a2 = collect(sums_a2)
+    sums_b1 = products(first_b)
+    second_b, sums_b1 = tied((second_b, sums_b1))
+    out_b1 = collect_late(sums_b1)
+    out_b2 = collect_late(products(second_b))
+    return jnp.concatenate([out_a1, out_a2, out_b1, out_b2], axis=0)
 
 
 def solution(mesh):

time: 422 us -> 413 us (0.979); the launches traced: 415 us -> 412 us
  blocking collectives: 20.4 us -> 0 us
  waiting for transfers between devices: 93.2 us -> 112 us
  Pallas kernels: 197 us -> 203 us
  other arithmetic: 21.1 us -> 15.8 us
    all_to_all x6 -> x8, waiting for transfers between devices: 54 us -> 87.3 us  [exchange(): return lax.all_to_all(sent, 'freq', split_axis=0, concat_axis=0, tiled=True)]
    all_to_all x1 -> x0, blocking collectives: 20.4 us -> none  [exchange(): return lax.all_to_all(sent, 'freq', split_axis=0, concat_axis=0, tiled=True)]
    ppermute x16 -> x12, waiting for transfers between devices: 38.4 us -> 22.8 us  [spread(): lax.ppermute(data, 'tmpl', [(n, n ^ bit) for n in range(4)])]
    all_to_all x6 -> x8, starting transfers between devices: 27.8 us -> 35.2 us  [exchange(): return lax.all_to_all(sent, 'freq', split_axis=0, concat_axis=0, tiled=True)]
    pallas_call x4, Pallas kernels: 136 us -> 142 us  [lag_products(): pl.pallas_call(lag_kernel, grid=(quads + 1,), in_specs=[pl.BlockSpec(memo...]
    slice x8 -> x0, local copies, waits for them, and re-layouts: 5.84 us -> none  [the longest x4 3.87 us: spread(): first[:middle]]
    concatenate x5 -> x1, other arithmetic: 7.01 us -> 1.6 us  [on_device(): return jnp.concatenate([out_a1, out_a2, out_b1, out_b2], axis=0)]
    ppermute x16 -> x12, starting transfers between devices: 19 us -> 14.2 us  [spread(): lax.ppermute(data, 'tmpl', [(n, n ^ bit) for n in range(4)])]
  transfers between devices with their start and end apart: 26 -> 23, of which waited for: 9 -> 7; matrix products, arithmetic and copies ran while one was open for 7% -> 4% of each run, Pallas kernels for 47% -> 47%
where the time goes in v6:
time: 413 us; the launch traced here: 412 us
  Pallas kernels  203 us (49%)
  waiting for transfers between devices  112 us (27%)
  starting transfers between devices  49.6 us (12%)
  local copies, waits for them, and re-layouts  16.4 us (4%)
  other arithmetic  15.8 us (4%)
  between operations  13.6 us (3%)
    pallas_call x4, Pallas kernels, lag_products(): pl.pallas_call(lag_kernel, grid=(quads + 1,), in_specs=[pl.BlockSpec(memo...  142 us
    all_to_all x8, waiting for transfers between devices, exchange(): return lax.all_to_all(sent, 'freq', split_axis=0, concat_axis=0, tiled=True)  87.3 us
    all_to_all x8, starting transfers between devices, exchange(): return lax.all_to_all(sent, 'freq', split_axis=0, concat_axis=0, tiled=True)  35.2 us
    pallas_call x2, Pallas kernels, lay_out(): pl.pallas_call(layout_kernel, grid=(steps, tmpl // batch), in_specs=[pl.B...  34.5 us
    ppermute x12, waiting for transfers between devices, spread(): lax.ppermute(data, 'tmpl', [(n, n ^ bit) for n in range(4)])  22.8 us
    pallas_call x2, Pallas kernels, second_section(): pl.pallas_call(second_kernel, grid=(segs,), in_specs=[pl.BlockSpec((parts...  21.1 us
    ppermute x12, starting transfers between devices, spread(): lax.ppermute(data, 'tmpl', [(n, n ^ bit) for n in range(4)])  14.2 us
  transfers between devices with their start and end apart: 23, of which 7 were waited for; matrix products, arithmetic and copies ran while one was open for 4% of the time, Pallas kernels for 47%

profile of v6, /device:TPU:0, one launch (start us, length us, event | category | flops | bytes accessed | tf_op | source)
XLA Modules:
  0.0 411.9 jit_solution(4290011159660270448)
XLA Ops:
  6.5 4.2 %reshape.164 = f32[2,2,4,65536]{3,2,1,0:T(4,128)} reshape(f32[16,65536]{1,0:T(8,128)} %param.17) | data formatting | bytes 8388608 | tf_op jit(solution)/shard_map/reshape | solution.py:471
  10.7 4.1 %fusion.1 = (f16[2,1,4,65536]{3,2,0,1:T(4,128)(2,1)}, f16[2,1,4,65536]{3,2,0,1:T(4,128)(2,1)S(1)}) fusion(f32[2,2,4,65536]{3,2,1,0:T(4,128)} %reshape.164), kind=kLoop, calls=%fused_computation.2 | loop fusion | flops 2097152 | bytes 6291456 | tf_op jit(solution)/shard_map/convert_element_type | solution.py:407
  14.9 1.1 convert_element_type.53
  16.0 1.3 copy.63
  17.3 6.3 %all-to-all-start = ((f16[8,8,64,128]{3,2,1,0:T(8,128)(2,1)}), f16[8,8,64,128]{3,2,1,0:T(8,128)(2,1)S(1)}, u32[]{:S(2)}, u32[]{:S(2)}) async-start(f16[8,8,64,128]{3,2,1,0:T(8,128)(2,1)} %bitcast.47), calls=%async_computation | async-start | bytes 2097152 | tf_op jit(solution)/shard_map/all_to_all | solution.py:402
  23.7 0.7 all-gather.2.cloned.1.call-update
  24.4 17.2 %lay_out.2.refs_0_ = bf16[64,2,256,512]{3,2,1,0:T(8,128)(2,1)} custom-call(s32[257]{0:T(512)S(1)} %get-tuple-element.88.cut_ref, bf16[256,2,64,512]{3,2,1,0:T(8,128)(2,1)} %t_ref.3), custom_call_target="tpu_custom_call" | custom-call | bytes 67108864 | tf_op jit(solution)/shard_map/lay_out/pallas_call | solution.py:337
  41.6 17.0 %all-to-all-done = f16[8,8,64,128]{3,2,1,0:T(8,128)(2,1)S(1)} async-done(((f16[8,8,64,128]{3,2,1,0:T(8,128)(2,1)}), f16[8,8,64,128]{3,2,1,0:T(8,128)(2,1)S(1)}, u32[]{:S(2)}, u32[]{:S(2)}) %all-to-all-start) | async-done | bytes 1048608 | tf_op jit(solution)/shard_map/all_to_all | solution.py:402
  58.7 0.3 convert_multiply_fusion.3.x_ref
  59.0 2.6 first_section.2
  61.5 1.3 fusion.6
  62.8 3.6 all-to-all-start.1
  66.4 2.2 convert_element_type.57
  68.6 1.3 copy.62
  70.3 2.6 multiply_add_fusion
  73.0 1.1 slice.34
  74.3 17.3 %lay_out.3 = bf16[64,2,256,512]{3,2,1,0:T(8,128)(2,1)} custom-call(s32[257]{0:T(512)S(1)} %get-tuple-element.87.cut_ref, bf16[256,2,64,512]{3,2,1,0:T(8,128)(2,1)} %t_ref.3, bf16[64,2,256,512]{3,2,1,0:T(8,128)(2,1)} %lay_out.2.refs_0_), custom_call_target="tpu_custom_call", output_to_operand_aliasing={{}: (2, {})} | custom-call | bytes 67108864 | tf_op jit(solution)/shard_map/lay_out/pallas_call | solution.py:337
  91.6 0.9 multiply_rsqrt_fusion.wa_ref
  92.5 1.8 fusion.5.wm_ref
  94.3 5.0 %all-to-all-start.2 = ((f16[8,8,64,128]{3,2,1,0:T(8,128)(2,1)}), f16[8,8,64,128]{3,2,1,0:T(8,128)(2,1)S(1)}, u32[]{:S(2)}, u32[]{:S(2)}) async-start(f16[8,8,64,128]{3,2,1,0:T(8,128)(2,1)} %bitcast.56), calls=%async_computation.2 | async-start | bytes 2097152 | tf_op jit(solution)/shard_map/all_to_all | solution.py:402
  99.3 1.5 convert_multiply_fusion.2.y_ref
  100.8 10.5 %second_section.2 = bf16[8,1,2,64,512]{4,3,2,1,0:T(8,128)(2,1)} custom-call(f32[8,1,512,128]{3,2,1,0:T(8,128)} %convert_multiply_fusion.2.y_ref, f32[256,1024]{1,0:T(8,128)} %constant.94.clone.tc_ref, f32[256,1024]{1,0:T(8,128)} %constant.95.clone.ts_ref, f32[1,1024]{1,0:T(1,128)} %constant.96.clone.ec_ref, f32[1,1024]{1,0:T(1,128)} %constant.97.clone.es_ref, ...), custom_call_target="tpu_custom_call" | custom-call | flops 3321888768 | bytes 3145728 | tf_op jit(solution)/shard_map/second_section/pallas_call | solution.py:177
  111.4 14.5 %all-to-all-done.2 = f16[8,8,64,128]{3,2,1,0:T(8,128)(2,1)S(1)} async-done(((f16[8,8,64,128]{3,2,1,0:T(8,128)(2,1)}), f16[8,8,64,128]{3,2,1,0:T(8,128)(2,1)S(1)}, u32[]{:S(2)}, u32[]{:S(2)}) %all-to-all-start.2) | async-done | bytes 1048608 | tf_op jit(solution)/shard_map/all_to_all | solution.py:402
  125.9 3.6 all-to-all-start.3
  129.5 0.3 convert_multiply_fusion.1.x_ref
  129.8 2.6 first_section.3
  132.3 1.2 fusion.7
  133.5 22.5 %all-to-all-done.3 = bf16[8,1,2,64,512]{4,3,2,1,0:T(8,128)(2,1)S(1)} async-done(((bf16[8,1,2,64,512]{4,3,2,1,0:T(8,128)(2,1)}), bf16[8,1,2,64,512]{4,3,2,1,0:T(8,128)(2,1)S(1)}, u32[]{:S(2)}, u32[]{:S(2)}) %all-to-all-start.3) | async-done | bytes 1048608 | tf_op jit(solution)/shard_map/all_to_all | solution.py:402
  156.0 3.6 all-to-all-start.4
  159.7 0.4 copy.67
  160.2 1.6 collective-permute-start
  161.8 1.5 collective-permute-start.1
  163.3 0.5 collective-permute-start.2
  163.8 0.4 copy.66
  164.3 10.8 %collective-permute-done.b_ref = bf16[64,8,512]{2,1,0:T(8,128)(2,1)} collective-permute-done((bf16[64,8,512]{2,1,0:T(8,128)(2,1)S(1)}, bf16[64,8,512]{2,1,0:T(8,128)(2,1)}, u32[]{:S(2)}, u32[]{:S(2)}) %collective-permute-start) | collective-permute-done | bytes 524320 | tf_op jit(solution)/shard_map/ppermute | solution.py:302
  175.1 12.0 %collective-permute-done.1.x_ref = bf16[64,8,512]{2,1,0:T(8,128)(2,1)} collective-permute-done((bf16[64,8,512]{2,1,0:T(8,128)(2,1)S(1)}, bf16[64,8,512]{2,1,0:T(8,128)(2,1)}, u32[]{:S(2)}, u32[]{:S(2)}) %collective-permute-start.1) | collective-permute-done | bytes 524320 | tf_op jit(solution)/shard_map/ppermute | solution.py:302
  187.1 1.5 convert_multiply_fusion.y_ref
  188.6 10.5 %second_section.3 = bf16[8,1,2,64,512]{4,3,2,1,0:T(8,128)(2,1)} custom-call(f32[8,1,512,128]{3,2,1,0:T(8,128)} %convert_multiply_fusion.y_ref, f32[256,1024]{1,0:T(8,128)} %constant.94.clone.tc_ref, f32[256,1024]{1,0:T(8,128)} %constant.95.clone.ts_ref, f32[1,1024]{1,0:T(1,128)} %constant.96.clone.ec_ref, f32[1,1024]{1,0:T(1,128)} %constant.97.clone.es_ref, ...), custom_call_target="tpu_custom_call" | custom-call | flops 3321888768 | bytes 3145728 | tf_op jit(solution)/shard_map/second_section/pallas_call | solution.py:177
  199.1 4.7 %all-to-all-start.5 = ((bf16[8,1,2,64,512]{4,3,2,1,0:T(8,128)(2,1)}), bf16[8,1,2,64,512]{4,3,2,1,0:T(8,128)(2,1)S(1)}, u32[]{:S(2)}, u32[]{:S(2)}) async-start(bf16[8,1,2,64,512]{4,3,2,1,0:T(8,128)(2,1)} %second_section.3), calls=%async_computation.5 | async-start | bytes 2097152 | tf_op jit(solution)/shard_map/all_to_all | solution.py:402
  203.9 1.3 collective-permute-start.3
  205.3 0.8 collective-permute-start.4
  206.1 1.4 collective-permute-start.5
  207.5 35.6 %lag_products.4 = f32[16,32,256]{2,1,0:T(8,128)} custom-call(s32[1]{0:T(128)} %bitcast.11.place_ref, bf16[64,8,512]{2,1,0:T(8,128)(2,1)} %copy-done.4, bf16[64,8,512]{2,1,0:T(8,128)(2,1)} %collective-permute-done.b_ref, bf16[64,8,512]{2,1,0:T(8,128)(2,1)} %collective-permute-done.1.x_ref, bf16[64,8,512]{2,1,0:T(8,128)(2,1)} %collective-permute-done.2.y_ref, ...), custom_call_target="tpu_custom_call" | custom-call | flops 17179869184 | bytes 35651584 | tf_op jit(solution)/shard_map/lag_products/pallas_call | solution.py:269
  243.2 0.8 copy-done.12
  244.2 0.4 copy.65
  244.7 1.3 collective-permute-start.6
  246.0 0.8 collective-permute-start.7
  246.9 1.4 collective-permute-start.8
  248.3 35.6 %lag_products.5 = f32[16,32,256]{2,1,0:T(8,128)} custom-call(s32[1]{0:T(128)} %bitcast.11.place_ref, bf16[64,8,512]{2,1,0:T(8,128)(2,1)} %copy-done.3, bf16[64,8,512]{2,1,0:T(8,128)(2,1)} %copy-done.10, bf16[64,8,512]{2,1,0:T(8,128)(2,1)} %copy-done.11, bf16[64,8,512]{2,1,0:T(8,128)(2,1)} %copy-done.12, bf16[64,512,512]{2,1,0:T(8,128)(2,1)} %bitcast.53, ...), custom_call_target="tpu_custom_call" | custom-call | flops 17179869184 | bytes 35651584 | tf_op jit(solution)/shard_map/lag_products/pallas_call | solution.py:269
  283.9 0.4 copy.64
  284.5 1.3 collective-permute-start.9
  285.8 0.8 collective-permute-start.10
  286.7 1.4 collective-permute-start.11
  288.1 35.6 %lag_products.6 = f32[16,32,256]{2,1,0:T(8,128)} custom-call(s32[1]{0:T(128)} %bitcast.11.place_ref, bf16[64,8,512]{2,1,0:T(8,128)(2,1)} %copy-done.5, bf16[64,8,512]{2,1,0:T(8,128)(2,1)} %copy-done.13, bf16[64,8,512]{2,1,0:T(8,128)(2,1)} %copy-done.14, bf16[64,8,512]{2,1,0:T(8,128)(2,1)} %copy-done.15, bf16[64,512,512]{2,1,0:T(8,128)(2,1)} %bitcast.54, ...), custom_call_target="tpu_custom_call" | custom-call | flops 17179869184 | bytes 35651584 | tf_op jit(solution)/shard_map/lag_products/pallas_call | solution.py:269
  323.8 0.8 copy-done.16
  324.5 0.2 copy-done.17
  324.8 0.8 copy-done.18
  325.6 35.6 %lag_products.7 = f32[16,32,256]{2,1,0:T(8,128)} custom-call(s32[1]{0:T(128)} %bitcast.11.place_ref, bf16[64,8,512]{2,1,0:T(8,128)(2,1)} %copy-done.6, bf16[64,8,512]{2,1,0:T(8,128)(2,1)} %copy-done.16, bf16[64,8,512]{2,1,0:T(8,128)(2,1)} %copy-done.17, bf16[64,8,512]{2,1,0:T(8,128)(2,1)} %copy-done.18, bf16[64,512,512]{2,1,0:T(8,128)(2,1)} %bitcast.55, ...), custom_call_target="tpu_custom_call" | custom-call | flops 17179869184 | bytes 35651584 | tf_op jit(solution)/shard_map/lag_products/pallas_call | solution.py:269
  361.2 5.0 %all-to-all-start.7 = ((f32[8,2,32,256]{3,2,1,0:T(8,128)}), f32[8,2,32,256]{3,2,1,0:T(8,128)S(1)}, u32[]{:S(2)}, u32[]{:S(2)}) async-start(f32[8,2,32,256]{3,2,1,0:T(8,128)} %bitcast.67), calls=%async_computation.9 | async-start | bytes 1048576 | tf_op jit(solution)/shard_map/all_to_all | solution.py:402
  366.2 0.7 reduce-scatter.5.cloned.1.call-update
  366.9 16.0 %all-to-all-done.7 = f32[8,2,32,256]{3,2,1,0:T(8,128)S(1)} async-done(((f32[8,2,32,256]{3,2,1,0:T(8,128)}), f32[8,2,32,256]{3,2,1,0:T(8,128)S(1)}, u32[]{:S(2)}, u32[]{:S(2)}) %all-to-all-start.7) | async-done | bytes 524320 | tf_op jit(solution)/shard_map/all_to_all | solution.py:402
  382.9 3.5 all-to-all-start.6
  386.5 17.2 %all-to-all-done.6 = f32[8,2,32,256]{3,2,1,0:T(8,128)S(1)} async-done(((f32[8,2,32,256]{3,2,1,0:T(8,128)}), f32[8,2,32,256]{3,2,1,0:T(8,128)S(1)}, u32[]{:S(2)}, u32[]{:S(2)}) %all-to-all-start.6) | async-done | bytes 524320 | tf_op jit(solution)/shard_map/all_to_all | solution.py:402
  403.8 1.6 pad_maximum_fusion
  (69 shorter events, 1.7 us)
Async XLA Ops:
  16.0 8.4 %copy-start.8 = (s32[256]{0:T(256)S(1)}, s32[256]{0:T(256)}, u32[]{:S(2)}) copy-start(s32[256]{0:T(256)} %param.20) | copy-start | bytes 3076
  17.3 41.3 %all-to-all-start = ((f16[8,8,64,128]{3,2,1,0:T(8,128)(2,1)}), f16[8,8,64,128]{3,2,1,0:T(8,128)(2,1)S(1)}, u32[]{:S(2)}, u32[]{:S(2)}) async-start(f16[8,8,64,128]{3,2,1,0:T(8,128)(2,1)} %bitcast.47), calls=%async_computation | async-start | bytes 2097152 | tf_op jit(solution)/shard_map/all_to_all | solution.py:402
  23.7 49.3 %all-gather.2.cloned.1.call-start = ((), (), s32[]{:S(2)}) async-start(), calls=%async_computation.10 | async-start | bytes 1179648 | tf_op jit(solution)/shard_map/all_gather | solution.py:463
  41.6 17.3 %copy-start = (bf16[512,512]{1,0:T(8,128)(2,1)S(1)}, bf16[512,512]{1,0:T(8,128)(2,1)}, u32[]{:S(2)}) copy-start(bf16[512,512]{1,0:T(8,128)(2,1)} %constant.92.clone.high_ref) | copy-start | bytes 1572868
  41.6 17.3 %copy-start.1 = (bf16[512,512]{1,0:T(8,128)(2,1)S(1)}, bf16[512,512]{1,0:T(8,128)(2,1)}, u32[]{:S(2)}) copy-start(bf16[512,512]{1,0:T(8,128)(2,1)} %constant.93.clone.low_ref) | copy-start | bytes 1572868
  62.8 31.5 %all-to-all-start.1 = ((f16[8,1,512,128]{3,2,1,0:T(8,128)(2,1)}), f16[8,1,512,128]{3,2,1,0:T(8,128)(2,1)S(1)}, u32[]{:S(2)}, u32[]{:S(2)}) async-start(f16[8,1,512,128]{3,2,1,0:T(8,128)(2,1)} %fusion.6), calls=%async_computation.1 | async-start | bytes 2097152 | tf_op jit(solution)/shard_map/all_to_all | solution.py:402
  66.4 3.5 copy-start.9
  74.2 18.2 %copy-start.2 = (f32[512,512]{0,1:T(8,128)S(1)}, f32[512,512]{0,1:T(8,128)}, u32[]{:S(2)}) copy-start(f32[512,512]{0,1:T(8,128)} %all-gather.2.cloned.1.call-done) | copy-start | bytes 3145732
  74.3 18.2 %copy-start.7 = (f32[256,256]{1,0:T(8,128)S(1)}, f32[256,256]{1,0:T(8,128)}, u32[]{:S(2)}) copy-start(f32[256,256]{1,0:T(8,128)} %constant.91.clone) | copy-start | bytes 786436
  94.3 31.6 %all-to-all-start.2 = ((f16[8,8,64,128]{3,2,1,0:T(8,128)(2,1)}), f16[8,8,64,128]{3,2,1,0:T(8,128)(2,1)S(1)}, u32[]{:S(2)}, u32[]{:S(2)}) async-start(f16[8,8,64,128]{3,2,1,0:T(8,128)(2,1)} %bitcast.56), calls=%async_computation.2 | async-start | bytes 2097152 | tf_op jit(solution)/shard_map/all_to_all | solution.py:402
  125.9 30.1 %all-to-all-start.3 = ((bf16[8,1,2,64,512]{4,3,2,1,0:T(8,128)(2,1)}), bf16[8,1,2,64,512]{4,3,2,1,0:T(8,128)(2,1)S(1)}, u32[]{:S(2)}, u32[]{:S(2)}) async-start(bf16[8,1,2,64,512]{4,3,2,1,0:T(8,128)(2,1)} %second_section.2), calls=%async_computation.3 | async-start | bytes 2097152 | tf_op jit(solution)/shard_map/all_to_all | solution.py:402
  156.0 31.1 %all-to-all-start.4 = ((f16[8,1,512,128]{3,2,1,0:T(8,128)(2,1)}), f16[8,1,512,128]{3,2,1,0:T(8,128)(2,1)S(1)}, u32[]{:S(2)}, u32[]{:S(2)}) async-start(f16[8,1,512,128]{3,2,1,0:T(8,128)(2,1)} %bitcast.5), calls=%async_computation.4 | async-start | bytes 2097152 | tf_op jit(solution)/shard_map/all_to_all | solution.py:402
  160.2 28.4 %copy-start.4 = (bf16[64,8,512]{2,1,0:T(8,128)(2,1)}, bf16[64,8,512]{2,1,0:T(8,128)(2,1)S(1)}, u32[]{:S(2)}) copy-start(bf16[64,8,512]{2,1,0:T(8,128)(2,1)S(1)} %reshape.168.a_ref) | copy-start | bytes 1572868
  160.2 14.9 %collective-permute-start = (bf16[64,8,512]{2,1,0:T(8,128)(2,1)S(1)}, bf16[64,8,512]{2,1,0:T(8,128)(2,1)}, u32[]{:S(2)}, u32[]{:S(2)}) collective-permute-start(bf16[64,8,512]{2,1,0:T(8,128)(2,1)S(1)} %reshape.168.a_ref), channel_id=1, source_target_pairs={{0,8},{8,0},{16,24},{24,16},{1,9},{9,1},{17,25},{25,17},{2,10},{10... | collective-permute-start | bytes 1572872 | tf_op jit(solution)/shard_map/ppermute | solution.py:302
  161.8 25.3 %collective-permute-start.1 = (bf16[64,8,512]{2,1,0:T(8,128)(2,1)S(1)}, bf16[64,8,512]{2,1,0:T(8,128)(2,1)}, u32[]{:S(2)}, u32[]{:S(2)}) collective-permute-start(bf16[64,8,512]{2,1,0:T(8,128)(2,1)S(1)} %reshape.168.a_ref), channel_id=1, source_target_pairs={{0,16},{8,24},{16,0},{24,8},{1,17},{9,25},{17,1},{25,9},{2,18},{10... | collective-permute-start | bytes 1572872 | tf_op jit(solution)/shard_map/ppermute | solution.py:302
  163.3 23.8 %collective-permute-start.2 = (bf16[64,8,512]{2,1,0:T(8,128)(2,1)S(1)}, bf16[64,8,512]{2,1,0:T(8,128)(2,1)}, u32[]{:S(2)}, u32[]{:S(2)}) collective-permute-start(bf16[64,8,512]{2,1,0:T(8,128)(2,1)S(1)} %reshape.168.a_ref), channel_id=1, source_target_pairs={{0,24},{8,16},{16,8},{24,0},{1,25},{9,17},{17,9},{25,1},{2,26},{10... | collective-permute-start | bytes 1572872 | tf_op jit(solution)/shard_map/ppermute | solution.py:302
  164.3 41.8 %copy-start.3 = (bf16[64,8,512]{2,1,0:T(8,128)(2,1)}, bf16[64,8,512]{2,1,0:T(8,128)(2,1)S(1)}, u32[]{:S(2)}) copy-start(bf16[64,8,512]{2,1,0:T(8,128)(2,1)S(1)} %reshape.169.a_ref) | copy-start | bytes 1572868
  199.1 44.1 %all-to-all-start.5 = ((bf16[8,1,2,64,512]{4,3,2,1,0:T(8,128)(2,1)}), bf16[8,1,2,64,512]{4,3,2,1,0:T(8,128)(2,1)S(1)}, u32[]{:S(2)}, u32[]{:S(2)}) async-start(bf16[8,1,2,64,512]{4,3,2,1,0:T(8,128)(2,1)} %second_section.3), calls=%async_computation.5 | async-start | bytes 2097152 | tf_op jit(solution)/shard_map/all_to_all | solution.py:402
  203.9 199.9 %reduce-scatter.3.cloned.1.call-start = ((), (), s32[]{:S(2)}) async-start(), calls=%async_computation.11 | async-start | bytes 589824 | tf_op jit(solution)/shard_map/reduce_scatter | solution.py:503
  203.9 39.2 %collective-permute-start.3 = (bf16[64,8,512]{2,1,0:T(8,128)(2,1)S(1)}, bf16[64,8,512]{2,1,0:T(8,128)(2,1)S(1)}, u32[]{:S(2)}, u32[]{:S(2)}) collective-permute-start(bf16[64,8,512]{2,1,0:T(8,128)(2,1)S(1)} %reshape.169.a_ref), channel_id=1, source_target_pairs={{0,8},{8,0},{16,24},{24,16},{1,9},{9,1},{17,25},{25,17},{2,10},{10... | collective-permute-start | bytes 1572872 | tf_op jit(solution)/shard_map/ppermute | solution.py:302
  205.3 37.9 %collective-permute-start.4 = (bf16[64,8,512]{2,1,0:T(8,128)(2,1)S(1)}, bf16[64,8,512]{2,1,0:T(8,128)(2,1)S(1)}, u32[]{:S(2)}, u32[]{:S(2)}) collective-permute-start(bf16[64,8,512]{2,1,0:T(8,128)(2,1)S(1)} %reshape.169.a_ref), channel_id=1, source_target_pairs={{0,16},{8,24},{16,0},{24,8},{1,17},{9,25},{17,1},{25,9},{2,18},{10... | collective-permute-start | bytes 1572872 | tf_op jit(solution)/shard_map/ppermute | solution.py:302
  206.1 37.1 %collective-permute-start.5 = (bf16[64,8,512]{2,1,0:T(8,128)(2,1)S(1)}, bf16[64,8,512]{2,1,0:T(8,128)(2,1)S(1)}, u32[]{:S(2)}, u32[]{:S(2)}) collective-permute-start(bf16[64,8,512]{2,1,0:T(8,128)(2,1)S(1)} %reshape.169.a_ref), channel_id=1, source_target_pairs={{0,24},{8,16},{16,8},{24,0},{1,25},{9,17},{17,9},{25,1},{2,26},{10... | collective-permute-start | bytes 1572872 | tf_op jit(solution)/shard_map/ppermute | solution.py:302
  243.2 1.5 copy-start.10
  243.2 1.5 copy-start.11
  243.2 0.9 copy-start.12
  244.7 39.2 %copy-start.5 = (bf16[64,8,512]{2,1,0:T(8,128)(2,1)}, bf16[64,8,512]{2,1,0:T(8,128)(2,1)S(1)}, u32[]{:S(2)}) copy-start(bf16[64,8,512]{2,1,0:T(8,128)(2,1)S(1)} %reshape.173.a_ref) | copy-start | bytes 1572868
  244.7 39.8 %collective-permute-start.6 = (bf16[64,8,512]{2,1,0:T(8,128)(2,1)S(1)}, bf16[64,8,512]{2,1,0:T(8,128)(2,1)S(1)}, u32[]{:S(2)}, u32[]{:S(2)}) collective-permute-start(bf16[64,8,512]{2,1,0:T(8,128)(2,1)S(1)} %reshape.173.a_ref), channel_id=1, source_target_pairs={{0,8},{8,0},{16,24},{24,16},{1,9},{9,1},{17,25},{25,17},{2,10},{10... | collective-permute-start | bytes 1572872 | tf_op jit(solution)/shard_map/ppermute | solution.py:302
  246.0 38.5 %collective-permute-start.7 = (bf16[64,8,512]{2,1,0:T(8,128)(2,1)S(1)}, bf16[64,8,512]{2,1,0:T(8,128)(2,1)S(1)}, u32[]{:S(2)}, u32[]{:S(2)}) collective-permute-start(bf16[64,8,512]{2,1,0:T(8,128)(2,1)S(1)} %reshape.173.a_ref), channel_id=1, source_target_pairs={{0,16},{8,24},{16,0},{24,8},{1,17},{9,25},{17,1},{25,9},{2,18},{10... | collective-permute-start | bytes 1572872 | tf_op jit(solution)/shard_map/ppermute | solution.py:302
  246.9 37.7 %collective-permute-start.8 = (bf16[64,8,512]{2,1,0:T(8,128)(2,1)S(1)}, bf16[64,8,512]{2,1,0:T(8,128)(2,1)S(1)}, u32[]{:S(2)}, u32[]{:S(2)}) collective-permute-start(bf16[64,8,512]{2,1,0:T(8,128)(2,1)S(1)} %reshape.173.a_ref), channel_id=1, source_target_pairs={{0,24},{8,16},{16,8},{24,0},{1,25},{9,17},{17,9},{25,1},{2,26},{10... | collective-permute-start | bytes 1572872 | tf_op jit(solution)/shard_map/ppermute | solution.py:302
  284.5 39.3 %copy-start.6 = (bf16[64,8,512]{2,1,0:T(8,128)(2,1)}, bf16[64,8,512]{2,1,0:T(8,128)(2,1)S(1)}, u32[]{:S(2)}) copy-start(bf16[64,8,512]{2,1,0:T(8,128)(2,1)S(1)} %reshape.174.a_ref) | copy-start | bytes 1572868
  284.5 3.6 copy-start.13
  284.5 3.6 copy-start.14
  284.5 3.6 copy-start.15
  284.5 39.2 %collective-permute-start.9 = (bf16[64,8,512]{2,1,0:T(8,128)(2,1)S(1)}, bf16[64,8,512]{2,1,0:T(8,128)(2,1)S(1)}, u32[]{:S(2)}, u32[]{:S(2)}) collective-permute-start(bf16[64,8,512]{2,1,0:T(8,128)(2,1)S(1)} %reshape.174.a_ref), channel_id=1, source_target_pairs={{0,8},{8,0},{16,24},{24,16},{1,9},{9,1},{17,25},{25,17},{2,10},{10... | collective-permute-start | bytes 1572872 | tf_op jit(solution)/shard_map/ppermute | solution.py:302
  285.8 37.9 %collective-permute-start.10 = (bf16[64,8,512]{2,1,0:T(8,128)(2,1)S(1)}, bf16[64,8,512]{2,1,0:T(8,128)(2,1)S(1)}, u32[]{:S(2)}, u32[]{:S(2)}) collective-permute-start(bf16[64,8,512]{2,1,0:T(8,128)(2,1)S(1)} %reshape.174.a_ref), channel_id=1, source_target_pairs={{0,16},{8,24},{16,0},{24,8},{1,17},{9,25},{17,1},{25,9},{2,18},{10... | collective-permute-start | bytes 1572872 | tf_op jit(solution)/shard_map/ppermute | solution.py:302
  286.7 37.1 %collective-permute-start.11 = (bf16[64,8,512]{2,1,0:T(8,128)(2,1)S(1)}, bf16[64,8,512]{2,1,0:T(8,128)(2,1)S(1)}, u32[]{:S(2)}, u32[]{:S(2)}) collective-permute-start(bf16[64,8,512]{2,1,0:T(8,128)(2,1)S(1)} %reshape.174.a_ref), channel_id=1, source_target_pairs={{0,24},{8,16},{16,8},{24,0},{1,25},{9,17},{17,9},{25,1},{2,26},{10... | collective-permute-start | bytes 1572872 | tf_op jit(solution)/shard_map/ppermute | solution.py:302
  323.7 0.8 copy-start.16
  323.8 1.0 copy-start.17
  324.8 0.8 copy-start.18
  361.2 21.7 %all-to-all-start.7 = ((f32[8,2,32,256]{3,2,1,0:T(8,128)}), f32[8,2,32,256]{3,2,1,0:T(8,128)S(1)}, u32[]{:S(2)}, u32[]{:S(2)}) async-start(f32[8,2,32,256]{3,2,1,0:T(8,128)} %bitcast.67), calls=%async_computation.9 | async-start | bytes 1048576 | tf_op jit(solution)/shard_map/all_to_all | solution.py:402
  366.2 37.6 %reduce-scatter.5.cloned.1.call-start = ((), (), s32[]{:S(2)}) async-start(), calls=%async_computation.12 | async-start | bytes 589824 | tf_op jit(solution)/shard_map/reduce_scatter | solution.py:503
  382.9 20.8 %all-to-all-start.6 = ((f32[8,2,32,256]{3,2,1,0:T(8,128)}), f32[8,2,32,256]{3,2,1,0:T(8,128)S(1)}, u32[]{:S(2)}, u32[]{:S(2)}) async-start(f32[8,2,32,256]{3,2,1,0:T(8,128)} %bitcast.18), calls=%async_computation.8 | async-start | bytes 1048576 | tf_op jit(solution)/shard_map/all_to_all | solution.py:402
Sparse Core Ops, SparseCore 0:
  26.1 33.3 all-gather.1
  248.4 31.3 reduce-scatter.2
  369.3 32.5 reduce-scatter.4

commit v7 on v6

--- a/solution.py
+++ b/solution.py
@@ -193,27 +193,27 @@
     sources = (a_ref, b_ref, x_ref, y_ref)
     segs = a_ref.shape[1] // 2
     per_quad = t_ref.shape[0]
-    lag_total = c_ref.shape[1]
+    lag_total = c_ref.shape[2]
     tmpl = out_ref.shape[2]
     step = pl.program_id(0)
     last = pl.num_programs(0) - 1
-    half = len(sources) * segs * lag_total
+    seg_total = len(sources) * segs
+    half = seg_total * lag_total
 
     def make_rows(rows_ref, jj):
         for chunk in range(A // 128):
             lanes = slice(chunk * 128, (chunk + 1) * 128)
-            lag_cos = c_ref[jj, :, lanes]
-            lag_sin = s_ref[jj, :, lanes]
-            for index, source in enumerate(sources):
-                value = source[jj, :, lanes].astype(jnp.float32)
-                for s in range(segs):
-                    real = value[s : s + 1]
-                    imag = value[segs + s : segs + s + 1]
-                    first_row = (index * segs + s) * lag_total
-                    rows = slice(first_row, first_row + lag_total)
-                    rows_ref[jj, rows, lanes] = (real * lag_cos - imag * lag_sin).astype(jnp.bfloat16)
-                    rows = slice(half + first_row, half + first_row + lag_total)
-                    rows_ref[jj, rows, lanes] = (real * lag_sin + imag * lag_cos).astype(jnp.bfloat16)
+            values = [source[jj, :, lanes].astype(jnp.float32) for source in sources]
+            real = jnp.concatenate([value[:segs] for value in values], axis=0)
+            imag = jnp.concatenate([value[segs:] for value in values], axis=0)
+            for lag in range(lag_total):
+                repeated = pl.ds(lag, 8, stride=0)
+                lag_cos = jnp.concatenate([c_ref[jj, chunk, repeated]] * (seg_total // 8), axis=0)
+                lag_sin = jnp.concatenate([s_ref[jj, chunk, repeated]] * (seg_total // 8), axis=0)
+                rows = slice(lag * seg_total, (lag + 1) * seg_total)
+                rows_ref[jj, rows, lanes] = (real * lag_cos - imag * lag_sin).astype(jnp.bfloat16)
+                rows = slice(half + lag * seg_total, half + (lag + 1) * seg_total)
+                rows_ref[jj, rows, lanes] = (real * lag_sin + imag * lag_cos).astype(jnp.bfloat16)
 
     def multiply(now_ref, jj):
         acc_ref[...] += dot_nt(now_ref[jj], t_ref[jj])
@@ -246,13 +246,16 @@
         def _(jj):
             multiply(odd_ref, jj)
 
-        shape = (segs, lag_total, tmpl)
+        shape = (lag_total, seg_total, tmpl)
+        real = acc_ref[:half, :tmpl] + acc_ref[half:, tmpl:]
+        imag = acc_ref[half:, :tmpl] - acc_ref[:half, tmpl:]
+        real = jnp.swapaxes(real.reshape(shape), 0, 1)
+        imag = jnp.swapaxes(imag.reshape(shape), 0, 1)
         for index in range(len(sources)):
-            low = slice(index * segs * lag_total, (index + 1) * segs * lag_total)
-            high = slice(half + low.start, half + low.stop)
+            here = slice(index * segs, (index + 1) * segs)
             place = pl.ds((place_ref[0] ^ index) * segs, segs)
-            out_ref[place, :lag_total] = (acc_ref[low, :tmpl] + acc_ref[high, tmpl:]).reshape(shape)
-            out_ref[place, lag_total:] = (acc_ref[high, :tmpl] - acc_ref[low, tmpl:]).reshape(shape)
+            out_ref[place, :lag_total] = real[here]
+            out_ref[place, lag_total:] = imag[here]
 
 
 def lag_products(sources, place, laid, lag_cos, lag_sin):
@@ -260,11 +263,14 @@
     tmpl2 = laid.shape[1]
     per_quad = min(4, blocks)
     quads = blocks // per_quad
-    lag_total = lag_cos.shape[1]
+    _, chunks, lag_total, lanes = lag_cos.shape
     segs = len(sources) * rows // 2
 
     def ahead(i):
         return (jnp.minimum(i, quads - 1), 0, 0)
+
+    def ahead_lags(i):
+        return (jnp.minimum(i, quads - 1), 0, 0, 0)
 
     return pl.pallas_call(
         lag_kernel,
@@ -273,8 +279,8 @@
         + [pl.BlockSpec((per_quad, rows, A), ahead)] * len(sources)
         + [
             pl.BlockSpec((per_quad, tmpl2, A), lambda i: (jnp.maximum(i - 1, 0), 0, 0)),
-            pl.BlockSpec((per_quad, lag_total, A), ahead),
-            pl.BlockSpec((per_quad, lag_total, A), ahead),
+            pl.BlockSpec((per_quad, chunks, lag_total, lanes), ahead_lags),
+            pl.BlockSpec((per_quad, chunks, lag_total, lanes), ahead_lags),
         ],
         out_specs=pl.BlockSpec((segs, 2 * lag_total, tmpl2 // 2), lambda i: (0, 0, 0)),
         out_shape=jax.ShapeDtypeStruct((segs, 2 * lag_total, tmpl2 // 2), jnp.float32),
@@ -432,12 +438,13 @@
     tied = lax.optimization_barrier
 
     block_cos, block_sin = cos_sin_table(block_ids, lags % B, B)
-    place = lags[:, None] * jnp.arange(A, dtype=jnp.int32)[None, :] % LEN
+    position = jnp.arange(A, dtype=jnp.int32).reshape(A // 128, 1, 128)
+    place = lags[None, :, None] * position % LEN
     place_angle = place.astype(jnp.float32) * (two_pi / LEN)
     place_cos = jnp.cos(place_angle)[None]
     place_sin = jnp.sin(place_angle)[None]
-    block_cos = block_cos[:, :, None]
-    block_sin = block_sin[:, :, None]
+    block_cos = block_cos[:, None, :, None]
+    block_sin = block_sin[:, None, :, None]
     lag_cos = block_cos * place_cos - block_sin * place_sin
     lag_sin = block_sin * place_cos + block_cos * place_sin
 
@@ -523,7 +530,9 @@
     sums_b1 = products(first_b)
     second_b, sums_b1 = tied((second_b, sums_b1))
     out_b1 = collect_late(sums_b1)
-    out_b2 = collect_late(products(second_b))
+    sums_b2 = products(second_b)
+    out_a1, out_a2, out_b1, sums_b2 = tied((out_a1, out_a2, out_b1, sums_b2))
+    out_b2 = collect_late(sums_b2)
     return jnp.concatenate([out_a1, out_a2, out_b1, out_b2], axis=0)
 
 

time: 413 us -> 401 us (0.971)
  waiting for transfers between devices: 112 us -> 77.5 us
  blocking collectives: 0 us -> 20.5 us
  Pallas kernels: 203 us -> 209 us
    all_to_all x8 -> x7, waiting for transfers between devices: 87.3 us -> 54 us  [exchange(): return lax.all_to_all(sent, 'freq', split_axis=0, concat_axis=0, tiled=True)]
    all_to_all x0 -> x1, blocking collectives: none -> 20.5 us  [exchange(): return lax.all_to_all(sent, 'freq', split_axis=0, concat_axis=0, tiled=True)]
    pallas_call x4, Pallas kernels: 142 us -> 148 us  [lag_products(): pl.pallas_call(lag_kernel, grid=(quads + 1,), in_specs=[pl.BlockSpec(memo...]
    all_to_all x8 -> x7, starting transfers between devices: 35.2 us -> 31.7 us  [exchange(): return lax.all_to_all(sent, 'freq', split_axis=0, concat_axis=0, tiled=True)]
  transfers between devices with their start and end apart: 23 -> 22, of which waited for: 7 -> 5; matrix products, arithmetic and copies ran while one was open for 4% -> 4% of each run, Pallas kernels for 47% -> 50%
where the time goes in v7:
time: 401 us; the launch traced here: 400 us
  Pallas kernels  209 us (52%)
  waiting for transfers between devices  77.5 us (19%)
  starting transfers between devices  46.1 us (11%)
  blocking collectives  20.5 us (5%)
  other arithmetic  15.8 us (4%)
  local copies, waits for them, and re-layouts  15.5 us (4%)
  between operations  13.6 us (3%)
    pallas_call x4, Pallas kernels, lag_products(): pl.pallas_call(lag_kernel, grid=(quads + 1,), in_specs=[pl.BlockSpec(memo...  148 us
    all_to_all x7, waiting for transfers between devices, exchange(): return lax.all_to_all(sent, 'freq', split_axis=0, concat_axis=0, tiled=True)  54 us
    pallas_call x2, Pallas kernels, lay_out(): pl.pallas_call(layout_kernel, grid=(steps, tmpl // batch), in_specs=[pl.B...  34.6 us
    all_to_all x7, starting transfers between devices, exchange(): return lax.all_to_all(sent, 'freq', split_axis=0, concat_axis=0, tiled=True)  31.7 us
    ppermute x12, waiting for transfers between devices, spread(): lax.ppermute(data, 'tmpl', [(n, n ^ bit) for n in range(4)])  22.8 us
    pallas_call x2, Pallas kernels, second_section(): pl.pallas_call(second_kernel, grid=(segs,), in_specs=[pl.BlockSpec((parts...  21.1 us
    all_to_all x1, blocking collectives, exchange(): return lax.all_to_all(sent, 'freq', split_axis=0, concat_axis=0, tiled=True)  20.5 us
    ppermute x12, starting transfers between devices, spread(): lax.ppermute(data, 'tmpl', [(n, n ^ bit) for n in range(4)])  14.2 us
  transfers between devices with their start and end apart: 22, of which 5 were waited for; matrix products, arithmetic and copies ran while one was open for 4% of the time, Pallas kernels for 50%

profile of v7, /device:TPU:0, one launch (start us, length us, event | category | flops | bytes accessed | tf_op | source)
XLA Modules:
  0.0 399.6 jit_solution(6019192439671063911)
XLA Ops:
  6.5 4.2 %reshape.154 = f32[2,2,4,65536]{3,2,1,0:T(4,128)} reshape(f32[16,65536]{1,0:T(8,128)} %param.17) | data formatting | bytes 8388608 | tf_op jit(solution)/shard_map/reshape | solution.py:478
  10.7 4.1 %fusion.1 = (f16[2,1,4,65536]{3,2,0,1:T(4,128)(2,1)}, f16[2,1,4,65536]{3,2,0,1:T(4,128)(2,1)S(1)}) fusion(f32[2,2,4,65536]{3,2,1,0:T(4,128)} %reshape.154), kind=kLoop, calls=%fused_computation.2 | loop fusion | flops 2097152 | bytes 6291456 | tf_op jit(solution)/shard_map/convert_element_type | solution.py:413
  14.9 1.1 convert_element_type.53
  16.0 1.3 copy.63
  17.3 6.3 %all-to-all-start = ((f16[8,8,64,128]{3,2,1,0:T(8,128)(2,1)}), f16[8,8,64,128]{3,2,1,0:T(8,128)(2,1)S(1)}, u32[]{:S(2)}, u32[]{:S(2)}) async-start(f16[8,8,64,128]{3,2,1,0:T(8,128)(2,1)} %bitcast.47), calls=%async_computation | async-start | bytes 2097152 | tf_op jit(solution)/shard_map/all_to_all | solution.py:408
  23.7 0.7 all-gather.2.cloned.1.call-update
  24.4 17.2 %lay_out.2.refs_0_ = bf16[64,2,256,512]{3,2,1,0:T(8,128)(2,1)} custom-call(s32[257]{0:T(512)S(1)} %get-tuple-element.98.cut_ref, bf16[256,2,64,512]{3,2,1,0:T(8,128)(2,1)} %t_ref.3), custom_call_target="tpu_custom_call" | custom-call | bytes 67108864 | tf_op jit(solution)/shard_map/lay_out/pallas_call | solution.py:343
  41.7 17.0 %all-to-all-done = f16[8,8,64,128]{3,2,1,0:T(8,128)(2,1)S(1)} async-done(((f16[8,8,64,128]{3,2,1,0:T(8,128)(2,1)}), f16[8,8,64,128]{3,2,1,0:T(8,128)(2,1)S(1)}, u32[]{:S(2)}, u32[]{:S(2)}) %all-to-all-start) | async-done | bytes 1048608 | tf_op jit(solution)/shard_map/all_to_all | solution.py:408
  58.7 0.3 convert_multiply_fusion.3.x_ref
  59.0 2.6 first_section.2
  61.5 1.3 fusion.6
  62.8 3.6 all-to-all-start.1
  66.4 2.2 convert_element_type.57
  68.6 1.3 copy.62
  69.9 0.2 fusion.18
  70.1 0.2 fusion.16
  70.3 2.6 multiply_add_fusion
  73.0 1.1 slice.34
  74.0 0.2 copy.55
  74.3 17.4 %lay_out.3 = bf16[64,2,256,512]{3,2,1,0:T(8,128)(2,1)} custom-call(s32[257]{0:T(512)S(1)} %get-tuple-element.97.cut_ref, bf16[256,2,64,512]{3,2,1,0:T(8,128)(2,1)} %t_ref.3, bf16[64,2,256,512]{3,2,1,0:T(8,128)(2,1)} %lay_out.2.refs_0_), custom_call_target="tpu_custom_call", output_to_operand_aliasing={{}: (2, {})} | custom-call | bytes 67108864 | tf_op jit(solution)/shard_map/lay_out/pallas_call | solution.py:343
  91.6 0.9 multiply_rsqrt_fusion.wa_ref
  92.5 1.9 fusion.5.wm_ref
  94.3 5.0 %all-to-all-start.2 = ((f16[8,8,64,128]{3,2,1,0:T(8,128)(2,1)}), f16[8,8,64,128]{3,2,1,0:T(8,128)(2,1)S(1)}, u32[]{:S(2)}, u32[]{:S(2)}) async-start(f16[8,8,64,128]{3,2,1,0:T(8,128)(2,1)} %bitcast.56), calls=%async_computation.2 | async-start | bytes 2097152 | tf_op jit(solution)/shard_map/all_to_all | solution.py:408
  99.4 1.5 convert_multiply_fusion.2.y_ref
  100.9 10.6 %second_section.2 = bf16[8,1,2,64,512]{4,3,2,1,0:T(8,128)(2,1)} custom-call(f32[8,1,512,128]{3,2,1,0:T(8,128)} %convert_multiply_fusion.2.y_ref, f32[256,1024]{1,0:T(8,128)} %constant.98.clone.tc_ref, f32[256,1024]{1,0:T(8,128)} %constant.99.clone.ts_ref, f32[1,1024]{1,0:T(1,128)} %constant.100.clone.ec_ref, f32[1,1024]{1,0:T(1,128)} %constant.101.clone.es_ref, ...), custom_call_target="tpu_custom_call" | custom-call | flops 3321888768 | bytes 3145728 | tf_op jit(solution)/shard_map/second_section/pallas_call | solution.py:177
  111.5 14.5 %all-to-all-done.2 = f16[8,8,64,128]{3,2,1,0:T(8,128)(2,1)S(1)} async-done(((f16[8,8,64,128]{3,2,1,0:T(8,128)(2,1)}), f16[8,8,64,128]{3,2,1,0:T(8,128)(2,1)S(1)}, u32[]{:S(2)}, u32[]{:S(2)}) %all-to-all-start.2) | async-done | bytes 1048608 | tf_op jit(solution)/shard_map/all_to_all | solution.py:408
  126.0 3.6 all-to-all-start.3
  129.5 0.3 convert_multiply_fusion.1.x_ref
  129.8 2.6 first_section.3
  132.4 1.2 fusion.7
  133.6 22.4 %all-to-all-done.3 = bf16[8,1,2,64,512]{4,3,2,1,0:T(8,128)(2,1)S(1)} async-done(((bf16[8,1,2,64,512]{4,3,2,1,0:T(8,128)(2,1)}), bf16[8,1,2,64,512]{4,3,2,1,0:T(8,128)(2,1)S(1)}, u32[]{:S(2)}, u32[]{:S(2)}) %all-to-all-start.3) | async-done | bytes 1048608 | tf_op jit(solution)/shard_map/all_to_all | solution.py:408
  156.1 3.6 all-to-all-start.4
  159.7 0.4 copy.67
  160.1 0.1 reshape.161.a_ref
  160.3 1.6 collective-permute-start
  161.8 1.5 collective-permute-start.1
  163.4 0.5 collective-permute-start.2
  163.8 0.4 copy.66
  164.2 0.1 reshape.162.a_ref
  164.4 10.8 %collective-permute-done.b_ref = bf16[64,8,512]{2,1,0:T(8,128)(2,1)} collective-permute-done((bf16[64,8,512]{2,1,0:T(8,128)(2,1)S(1)}, bf16[64,8,512]{2,1,0:T(8,128)(2,1)}, u32[]{:S(2)}, u32[]{:S(2)}) %collective-permute-start) | collective-permute-done | bytes 524320 | tf_op jit(solution)/shard_map/ppermute | solution.py:308
  175.2 12.0 %collective-permute-done.1.x_ref = bf16[64,8,512]{2,1,0:T(8,128)(2,1)} collective-permute-done((bf16[64,8,512]{2,1,0:T(8,128)(2,1)S(1)}, bf16[64,8,512]{2,1,0:T(8,128)(2,1)}, u32[]{:S(2)}, u32[]{:S(2)}) %collective-permute-start.1) | collective-permute-done | bytes 524320 | tf_op jit(solution)/shard_map/ppermute | solution.py:308
  187.2 1.5 convert_multiply_fusion.y_ref
  188.7 10.5 %second_section.3 = bf16[8,1,2,64,512]{4,3,2,1,0:T(8,128)(2,1)} custom-call(f32[8,1,512,128]{3,2,1,0:T(8,128)} %convert_multiply_fusion.y_ref, f32[256,1024]{1,0:T(8,128)} %constant.98.clone.tc_ref, f32[256,1024]{1,0:T(8,128)} %constant.99.clone.ts_ref, f32[1,1024]{1,0:T(1,128)} %constant.100.clone.ec_ref, f32[1,1024]{1,0:T(1,128)} %constant.101.clone.es_ref, ...), custom_call_target="tpu_custom_call" | custom-call | flops 3321888768 | bytes 3145728 | tf_op jit(solution)/shard_map/second_section/pallas_call | solution.py:177
  199.2 4.7 %all-to-all-start.5 = ((bf16[8,1,2,64,512]{4,3,2,1,0:T(8,128)(2,1)}), bf16[8,1,2,64,512]{4,3,2,1,0:T(8,128)(2,1)S(1)}, u32[]{:S(2)}, u32[]{:S(2)}) async-start(bf16[8,1,2,64,512]{4,3,2,1,0:T(8,128)(2,1)} %second_section.3), calls=%async_computation.5 | async-start | bytes 2097152 | tf_op jit(solution)/shard_map/all_to_all | solution.py:408
  204.0 1.3 collective-permute-start.3
  205.3 0.8 collective-permute-start.4
  206.2 1.4 collective-permute-start.5
  207.6 37.0 %lag_products.4 = f32[16,32,256]{2,1,0:T(8,128)} custom-call(s32[1]{0:T(128)} %bitcast.11.place_ref, bf16[64,8,512]{2,1,0:T(8,128)(2,1)} %copy-done.4, bf16[64,8,512]{2,1,0:T(8,128)(2,1)} %collective-permute-done.b_ref, bf16[64,8,512]{2,1,0:T(8,128)(2,1)} %collective-permute-done.1.x_ref, bf16[64,8,512]{2,1,0:T(8,128)(2,1)} %collective-permute-done.2.y_ref, ...), custom_call_target="tpu_custom_call" | custom-call | flops 17179869184 | bytes 35651584 | tf_op jit(solution)/shard_map/lag_products/pallas_call | solution.py:275
  244.7 0.8 copy-done.14
  245.6 0.4 copy.65
  246.2 1.3 collective-permute-start.6
  247.5 0.8 collective-permute-start.7
  248.3 1.4 collective-permute-start.8
  249.8 37.0 %lag_products.5 = f32[16,32,256]{2,1,0:T(8,128)} custom-call(s32[1]{0:T(128)} %bitcast.11.place_ref, bf16[64,8,512]{2,1,0:T(8,128)(2,1)} %copy-done.3, bf16[64,8,512]{2,1,0:T(8,128)(2,1)} %copy-done.10, bf16[64,8,512]{2,1,0:T(8,128)(2,1)} %copy-done.12, bf16[64,8,512]{2,1,0:T(8,128)(2,1)} %copy-done.14, bf16[64,512,512]{2,1,0:T(8,128)(2,1)} %bitcast.53, ...), custom_call_target="tpu_custom_call" | custom-call | flops 17179869184 | bytes 35651584 | tf_op jit(solution)/shard_map/lag_products/pallas_call | solution.py:275
  286.8 0.4 copy.64
  287.4 1.3 collective-permute-start.9
  288.7 0.8 collective-permute-start.10
  289.5 1.4 collective-permute-start.11
  291.0 37.1 %lag_products.6 = f32[16,32,256]{2,1,0:T(8,128)} custom-call(s32[1]{0:T(128)} %bitcast.11.place_ref, bf16[64,8,512]{2,1,0:T(8,128)(2,1)} %copy-done.5, bf16[64,8,512]{2,1,0:T(8,128)(2,1)} %copy-done.11, bf16[64,8,512]{2,1,0:T(8,128)(2,1)} %copy-done.13, bf16[64,8,512]{2,1,0:T(8,128)(2,1)} %copy-done.15, bf16[64,512,512]{2,1,0:T(8,128)(2,1)} %bitcast.54, ...), custom_call_target="tpu_custom_call" | custom-call | flops 17179869184 | bytes 35651584 | tf_op jit(solution)/shard_map/lag_products/pallas_call | solution.py:275
  328.1 0.8 copy-done.17
  328.9 4.9 %all-to-all-start.6 = ((f32[8,2,32,256]{3,2,1,0:T(8,128)}), f32[8,2,32,256]{3,2,1,0:T(8,128)S(1)}, u32[]{:S(2)}, u32[]{:S(2)}) async-start(f32[8,2,32,256]{3,2,1,0:T(8,128)} %bitcast.67), calls=%async_computation.8 | async-start | bytes 1048576 | tf_op jit(solution)/shard_map/all_to_all | solution.py:408
  333.9 37.0 %lag_products.7 = f32[16,32,256]{2,1,0:T(8,128)} custom-call(s32[1]{0:T(128)} %bitcast.11.place_ref, bf16[64,8,512]{2,1,0:T(8,128)(2,1)} %copy-done.6, bf16[64,8,512]{2,1,0:T(8,128)(2,1)} %copy-done.16, bf16[64,8,512]{2,1,0:T(8,128)(2,1)} %copy-done.17, bf16[64,8,512]{2,1,0:T(8,128)(2,1)} %collective-permute-done.11.y_ref, bf16[64,512,512]{2,1,0:T(8,128)(2,1)} %bitcast.55, ...), custom_call_target="tpu_custom_call" | custom-call | flops 17179869184 | bytes 35651584 | tf_op jit(solution)/shard_map/lag_products/pallas_call | solution.py:275
  371.0 20.5 %all_to_all.40 = f32[8,2,32,256]{3,2,1,0:T(8,128)S(1)} all-to-all(f32[8,2,32,256]{3,2,1,0:T(8,128)} %bitcast.68), channel_id=1, replica_groups=mesh['tmpl'=4,'freq'=8] {'freq'}, dimensions={0} | all-to-all | bytes 1048576 | tf_op jit(solution)/shard_map/all_to_all | solution.py:408
  391.5 1.6 pad_maximum_fusion
  (67 shorter events, 0.8 us)
Async XLA Ops:
  16.0 8.4 %copy-start.8 = (s32[256]{0:T(256)S(1)}, s32[256]{0:T(256)}, u32[]{:S(2)}) copy-start(s32[256]{0:T(256)} %param.20) | copy-start | bytes 3076
  17.3 41.3 %all-to-all-start = ((f16[8,8,64,128]{3,2,1,0:T(8,128)(2,1)}), f16[8,8,64,128]{3,2,1,0:T(8,128)(2,1)S(1)}, u32[]{:S(2)}, u32[]{:S(2)}) async-start(f16[8,8,64,128]{3,2,1,0:T(8,128)(2,1)} %bitcast.47), calls=%async_computation | async-start | bytes 2097152 | tf_op jit(solution)/shard_map/all_to_all | solution.py:408
  23.6 49.3 %all-gather.2.cloned.1.call-start = ((), (), s32[]{:S(2)}) async-start(), calls=%async_computation.10 | async-start | bytes 1179648 | tf_op jit(solution)/shard_map/all_gather | solution.py:470
  41.7 17.3 %copy-start = (bf16[512,512]{1,0:T(8,128)(2,1)S(1)}, bf16[512,512]{1,0:T(8,128)(2,1)}, u32[]{:S(2)}) copy-start(bf16[512,512]{1,0:T(8,128)(2,1)} %constant.96.clone.high_ref) | copy-start | bytes 1572868
  41.7 17.3 %copy-start.1 = (bf16[512,512]{1,0:T(8,128)(2,1)S(1)}, bf16[512,512]{1,0:T(8,128)(2,1)}, u32[]{:S(2)}) copy-start(bf16[512,512]{1,0:T(8,128)(2,1)} %constant.97.clone.low_ref) | copy-start | bytes 1572868
  62.8 31.6 %all-to-all-start.1 = ((f16[8,1,512,128]{3,2,1,0:T(8,128)(2,1)}), f16[8,1,512,128]{3,2,1,0:T(8,128)(2,1)S(1)}, u32[]{:S(2)}, u32[]{:S(2)}) async-start(f16[8,1,512,128]{3,2,1,0:T(8,128)(2,1)} %fusion.6), calls=%async_computation.1 | async-start | bytes 2097152 | tf_op jit(solution)/shard_map/all_to_all | solution.py:408
  66.4 3.5 copy-start.9
  74.2 18.3 %copy-start.2 = (f32[512,512]{0,1:T(8,128)S(1)}, f32[512,512]{0,1:T(8,128)}, u32[]{:S(2)}) copy-start(f32[512,512]{0,1:T(8,128)} %all-gather.2.cloned.1.call-done) | copy-start | bytes 3145732
  74.2 18.2 %copy-start.7 = (f32[256,256]{1,0:T(8,128)S(1)}, f32[256,256]{1,0:T(8,128)}, u32[]{:S(2)}) copy-start(f32[256,256]{1,0:T(8,128)} %constant.95.clone) | copy-start | bytes 786436
  94.3 31.6 %all-to-all-start.2 = ((f16[8,8,64,128]{3,2,1,0:T(8,128)(2,1)}), f16[8,8,64,128]{3,2,1,0:T(8,128)(2,1)S(1)}, u32[]{:S(2)}, u32[]{:S(2)}) async-start(f16[8,8,64,128]{3,2,1,0:T(8,128)(2,1)} %bitcast.56), calls=%async_computation.2 | async-start | bytes 2097152 | tf_op jit(solution)/shard_map/all_to_all | solution.py:408
  126.0 30.1 %all-to-all-start.3 = ((bf16[8,1,2,64,512]{4,3,2,1,0:T(8,128)(2,1)}), bf16[8,1,2,64,512]{4,3,2,1,0:T(8,128)(2,1)S(1)}, u32[]{:S(2)}, u32[]{:S(2)}) async-start(bf16[8,1,2,64,512]{4,3,2,1,0:T(8,128)(2,1)} %second_section.2), calls=%async_computation.3 | async-start | bytes 2097152 | tf_op jit(solution)/shard_map/all_to_all | solution.py:408
  156.1 31.1 %all-to-all-start.4 = ((f16[8,1,512,128]{3,2,1,0:T(8,128)(2,1)}), f16[8,1,512,128]{3,2,1,0:T(8,128)(2,1)S(1)}, u32[]{:S(2)}, u32[]{:S(2)}) async-start(f16[8,1,512,128]{3,2,1,0:T(8,128)(2,1)} %bitcast.5), calls=%async_computation.4 | async-start | bytes 2097152 | tf_op jit(solution)/shard_map/all_to_all | solution.py:408
  160.3 28.4 %copy-start.4 = (bf16[64,8,512]{2,1,0:T(8,128)(2,1)}, bf16[64,8,512]{2,1,0:T(8,128)(2,1)S(1)}, u32[]{:S(2)}) copy-start(bf16[64,8,512]{2,1,0:T(8,128)(2,1)S(1)} %reshape.161.a_ref) | copy-start | bytes 1572868
  160.3 14.9 %collective-permute-start = (bf16[64,8,512]{2,1,0:T(8,128)(2,1)S(1)}, bf16[64,8,512]{2,1,0:T(8,128)(2,1)}, u32[]{:S(2)}, u32[]{:S(2)}) collective-permute-start(bf16[64,8,512]{2,1,0:T(8,128)(2,1)S(1)} %reshape.161.a_ref), channel_id=1, source_target_pairs={{0,8},{8,0},{16,24},{24,16},{1,9},{9,1},{17,25},{25,17},{2,10},{10... | collective-permute-start | bytes 1572872 | tf_op jit(solution)/shard_map/ppermute | solution.py:308
  161.8 25.3 %collective-permute-start.1 = (bf16[64,8,512]{2,1,0:T(8,128)(2,1)S(1)}, bf16[64,8,512]{2,1,0:T(8,128)(2,1)}, u32[]{:S(2)}, u32[]{:S(2)}) collective-permute-start(bf16[64,8,512]{2,1,0:T(8,128)(2,1)S(1)} %reshape.161.a_ref), channel_id=1, source_target_pairs={{0,16},{8,24},{16,0},{24,8},{1,17},{9,25},{17,1},{25,9},{2,18},{10... | collective-permute-start | bytes 1572872 | tf_op jit(solution)/shard_map/ppermute | solution.py:308
  163.4 23.8 %collective-permute-start.2 = (bf16[64,8,512]{2,1,0:T(8,128)(2,1)S(1)}, bf16[64,8,512]{2,1,0:T(8,128)(2,1)}, u32[]{:S(2)}, u32[]{:S(2)}) collective-permute-start(bf16[64,8,512]{2,1,0:T(8,128)(2,1)S(1)} %reshape.161.a_ref), channel_id=1, source_target_pairs={{0,24},{8,16},{16,8},{24,0},{1,25},{9,17},{17,9},{25,1},{2,26},{10... | collective-permute-start | bytes 1572872 | tf_op jit(solution)/shard_map/ppermute | solution.py:308
  164.4 41.8 %copy-start.3 = (bf16[64,8,512]{2,1,0:T(8,128)(2,1)}, bf16[64,8,512]{2,1,0:T(8,128)(2,1)S(1)}, u32[]{:S(2)}) copy-start(bf16[64,8,512]{2,1,0:T(8,128)(2,1)S(1)} %reshape.162.a_ref) | copy-start | bytes 1572868
  199.2 45.4 %all-to-all-start.5 = ((bf16[8,1,2,64,512]{4,3,2,1,0:T(8,128)(2,1)}), bf16[8,1,2,64,512]{4,3,2,1,0:T(8,128)(2,1)S(1)}, u32[]{:S(2)}, u32[]{:S(2)}) async-start(bf16[8,1,2,64,512]{4,3,2,1,0:T(8,128)(2,1)} %second_section.3), calls=%async_computation.5 | async-start | bytes 2097152 | tf_op jit(solution)/shard_map/all_to_all | solution.py:408
  204.0 167.0 %reduce-scatter.3.cloned.1.call-start = ((), (), s32[]{:S(2)}) async-start(), calls=%async_computation.11 | async-start | bytes 589824 | tf_op jit(solution)/shard_map/reduce_scatter | solution.py:510
  204.0 40.6 %collective-permute-start.3 = (bf16[64,8,512]{2,1,0:T(8,128)(2,1)S(1)}, bf16[64,8,512]{2,1,0:T(8,128)(2,1)S(1)}, u32[]{:S(2)}, u32[]{:S(2)}) collective-permute-start(bf16[64,8,512]{2,1,0:T(8,128)(2,1)S(1)} %reshape.162.a_ref), channel_id=1, source_target_pairs={{0,8},{8,0},{16,24},{24,16},{1,9},{9,1},{17,25},{25,17},{2,10},{10... | collective-permute-start | bytes 1572872 | tf_op jit(solution)/shard_map/ppermute | solution.py:308
  205.3 39.3 %collective-permute-start.4 = (bf16[64,8,512]{2,1,0:T(8,128)(2,1)S(1)}, bf16[64,8,512]{2,1,0:T(8,128)(2,1)S(1)}, u32[]{:S(2)}, u32[]{:S(2)}) collective-permute-start(bf16[64,8,512]{2,1,0:T(8,128)(2,1)S(1)} %reshape.162.a_ref), channel_id=1, source_target_pairs={{0,16},{8,24},{16,0},{24,8},{1,17},{9,25},{17,1},{25,9},{2,18},{10... | collective-permute-start | bytes 1572872 | tf_op jit(solution)/shard_map/ppermute | solution.py:308
  206.2 38.5 %collective-permute-start.5 = (bf16[64,8,512]{2,1,0:T(8,128)(2,1)S(1)}, bf16[64,8,512]{2,1,0:T(8,128)(2,1)S(1)}, u32[]{:S(2)}, u32[]{:S(2)}) collective-permute-start(bf16[64,8,512]{2,1,0:T(8,128)(2,1)S(1)} %reshape.162.a_ref), channel_id=1, source_target_pairs={{0,24},{8,16},{16,8},{24,0},{1,25},{9,17},{17,9},{25,1},{2,26},{10... | collective-permute-start | bytes 1572872 | tf_op jit(solution)/shard_map/ppermute | solution.py:308
  244.6 1.5 copy-start.10
  244.6 1.5 copy-start.12
  244.6 0.9 copy-start.14
  246.2 40.6 %copy-start.5 = (bf16[64,8,512]{2,1,0:T(8,128)(2,1)}, bf16[64,8,512]{2,1,0:T(8,128)(2,1)S(1)}, u32[]{:S(2)}) copy-start(bf16[64,8,512]{2,1,0:T(8,128)(2,1)S(1)} %reshape.166.a_ref) | copy-start | bytes 1572868
  246.2 41.2 %collective-permute-start.6 = (bf16[64,8,512]{2,1,0:T(8,128)(2,1)S(1)}, bf16[64,8,512]{2,1,0:T(8,128)(2,1)S(1)}, u32[]{:S(2)}, u32[]{:S(2)}) collective-permute-start(bf16[64,8,512]{2,1,0:T(8,128)(2,1)S(1)} %reshape.166.a_ref), channel_id=1, source_target_pairs={{0,8},{8,0},{16,24},{24,16},{1,9},{9,1},{17,25},{25,17},{2,10},{10... | collective-permute-start | bytes 1572872 | tf_op jit(solution)/shard_map/ppermute | solution.py:308
  247.5 39.9 %collective-permute-start.7 = (bf16[64,8,512]{2,1,0:T(8,128)(2,1)S(1)}, bf16[64,8,512]{2,1,0:T(8,128)(2,1)S(1)}, u32[]{:S(2)}, u32[]{:S(2)}) collective-permute-start(bf16[64,8,512]{2,1,0:T(8,128)(2,1)S(1)} %reshape.166.a_ref), channel_id=1, source_target_pairs={{0,16},{8,24},{16,0},{24,8},{1,17},{9,25},{17,1},{25,9},{2,18},{10... | collective-permute-start | bytes 1572872 | tf_op jit(solution)/shard_map/ppermute | solution.py:308
  248.3 39.1 %collective-permute-start.8 = (bf16[64,8,512]{2,1,0:T(8,128)(2,1)S(1)}, bf16[64,8,512]{2,1,0:T(8,128)(2,1)S(1)}, u32[]{:S(2)}, u32[]{:S(2)}) collective-permute-start(bf16[64,8,512]{2,1,0:T(8,128)(2,1)S(1)} %reshape.166.a_ref), channel_id=1, source_target_pairs={{0,24},{8,16},{16,8},{24,0},{1,25},{9,17},{17,9},{25,1},{2,26},{10... | collective-permute-start | bytes 1572872 | tf_op jit(solution)/shard_map/ppermute | solution.py:308
  249.8 121.2 %reduce-scatter.5.cloned.1.call-start = ((), (), s32[]{:S(2)}) async-start(), calls=%async_computation.12 | async-start | bytes 589824 | tf_op jit(solution)/shard_map/reduce_scatter | solution.py:510
  287.3 40.7 %copy-start.6 = (bf16[64,8,512]{2,1,0:T(8,128)(2,1)}, bf16[64,8,512]{2,1,0:T(8,128)(2,1)S(1)}, u32[]{:S(2)}) copy-start(bf16[64,8,512]{2,1,0:T(8,128)(2,1)S(1)} %reshape.167.a_ref) | copy-start | bytes 1572868
  287.4 3.6 copy-start.11
  287.4 3.6 copy-start.13
  287.4 3.6 copy-start.15
  287.4 40.7 %collective-permute-start.9 = (bf16[64,8,512]{2,1,0:T(8,128)(2,1)S(1)}, bf16[64,8,512]{2,1,0:T(8,128)(2,1)S(1)}, u32[]{:S(2)}, u32[]{:S(2)}) collective-permute-start(bf16[64,8,512]{2,1,0:T(8,128)(2,1)S(1)} %reshape.167.a_ref), channel_id=1, source_target_pairs={{0,8},{8,0},{16,24},{24,16},{1,9},{9,1},{17,25},{25,17},{2,10},{10... | collective-permute-start | bytes 1572872 | tf_op jit(solution)/shard_map/ppermute | solution.py:308
  288.7 39.4 %collective-permute-start.10 = (bf16[64,8,512]{2,1,0:T(8,128)(2,1)S(1)}, bf16[64,8,512]{2,1,0:T(8,128)(2,1)S(1)}, u32[]{:S(2)}, u32[]{:S(2)}) collective-permute-start(bf16[64,8,512]{2,1,0:T(8,128)(2,1)S(1)} %reshape.167.a_ref), channel_id=1, source_target_pairs={{0,16},{8,24},{16,0},{24,8},{1,17},{9,25},{17,1},{25,9},{2,18},{10... | collective-permute-start | bytes 1572872 | tf_op jit(solution)/shard_map/ppermute | solution.py:308
  289.5 38.6 %collective-permute-start.11 = (bf16[64,8,512]{2,1,0:T(8,128)(2,1)S(1)}, bf16[64,8,512]{2,1,0:T(8,128)(2,1)}, u32[]{:S(2)}, u32[]{:S(2)}) collective-permute-start(bf16[64,8,512]{2,1,0:T(8,128)(2,1)S(1)} %reshape.167.a_ref), channel_id=1, source_target_pairs={{0,24},{8,16},{16,8},{24,0},{1,25},{9,17},{17,9},{25,1},{2,26},{10... | collective-permute-start | bytes 1572872 | tf_op jit(solution)/shard_map/ppermute | solution.py:308
  328.1 5.8 %copy-start.16 = (bf16[64,8,512]{2,1,0:T(8,128)(2,1)}, bf16[64,8,512]{2,1,0:T(8,128)(2,1)S(1)}, u32[]{:S(2)}) copy-start(bf16[64,8,512]{2,1,0:T(8,128)(2,1)S(1)} %collective-permute-done.9.b_ref) | copy-start | bytes 1572868
  328.1 0.8 copy-start.17
  328.9 42.0 %all-to-all-start.6 = ((f32[8,2,32,256]{3,2,1,0:T(8,128)}), f32[8,2,32,256]{3,2,1,0:T(8,128)S(1)}, u32[]{:S(2)}, u32[]{:S(2)}) async-start(f32[8,2,32,256]{3,2,1,0:T(8,128)} %bitcast.67), calls=%async_computation.8 | async-start | bytes 1048576 | tf_op jit(solution)/shard_map/all_to_all | solution.py:408
Sparse Core Ops, SparseCore 0:
  26.1 33.3 all-gather.1
  249.9 31.2 reduce-scatter.2
  291.1 31.2 reduce-scatter.4

commit v8 on v7

--- a/solution.py
+++ b/solution.py
@@ -200,23 +200,46 @@
     seg_total = len(sources) * segs
     half = seg_total * lag_total
 
-    def make_rows(rows_ref, jj):
-        for chunk in range(A // 128):
-            lanes = slice(chunk * 128, (chunk + 1) * 128)
-            values = [source[jj, :, lanes].astype(jnp.float32) for source in sources]
-            real = jnp.concatenate([value[:segs] for value in values], axis=0)
-            imag = jnp.concatenate([value[segs:] for value in values], axis=0)
-            for lag in range(lag_total):
-                repeated = pl.ds(lag, 8, stride=0)
-                lag_cos = jnp.concatenate([c_ref[jj, chunk, repeated]] * (seg_total // 8), axis=0)
-                lag_sin = jnp.concatenate([s_ref[jj, chunk, repeated]] * (seg_total // 8), axis=0)
-                rows = slice(lag * seg_total, (lag + 1) * seg_total)
-                rows_ref[jj, rows, lanes] = (real * lag_cos - imag * lag_sin).astype(jnp.bfloat16)
-                rows = slice(half + lag * seg_total, half + (lag + 1) * seg_total)
-                rows_ref[jj, rows, lanes] = (real * lag_sin + imag * lag_cos).astype(jnp.bfloat16)
-
-    def multiply(now_ref, jj):
-        acc_ref[...] += dot_nt(now_ref[jj], t_ref[jj])
+    def make_rows(rows_ref, jj, chunk):
+        lanes = slice(chunk * 128, (chunk + 1) * 128)
+        values = [source[jj, :, lanes].astype(jnp.float32) for source in sources]
+        real = jnp.concatenate([value[:segs] for value in values], axis=0)
+        imag = jnp.concatenate([value[segs:] for value in values], axis=0)
+        for lag in range(lag_total):
+            repeated = pl.ds(lag, 8, stride=0)
+            lag_cos = jnp.concatenate([c_ref[jj, chunk, repeated]] * (seg_total // 8), axis=0)
+            lag_sin = jnp.concatenate([s_ref[jj, chunk, repeated]] * (seg_total // 8), axis=0)
+            rows = slice(lag * seg_total, (lag + 1) * seg_total)
+            rows_ref[jj, rows, lanes] = (real * lag_cos - imag * lag_sin).astype(jnp.bfloat16)
+            rows = slice(half + lag * seg_total, half + (lag + 1) * seg_total)
+            rows_ref[jj, rows, lanes] = (real * lag_sin + imag * lag_cos).astype(jnp.bfloat16)
+
+    def one_block(next_ref, now_ref, units, jj):
+        deep = 256
+        for k in range(A // deep):
+            inner = slice(k * deep, (k + 1) * deep)
+            if now_ref is not None:
+                for unit in range(2):
+                    columns = t_ref[jj, unit * tmpl : (unit + 1) * tmpl, inner]
+                    pltpu.matmul_push_rhs(columns, k % 2, unit, transpose=True)
+            if next_ref is not None:
+                for chunk in range(k * deep // 128, (k + 1) * deep // 128):
+                    make_rows(next_ref, jj, chunk)
+            if now_ref is not None:
+                for unit_ref in units:
+                    pltpu.matmul_acc_lhs(unit_ref, now_ref[jj, :, inner], load_staged_rhs=k % 2)
+
+    def one_group(next_ref, now_ref):
+        def scoped(*units):
+            @pl.loop(0, per_quad)
+            def _(jj):
+                one_block(next_ref, now_ref, units, jj)
+
+            for unit, unit_ref in enumerate(units):
+                acc_ref[unit] += pltpu.matmul_pop(unit_ref)
+
+        shape = acc_ref.shape[1:]
+        pl.run_scoped(scoped, pltpu.ACC(0)(shape, jnp.float32), pltpu.ACC(1)(shape, jnp.float32))
 
     @pl.when(step == 0)
     def _():
@@ -224,31 +247,24 @@
 
         @pl.loop(0, per_quad)
         def _(jj):
-            make_rows(even_ref, jj)
+            one_block(even_ref, None, (), jj)
 
     @pl.when((step % 2 == 1) & (step < last))
     def _():
-        @pl.loop(0, per_quad)
-        def _(jj):
-            make_rows(odd_ref, jj)
-            multiply(even_ref, jj)
+        one_group(odd_ref, even_ref)
 
     @pl.when((step % 2 == 0) & (step > 0) & (step < last))
     def _():
-        @pl.loop(0, per_quad)
-        def _(jj):
-            make_rows(even_ref, jj)
-            multiply(odd_ref, jj)
+        one_group(even_ref, odd_ref)
 
     @pl.when(step == last)
     def _():
-        @pl.loop(0, per_quad)
-        def _(jj):
-            multiply(odd_ref, jj)
-
+        one_group(None, odd_ref)
+        by_real = acc_ref[0]
+        by_imag = acc_ref[1]
         shape = (lag_total, seg_total, tmpl)
-        real = acc_ref[:half, :tmpl] + acc_ref[half:, tmpl:]
-        imag = acc_ref[half:, :tmpl] - acc_ref[:half, tmpl:]
+        real = by_real[:half] + by_imag[half:]
+        imag = by_real[half:] - by_imag[:half]
         real = jnp.swapaxes(real.reshape(shape), 0, 1)
         imag = jnp.swapaxes(imag.reshape(shape), 0, 1)
         for index in range(len(sources)):
@@ -285,7 +301,7 @@
         out_specs=pl.BlockSpec((segs, 2 * lag_total, tmpl2 // 2), lambda i: (0, 0, 0)),
         out_shape=jax.ShapeDtypeStruct((segs, 2 * lag_total, tmpl2 // 2), jnp.float32),
         scratch_shapes=[
-            pltpu.VMEM((2 * segs * lag_total, tmpl2), jnp.float32),
+            pltpu.VMEM((2, 2 * segs * lag_total, tmpl2 // 2), jnp.float32),
             pltpu.VMEM((per_quad, 2 * segs * lag_total, A), jnp.bfloat16),
             pltpu.VMEM((per_quad, 2 * segs * lag_total, A), jnp.bfloat16),
         ],

time: 401 us -> 379 us (0.945)
  Pallas kernels: 209 us -> 186 us
    pallas_call x4, Pallas kernels: 148 us -> 125 us  [lag_products(): pl.pallas_call(lag_kernel, grid=(quads + 1,), in_specs=[pl.BlockSpec(memo...]
  transfers between devices with their start and end apart: 22 -> 22, of which waited for: 5 -> 5; matrix products, arithmetic and copies ran while one was open for 4% -> 4% of each run, Pallas kernels for 50% -> 47%
where the time goes in v8:
time: 379 us; the launch traced here: 376 us
  Pallas kernels  186 us (49%)
  waiting for transfers between devices  77.5 us (20%)
  starting transfers between devices  46.1 us (12%)
  blocking collectives  20.5 us (5%)
  other arithmetic  15.8 us (4%)
  local copies, waits for them, and re-layouts  15.5 us (4%)
  between operations  13.6 us (4%)
    pallas_call x4, Pallas kernels, lag_products(): pl.pallas_call(lag_kernel, grid=(quads + 1,), in_specs=[pl.BlockSpec(memo...  125 us
    all_to_all x7, waiting for transfers between devices, exchange(): return lax.all_to_all(sent, 'freq', split_axis=0, concat_axis=0, tiled=True)  54 us
    pallas_call x2, Pallas kernels, lay_out(): pl.pallas_call(layout_kernel, grid=(steps, tmpl // batch), in_specs=[pl.B...  34.6 us
    all_to_all x7, starting transfers between devices, exchange(): return lax.all_to_all(sent, 'freq', split_axis=0, concat_axis=0, tiled=True)  31.7 us
    ppermute x12, waiting for transfers between devices, spread(): lax.ppermute(data, 'tmpl', [(n, n ^ bit) for n in range(4)])  22.8 us
    pallas_call x2, Pallas kernels, second_section(): pl.pallas_call(second_kernel, grid=(segs,), in_specs=[pl.BlockSpec((parts...  21.1 us
    all_to_all x1, blocking collectives, exchange(): return lax.all_to_all(sent, 'freq', split_axis=0, concat_axis=0, tiled=True)  20.5 us
    ppermute x12, starting transfers between devices, spread(): lax.ppermute(data, 'tmpl', [(n, n ^ bit) for n in range(4)])  14.2 us
  transfers between devices with their start and end apart: 22, of which 5 were waited for; matrix products, arithmetic and copies ran while one was open for 4% of the time, Pallas kernels for 47%

profile of v8, /device:TPU:0, one launch (start us, length us, event | category | flops | bytes accessed | tf_op | source)
XLA Modules:
  0.0 376.4 jit_solution(15639651969863712551)
XLA Ops:
  6.5 4.2 %reshape.154 = f32[2,2,4,65536]{3,2,1,0:T(4,128)} reshape(f32[16,65536]{1,0:T(8,128)} %param.17) | data formatting | bytes 8388608 | tf_op jit(solution)/shard_map/reshape | solution.py:494
  10.7 4.1 %fusion.1 = (f16[2,1,4,65536]{3,2,0,1:T(4,128)(2,1)}, f16[2,1,4,65536]{3,2,0,1:T(4,128)(2,1)S(1)}) fusion(f32[2,2,4,65536]{3,2,1,0:T(4,128)} %reshape.154), kind=kLoop, calls=%fused_computation.2 | loop fusion | flops 2097152 | bytes 6291456 | tf_op jit(solution)/shard_map/convert_element_type | solution.py:429
  14.9 1.1 convert_element_type.53
  16.0 1.3 copy.63
  17.3 6.3 %all-to-all-start = ((f16[8,8,64,128]{3,2,1,0:T(8,128)(2,1)}), f16[8,8,64,128]{3,2,1,0:T(8,128)(2,1)S(1)}, u32[]{:S(2)}, u32[]{:S(2)}) async-start(f16[8,8,64,128]{3,2,1,0:T(8,128)(2,1)} %bitcast.47), calls=%async_computation | async-start | bytes 2097152 | tf_op jit(solution)/shard_map/all_to_all | solution.py:424
  23.7 0.7 all-gather.2.cloned.1.call-update
  24.4 17.2 %lay_out.2.refs_0_ = bf16[64,2,256,512]{3,2,1,0:T(8,128)(2,1)} custom-call(s32[257]{0:T(512)S(1)} %get-tuple-element.98.cut_ref, bf16[256,2,64,512]{3,2,1,0:T(8,128)(2,1)} %t_ref.3), custom_call_target="tpu_custom_call" | custom-call | bytes 67108864 | tf_op jit(solution)/shard_map/lay_out/pallas_call | solution.py:359
  41.7 17.0 %all-to-all-done = f16[8,8,64,128]{3,2,1,0:T(8,128)(2,1)S(1)} async-done(((f16[8,8,64,128]{3,2,1,0:T(8,128)(2,1)}), f16[8,8,64,128]{3,2,1,0:T(8,128)(2,1)S(1)}, u32[]{:S(2)}, u32[]{:S(2)}) %all-to-all-start) | async-done | bytes 1048608 | tf_op jit(solution)/shard_map/all_to_all | solution.py:424
  58.7 0.3 convert_multiply_fusion.3.x_ref
  59.0 2.6 first_section.2
  61.5 1.3 fusion.6
  62.8 3.6 all-to-all-start.1
  66.4 2.2 convert_element_type.57
  68.6 1.3 copy.62
  69.9 0.2 fusion.18
  70.1 0.2 fusion.16
  70.3 2.6 multiply_add_fusion
  73.0 1.1 slice.34
  74.0 0.2 copy.55
  74.3 17.4 %lay_out.3 = bf16[64,2,256,512]{3,2,1,0:T(8,128)(2,1)} custom-call(s32[257]{0:T(512)S(1)} %get-tuple-element.97.cut_ref, bf16[256,2,64,512]{3,2,1,0:T(8,128)(2,1)} %t_ref.3, bf16[64,2,256,512]{3,2,1,0:T(8,128)(2,1)} %lay_out.2.refs_0_), custom_call_target="tpu_custom_call", output_to_operand_aliasing={{}: (2, {})} | custom-call | bytes 67108864 | tf_op jit(solution)/shard_map/lay_out/pallas_call | solution.py:359
  91.6 0.9 multiply_rsqrt_fusion.wa_ref
  92.5 1.9 fusion.5.wm_ref
  94.3 5.0 %all-to-all-start.2 = ((f16[8,8,64,128]{3,2,1,0:T(8,128)(2,1)}), f16[8,8,64,128]{3,2,1,0:T(8,128)(2,1)S(1)}, u32[]{:S(2)}, u32[]{:S(2)}) async-start(f16[8,8,64,128]{3,2,1,0:T(8,128)(2,1)} %bitcast.56), calls=%async_computation.2 | async-start | bytes 2097152 | tf_op jit(solution)/shard_map/all_to_all | solution.py:424
  99.4 1.5 convert_multiply_fusion.2.y_ref
  100.9 10.6 %second_section.2 = bf16[8,1,2,64,512]{4,3,2,1,0:T(8,128)(2,1)} custom-call(f32[8,1,512,128]{3,2,1,0:T(8,128)} %convert_multiply_fusion.2.y_ref, f32[256,1024]{1,0:T(8,128)} %constant.98.clone.tc_ref, f32[256,1024]{1,0:T(8,128)} %constant.99.clone.ts_ref, f32[1,1024]{1,0:T(1,128)} %constant.100.clone.ec_ref, f32[1,1024]{1,0:T(1,128)} %constant.101.clone.es_ref, ...), custom_call_target="tpu_custom_call" | custom-call | flops 3321888768 | bytes 3145728 | tf_op jit(solution)/shard_map/second_section/pallas_call | solution.py:177
  111.5 14.5 %all-to-all-done.2 = f16[8,8,64,128]{3,2,1,0:T(8,128)(2,1)S(1)} async-done(((f16[8,8,64,128]{3,2,1,0:T(8,128)(2,1)}), f16[8,8,64,128]{3,2,1,0:T(8,128)(2,1)S(1)}, u32[]{:S(2)}, u32[]{:S(2)}) %all-to-all-start.2) | async-done | bytes 1048608 | tf_op jit(solution)/shard_map/all_to_all | solution.py:424
  126.0 3.6 all-to-all-start.3
  129.5 0.3 convert_multiply_fusion.1.x_ref
  129.8 2.6 first_section.3
  132.4 1.2 fusion.7
  133.6 22.4 %all-to-all-done.3 = bf16[8,1,2,64,512]{4,3,2,1,0:T(8,128)(2,1)S(1)} async-done(((bf16[8,1,2,64,512]{4,3,2,1,0:T(8,128)(2,1)}), bf16[8,1,2,64,512]{4,3,2,1,0:T(8,128)(2,1)S(1)}, u32[]{:S(2)}, u32[]{:S(2)}) %all-to-all-start.3) | async-done | bytes 1048608 | tf_op jit(solution)/shard_map/all_to_all | solution.py:424
  156.1 3.6 all-to-all-start.4
  159.7 0.4 copy.67
  160.1 0.1 reshape.161.a_ref
  160.3 1.6 collective-permute-start
  161.8 1.5 collective-permute-start.1
  163.4 0.5 collective-permute-start.2
  163.8 0.4 copy.66
  164.2 0.1 reshape.162.a_ref
  164.4 10.8 %collective-permute-done.b_ref = bf16[64,8,512]{2,1,0:T(8,128)(2,1)} collective-permute-done((bf16[64,8,512]{2,1,0:T(8,128)(2,1)S(1)}, bf16[64,8,512]{2,1,0:T(8,128)(2,1)}, u32[]{:S(2)}, u32[]{:S(2)}) %collective-permute-start) | collective-permute-done | bytes 524320 | tf_op jit(solution)/shard_map/ppermute | solution.py:324
  175.2 12.0 %collective-permute-done.1.x_ref = bf16[64,8,512]{2,1,0:T(8,128)(2,1)} collective-permute-done((bf16[64,8,512]{2,1,0:T(8,128)(2,1)S(1)}, bf16[64,8,512]{2,1,0:T(8,128)(2,1)}, u32[]{:S(2)}, u32[]{:S(2)}) %collective-permute-start.1) | collective-permute-done | bytes 524320 | tf_op jit(solution)/shard_map/ppermute | solution.py:324
  187.2 1.5 convert_multiply_fusion.y_ref
  188.7 10.5 %second_section.3 = bf16[8,1,2,64,512]{4,3,2,1,0:T(8,128)(2,1)} custom-call(f32[8,1,512,128]{3,2,1,0:T(8,128)} %convert_multiply_fusion.y_ref, f32[256,1024]{1,0:T(8,128)} %constant.98.clone.tc_ref, f32[256,1024]{1,0:T(8,128)} %constant.99.clone.ts_ref, f32[1,1024]{1,0:T(1,128)} %constant.100.clone.ec_ref, f32[1,1024]{1,0:T(1,128)} %constant.101.clone.es_ref, ...), custom_call_target="tpu_custom_call" | custom-call | flops 3321888768 | bytes 3145728 | tf_op jit(solution)/shard_map/second_section/pallas_call | solution.py:177
  199.2 4.7 %all-to-all-start.5 = ((bf16[8,1,2,64,512]{4,3,2,1,0:T(8,128)(2,1)}), bf16[8,1,2,64,512]{4,3,2,1,0:T(8,128)(2,1)S(1)}, u32[]{:S(2)}, u32[]{:S(2)}) async-start(bf16[8,1,2,64,512]{4,3,2,1,0:T(8,128)(2,1)} %second_section.3), calls=%async_computation.5 | async-start | bytes 2097152 | tf_op jit(solution)/shard_map/all_to_all | solution.py:424
  204.0 1.3 collective-permute-start.3
  205.3 0.8 collective-permute-start.4
  206.2 1.4 collective-permute-start.5
  207.6 31.2 %lag_products.4 = f32[16,32,256]{2,1,0:T(8,128)} custom-call(s32[1]{0:T(128)} %bitcast.11.place_ref, bf16[64,8,512]{2,1,0:T(8,128)(2,1)} %copy-done.4, bf16[64,8,512]{2,1,0:T(8,128)(2,1)} %collective-permute-done.b_ref, bf16[64,8,512]{2,1,0:T(8,128)(2,1)} %collective-permute-done.1.x_ref, bf16[64,8,512]{2,1,0:T(8,128)(2,1)} %collective-permute-done.2.y_ref, ...), custom_call_target="tpu_custom_call" | custom-call | flops 17179869184 | bytes 35651584 | tf_op jit(solution)/shard_map/lag_products/pallas_call | solution.py:291
  238.9 0.8 copy-done.14
  239.8 0.4 copy.65
  240.4 1.2 collective-permute-start.6
  241.6 0.8 collective-permute-start.7
  242.4 1.6 collective-permute-start.8
  244.0 31.2 %lag_products.5 = f32[16,32,256]{2,1,0:T(8,128)} custom-call(s32[1]{0:T(128)} %bitcast.11.place_ref, bf16[64,8,512]{2,1,0:T(8,128)(2,1)} %copy-done.3, bf16[64,8,512]{2,1,0:T(8,128)(2,1)} %copy-done.10, bf16[64,8,512]{2,1,0:T(8,128)(2,1)} %copy-done.12, bf16[64,8,512]{2,1,0:T(8,128)(2,1)} %copy-done.14, bf16[64,512,512]{2,1,0:T(8,128)(2,1)} %bitcast.53, ...), custom_call_target="tpu_custom_call" | custom-call | flops 17179869184 | bytes 35651584 | tf_op jit(solution)/shard_map/lag_products/pallas_call | solution.py:291
  275.2 0.4 copy.64
  275.8 1.2 collective-permute-start.9
  277.0 0.7 collective-permute-start.10
  277.7 1.7 collective-permute-start.11
  279.4 31.2 %lag_products.6 = f32[16,32,256]{2,1,0:T(8,128)} custom-call(s32[1]{0:T(128)} %bitcast.11.place_ref, bf16[64,8,512]{2,1,0:T(8,128)(2,1)} %copy-done.5, bf16[64,8,512]{2,1,0:T(8,128)(2,1)} %copy-done.11, bf16[64,8,512]{2,1,0:T(8,128)(2,1)} %copy-done.13, bf16[64,8,512]{2,1,0:T(8,128)(2,1)} %copy-done.15, bf16[64,512,512]{2,1,0:T(8,128)(2,1)} %bitcast.54, ...), custom_call_target="tpu_custom_call" | custom-call | flops 17179869184 | bytes 35651584 | tf_op jit(solution)/shard_map/lag_products/pallas_call | solution.py:291
  310.6 0.8 copy-done.17
  311.5 5.0 %all-to-all-start.6 = ((f32[8,2,32,256]{3,2,1,0:T(8,128)}), f32[8,2,32,256]{3,2,1,0:T(8,128)S(1)}, u32[]{:S(2)}, u32[]{:S(2)}) async-start(f32[8,2,32,256]{3,2,1,0:T(8,128)} %bitcast.67), calls=%async_computation.8 | async-start | bytes 1048576 | tf_op jit(solution)/shard_map/all_to_all | solution.py:424
  316.4 31.2 %lag_products.7 = f32[16,32,256]{2,1,0:T(8,128)} custom-call(s32[1]{0:T(128)} %bitcast.11.place_ref, bf16[64,8,512]{2,1,0:T(8,128)(2,1)} %copy-done.6, bf16[64,8,512]{2,1,0:T(8,128)(2,1)} %copy-done.16, bf16[64,8,512]{2,1,0:T(8,128)(2,1)} %copy-done.17, bf16[64,8,512]{2,1,0:T(8,128)(2,1)} %collective-permute-done.11.y_ref, bf16[64,512,512]{2,1,0:T(8,128)(2,1)} %bitcast.55, ...), custom_call_target="tpu_custom_call" | custom-call | flops 17179869184 | bytes 35651584 | tf_op jit(solution)/shard_map/lag_products/pallas_call | solution.py:291
  347.8 20.5 %all_to_all.40 = f32[8,2,32,256]{3,2,1,0:T(8,128)S(1)} all-to-all(f32[8,2,32,256]{3,2,1,0:T(8,128)} %bitcast.68), channel_id=1, replica_groups=mesh['tmpl'=4,'freq'=8] {'freq'}, dimensions={0} | all-to-all | bytes 1048576 | tf_op jit(solution)/shard_map/all_to_all | solution.py:424
  368.3 1.6 pad_maximum_fusion
  (67 shorter events, 0.8 us)
Async XLA Ops:
  16.0 8.4 %copy-start.8 = (s32[256]{0:T(256)S(1)}, s32[256]{0:T(256)}, u32[]{:S(2)}) copy-start(s32[256]{0:T(256)} %param.20) | copy-start | bytes 3076
  17.3 41.3 %all-to-all-start = ((f16[8,8,64,128]{3,2,1,0:T(8,128)(2,1)}), f16[8,8,64,128]{3,2,1,0:T(8,128)(2,1)S(1)}, u32[]{:S(2)}, u32[]{:S(2)}) async-start(f16[8,8,64,128]{3,2,1,0:T(8,128)(2,1)} %bitcast.47), calls=%async_computation | async-start | bytes 2097152 | tf_op jit(solution)/shard_map/all_to_all | solution.py:424
  23.6 49.3 %all-gather.2.cloned.1.call-start = ((), (), s32[]{:S(2)}) async-start(), calls=%async_computation.10 | async-start | bytes 1179648 | tf_op jit(solution)/shard_map/all_gather | solution.py:486
  41.7 17.3 %copy-start = (bf16[512,512]{1,0:T(8,128)(2,1)S(1)}, bf16[512,512]{1,0:T(8,128)(2,1)}, u32[]{:S(2)}) copy-start(bf16[512,512]{1,0:T(8,128)(2,1)} %constant.96.clone.high_ref) | copy-start | bytes 1572868
  41.7 17.3 %copy-start.1 = (bf16[512,512]{1,0:T(8,128)(2,1)S(1)}, bf16[512,512]{1,0:T(8,128)(2,1)}, u32[]{:S(2)}) copy-start(bf16[512,512]{1,0:T(8,128)(2,1)} %constant.97.clone.low_ref) | copy-start | bytes 1572868
  62.8 31.6 %all-to-all-start.1 = ((f16[8,1,512,128]{3,2,1,0:T(8,128)(2,1)}), f16[8,1,512,128]{3,2,1,0:T(8,128)(2,1)S(1)}, u32[]{:S(2)}, u32[]{:S(2)}) async-start(f16[8,1,512,128]{3,2,1,0:T(8,128)(2,1)} %fusion.6), calls=%async_computation.1 | async-start | bytes 2097152 | tf_op jit(solution)/shard_map/all_to_all | solution.py:424
  66.4 3.5 copy-start.9
  74.2 18.3 %copy-start.2 = (f32[512,512]{0,1:T(8,128)S(1)}, f32[512,512]{0,1:T(8,128)}, u32[]{:S(2)}) copy-start(f32[512,512]{0,1:T(8,128)} %all-gather.2.cloned.1.call-done) | copy-start | bytes 3145732
  74.2 18.2 %copy-start.7 = (f32[256,256]{1,0:T(8,128)S(1)}, f32[256,256]{1,0:T(8,128)}, u32[]{:S(2)}) copy-start(f32[256,256]{1,0:T(8,128)} %constant.95.clone) | copy-start | bytes 786436
  94.3 31.6 %all-to-all-start.2 = ((f16[8,8,64,128]{3,2,1,0:T(8,128)(2,1)}), f16[8,8,64,128]{3,2,1,0:T(8,128)(2,1)S(1)}, u32[]{:S(2)}, u32[]{:S(2)}) async-start(f16[8,8,64,128]{3,2,1,0:T(8,128)(2,1)} %bitcast.56), calls=%async_computation.2 | async-start | bytes 2097152 | tf_op jit(solution)/shard_map/all_to_all | solution.py:424
  126.0 30.1 %all-to-all-start.3 = ((bf16[8,1,2,64,512]{4,3,2,1,0:T(8,128)(2,1)}), bf16[8,1,2,64,512]{4,3,2,1,0:T(8,128)(2,1)S(1)}, u32[]{:S(2)}, u32[]{:S(2)}) async-start(bf16[8,1,2,64,512]{4,3,2,1,0:T(8,128)(2,1)} %second_section.2), calls=%async_computation.3 | async-start | bytes 2097152 | tf_op jit(solution)/shard_map/all_to_all | solution.py:424
  156.1 31.1 %all-to-all-start.4 = ((f16[8,1,512,128]{3,2,1,0:T(8,128)(2,1)}), f16[8,1,512,128]{3,2,1,0:T(8,128)(2,1)S(1)}, u32[]{:S(2)}, u32[]{:S(2)}) async-start(f16[8,1,512,128]{3,2,1,0:T(8,128)(2,1)} %bitcast.5), calls=%async_computation.4 | async-start | bytes 2097152 | tf_op jit(solution)/shard_map/all_to_all | solution.py:424
  160.3 28.4 %copy-start.4 = (bf16[64,8,512]{2,1,0:T(8,128)(2,1)}, bf16[64,8,512]{2,1,0:T(8,128)(2,1)S(1)}, u32[]{:S(2)}) copy-start(bf16[64,8,512]{2,1,0:T(8,128)(2,1)S(1)} %reshape.161.a_ref) | copy-start | bytes 1572868
  160.3 14.9 %collective-permute-start = (bf16[64,8,512]{2,1,0:T(8,128)(2,1)S(1)}, bf16[64,8,512]{2,1,0:T(8,128)(2,1)}, u32[]{:S(2)}, u32[]{:S(2)}) collective-permute-start(bf16[64,8,512]{2,1,0:T(8,128)(2,1)S(1)} %reshape.161.a_ref), channel_id=1, source_target_pairs={{0,8},{8,0},{16,24},{24,16},{1,9},{9,1},{17,25},{25,17},{2,10},{10... | collective-permute-start | bytes 1572872 | tf_op jit(solution)/shard_map/ppermute | solution.py:324
  161.8 25.3 %collective-permute-start.1 = (bf16[64,8,512]{2,1,0:T(8,128)(2,1)S(1)}, bf16[64,8,512]{2,1,0:T(8,128)(2,1)}, u32[]{:S(2)}, u32[]{:S(2)}) collective-permute-start(bf16[64,8,512]{2,1,0:T(8,128)(2,1)S(1)} %reshape.161.a_ref), channel_id=1, source_target_pairs={{0,16},{8,24},{16,0},{24,8},{1,17},{9,25},{17,1},{25,9},{2,18},{10... | collective-permute-start | bytes 1572872 | tf_op jit(solution)/shard_map/ppermute | solution.py:324
  163.4 23.8 %collective-permute-start.2 = (bf16[64,8,512]{2,1,0:T(8,128)(2,1)S(1)}, bf16[64,8,512]{2,1,0:T(8,128)(2,1)}, u32[]{:S(2)}, u32[]{:S(2)}) collective-permute-start(bf16[64,8,512]{2,1,0:T(8,128)(2,1)S(1)} %reshape.161.a_ref), channel_id=1, source_target_pairs={{0,24},{8,16},{16,8},{24,0},{1,25},{9,17},{17,9},{25,1},{2,26},{10... | collective-permute-start | bytes 1572872 | tf_op jit(solution)/shard_map/ppermute | solution.py:324
  164.4 41.8 %copy-start.3 = (bf16[64,8,512]{2,1,0:T(8,128)(2,1)}, bf16[64,8,512]{2,1,0:T(8,128)(2,1)S(1)}, u32[]{:S(2)}) copy-start(bf16[64,8,512]{2,1,0:T(8,128)(2,1)S(1)} %reshape.162.a_ref) | copy-start | bytes 1572868
  199.2 39.7 %all-to-all-start.5 = ((bf16[8,1,2,64,512]{4,3,2,1,0:T(8,128)(2,1)}), bf16[8,1,2,64,512]{4,3,2,1,0:T(8,128)(2,1)S(1)}, u32[]{:S(2)}, u32[]{:S(2)}) async-start(bf16[8,1,2,64,512]{4,3,2,1,0:T(8,128)(2,1)} %second_section.3), calls=%async_computation.5 | async-start | bytes 2097152 | tf_op jit(solution)/shard_map/all_to_all | solution.py:424
  204.0 143.8 %reduce-scatter.3.cloned.1.call-start = ((), (), s32[]{:S(2)}) async-start(), calls=%async_computation.11 | async-start | bytes 589824 | tf_op jit(solution)/shard_map/reduce_scatter | solution.py:526
  204.0 34.8 %collective-permute-start.3 = (bf16[64,8,512]{2,1,0:T(8,128)(2,1)S(1)}, bf16[64,8,512]{2,1,0:T(8,128)(2,1)S(1)}, u32[]{:S(2)}, u32[]{:S(2)}) collective-permute-start(bf16[64,8,512]{2,1,0:T(8,128)(2,1)S(1)} %reshape.162.a_ref), channel_id=1, source_target_pairs={{0,8},{8,0},{16,24},{24,16},{1,9},{9,1},{17,25},{25,17},{2,10},{10... | collective-permute-start | bytes 1572872 | tf_op jit(solution)/shard_map/ppermute | solution.py:324
  205.3 33.5 %collective-permute-start.4 = (bf16[64,8,512]{2,1,0:T(8,128)(2,1)S(1)}, bf16[64,8,512]{2,1,0:T(8,128)(2,1)S(1)}, u32[]{:S(2)}, u32[]{:S(2)}) collective-permute-start(bf16[64,8,512]{2,1,0:T(8,128)(2,1)S(1)} %reshape.162.a_ref), channel_id=1, source_target_pairs={{0,16},{8,24},{16,0},{24,8},{1,17},{9,25},{17,1},{25,9},{2,18},{10... | collective-permute-start | bytes 1572872 | tf_op jit(solution)/shard_map/ppermute | solution.py:324
  206.2 32.7 %collective-permute-start.5 = (bf16[64,8,512]{2,1,0:T(8,128)(2,1)S(1)}, bf16[64,8,512]{2,1,0:T(8,128)(2,1)S(1)}, u32[]{:S(2)}, u32[]{:S(2)}) collective-permute-start(bf16[64,8,512]{2,1,0:T(8,128)(2,1)S(1)} %reshape.162.a_ref), channel_id=1, source_target_pairs={{0,24},{8,16},{16,8},{24,0},{1,25},{9,17},{17,9},{25,1},{2,26},{10... | collective-permute-start | bytes 1572872 | tf_op jit(solution)/shard_map/ppermute | solution.py:324
  238.8 1.5 copy-start.10
  238.9 1.5 copy-start.12
  238.9 0.9 copy-start.14
  240.4 34.8 %copy-start.5 = (bf16[64,8,512]{2,1,0:T(8,128)(2,1)}, bf16[64,8,512]{2,1,0:T(8,128)(2,1)S(1)}, u32[]{:S(2)}) copy-start(bf16[64,8,512]{2,1,0:T(8,128)(2,1)S(1)} %reshape.166.a_ref) | copy-start | bytes 1572868
  240.4 35.3 %collective-permute-start.6 = (bf16[64,8,512]{2,1,0:T(8,128)(2,1)S(1)}, bf16[64,8,512]{2,1,0:T(8,128)(2,1)S(1)}, u32[]{:S(2)}, u32[]{:S(2)}) collective-permute-start(bf16[64,8,512]{2,1,0:T(8,128)(2,1)S(1)} %reshape.166.a_ref), channel_id=1, source_target_pairs={{0,8},{8,0},{16,24},{24,16},{1,9},{9,1},{17,25},{25,17},{2,10},{10... | collective-permute-start | bytes 1572872 | tf_op jit(solution)/shard_map/ppermute | solution.py:324
  241.6 34.2 %collective-permute-start.7 = (bf16[64,8,512]{2,1,0:T(8,128)(2,1)S(1)}, bf16[64,8,512]{2,1,0:T(8,128)(2,1)S(1)}, u32[]{:S(2)}, u32[]{:S(2)}) collective-permute-start(bf16[64,8,512]{2,1,0:T(8,128)(2,1)S(1)} %reshape.166.a_ref), channel_id=1, source_target_pairs={{0,16},{8,24},{16,0},{24,8},{1,17},{9,25},{17,1},{25,9},{2,18},{10... | collective-permute-start | bytes 1572872 | tf_op jit(solution)/shard_map/ppermute | solution.py:324
  242.4 33.4 %collective-permute-start.8 = (bf16[64,8,512]{2,1,0:T(8,128)(2,1)S(1)}, bf16[64,8,512]{2,1,0:T(8,128)(2,1)S(1)}, u32[]{:S(2)}, u32[]{:S(2)}) collective-permute-start(bf16[64,8,512]{2,1,0:T(8,128)(2,1)S(1)} %reshape.166.a_ref), channel_id=1, source_target_pairs={{0,24},{8,16},{16,8},{24,0},{1,25},{9,17},{17,9},{25,1},{2,26},{10... | collective-permute-start | bytes 1572872 | tf_op jit(solution)/shard_map/ppermute | solution.py:324
  244.0 103.8 %reduce-scatter.5.cloned.1.call-start = ((), (), s32[]{:S(2)}) async-start(), calls=%async_computation.12 | async-start | bytes 589824 | tf_op jit(solution)/shard_map/reduce_scatter | solution.py:526
  275.7 34.9 %copy-start.6 = (bf16[64,8,512]{2,1,0:T(8,128)(2,1)}, bf16[64,8,512]{2,1,0:T(8,128)(2,1)S(1)}, u32[]{:S(2)}) copy-start(bf16[64,8,512]{2,1,0:T(8,128)(2,1)S(1)} %reshape.167.a_ref) | copy-start | bytes 1572868
  275.8 3.6 copy-start.11
  275.8 3.6 copy-start.13
  275.8 3.6 copy-start.15
  275.8 34.8 %collective-permute-start.9 = (bf16[64,8,512]{2,1,0:T(8,128)(2,1)S(1)}, bf16[64,8,512]{2,1,0:T(8,128)(2,1)S(1)}, u32[]{:S(2)}, u32[]{:S(2)}) collective-permute-start(bf16[64,8,512]{2,1,0:T(8,128)(2,1)S(1)} %reshape.167.a_ref), channel_id=1, source_target_pairs={{0,8},{8,0},{16,24},{24,16},{1,9},{9,1},{17,25},{25,17},{2,10},{10... | collective-permute-start | bytes 1572872 | tf_op jit(solution)/shard_map/ppermute | solution.py:324
  277.0 33.6 %collective-permute-start.10 = (bf16[64,8,512]{2,1,0:T(8,128)(2,1)S(1)}, bf16[64,8,512]{2,1,0:T(8,128)(2,1)S(1)}, u32[]{:S(2)}, u32[]{:S(2)}) collective-permute-start(bf16[64,8,512]{2,1,0:T(8,128)(2,1)S(1)} %reshape.167.a_ref), channel_id=1, source_target_pairs={{0,16},{8,24},{16,0},{24,8},{1,17},{9,25},{17,1},{25,9},{2,18},{10... | collective-permute-start | bytes 1572872 | tf_op jit(solution)/shard_map/ppermute | solution.py:324
  277.7 32.9 %collective-permute-start.11 = (bf16[64,8,512]{2,1,0:T(8,128)(2,1)S(1)}, bf16[64,8,512]{2,1,0:T(8,128)(2,1)}, u32[]{:S(2)}, u32[]{:S(2)}) collective-permute-start(bf16[64,8,512]{2,1,0:T(8,128)(2,1)S(1)} %reshape.167.a_ref), channel_id=1, source_target_pairs={{0,24},{8,16},{16,8},{24,0},{1,25},{9,17},{17,9},{25,1},{2,26},{10... | collective-permute-start | bytes 1572872 | tf_op jit(solution)/shard_map/ppermute | solution.py:324
  310.6 5.8 %copy-start.16 = (bf16[64,8,512]{2,1,0:T(8,128)(2,1)}, bf16[64,8,512]{2,1,0:T(8,128)(2,1)S(1)}, u32[]{:S(2)}) copy-start(bf16[64,8,512]{2,1,0:T(8,128)(2,1)S(1)} %collective-permute-done.9.b_ref) | copy-start | bytes 1572868
  310.6 0.8 copy-start.17
  311.5 36.2 %all-to-all-start.6 = ((f32[8,2,32,256]{3,2,1,0:T(8,128)}), f32[8,2,32,256]{3,2,1,0:T(8,128)S(1)}, u32[]{:S(2)}, u32[]{:S(2)}) async-start(f32[8,2,32,256]{3,2,1,0:T(8,128)} %bitcast.67), calls=%async_computation.8 | async-start | bytes 1048576 | tf_op jit(solution)/shard_map/all_to_all | solution.py:424
Sparse Core Ops, SparseCore 0:
  26.1 33.3 all-gather.1
  244.1 31.2 reduce-scatter.2
  279.5 31.2 reduce-scatter.4

commit v9 on v8

--- a/solution.py
+++ b/solution.py
@@ -214,27 +214,27 @@
             rows = slice(half + lag * seg_total, half + (lag + 1) * seg_total)
             rows_ref[jj, rows, lanes] = (real * lag_sin + imag * lag_cos).astype(jnp.bfloat16)
 
-    def one_block(next_ref, now_ref, units, jj):
-        deep = 256
-        for k in range(A // deep):
-            inner = slice(k * deep, (k + 1) * deep)
-            if now_ref is not None:
-                for unit in range(2):
-                    columns = t_ref[jj, unit * tmpl : (unit + 1) * tmpl, inner]
-                    pltpu.matmul_push_rhs(columns, k % 2, unit, transpose=True)
-            if next_ref is not None:
-                for chunk in range(k * deep // 128, (k + 1) * deep // 128):
-                    make_rows(next_ref, jj, chunk)
-            if now_ref is not None:
-                for unit_ref in units:
-                    pltpu.matmul_acc_lhs(unit_ref, now_ref[jj, :, inner], load_staged_rhs=k % 2)
+    deep = 256
+    tiles = [(jj, k) for jj in range(per_quad) for k in range(A // deep)]
+
+    def push(index):
+        jj, k = tiles[index]
+        for unit in range(2):
+            columns = t_ref[jj, unit * tmpl : (unit + 1) * tmpl, k * deep : (k + 1) * deep]
+            pltpu.matmul_push_rhs(columns, index % 2, unit, transpose=True)
 
     def one_group(next_ref, now_ref):
         def scoped(*units):
-            @pl.loop(0, per_quad)
-            def _(jj):
-                one_block(next_ref, now_ref, units, jj)
-
+            push(0)
+            for index, (jj, k) in enumerate(tiles):
+                if index + 1 < len(tiles):
+                    push(index + 1)
+                for unit_ref in units:
+                    rows = now_ref[jj, :, k * deep : (k + 1) * deep]
+                    pltpu.matmul_acc_lhs(unit_ref, rows, load_staged_rhs=index % 2)
+                if next_ref is not None:
+                    for chunk in range(k * deep // 128, (k + 1) * deep // 128):
+                        make_rows(next_ref, jj, chunk)
             for unit, unit_ref in enumerate(units):
                 acc_ref[unit] += pltpu.matmul_pop(unit_ref)
 
@@ -247,7 +247,8 @@
 
         @pl.loop(0, per_quad)
         def _(jj):
-            one_block(even_ref, None, (), jj)
+            for chunk in range(A // 128):
+                make_rows(even_ref, jj, chunk)
 
     @pl.when((step % 2 == 1) & (step < last))
     def _():

time: 379 us -> 378 us (level)
  Pallas kernels: 186 us -> 173 us
  starting transfers between devices: 46.1 us -> 56.6 us
    pallas_call x4, Pallas kernels: 125 us -> 113 us  [lag_products(): pl.pallas_call(lag_kernel, grid=(quads + 1,), in_specs=[pl.BlockSpec(memo...]
    all_to_all x7, starting transfers between devices: 31.7 us -> 42.3 us  [exchange(): return lax.all_to_all(sent, 'freq', split_axis=0, concat_axis=0, tiled=True)]
  transfers between devices with their start and end apart: 22 -> 22, of which waited for: 5 -> 5; matrix products, arithmetic and copies ran while one was open for 4% -> 4% of each run, Pallas kernels for 47% -> 43%
where the time goes in v9:
time: 378 us; the launch traced here: 375 us
  Pallas kernels  173 us (46%)
  waiting for transfers between devices  77.5 us (21%)
  starting transfers between devices  56.6 us (15%)
  blocking collectives  20.5 us (5%)
  other arithmetic  15.8 us (4%)
  local copies, waits for them, and re-layouts  15.5 us (4%)
  between operations  13.8 us (4%)
    pallas_call x4, Pallas kernels, lag_products(): pl.pallas_call(lag_kernel, grid=(quads + 1,), in_specs=[pl.BlockSpec(memo...  113 us
    all_to_all x7, waiting for transfers between devices, exchange(): return lax.all_to_all(sent, 'freq', split_axis=0, concat_axis=0, tiled=True)  53.9 us
    all_to_all x7, starting transfers between devices, exchange(): return lax.all_to_all(sent, 'freq', split_axis=0, concat_axis=0, tiled=True)  42.3 us
    pallas_call x2, Pallas kernels, lay_out(): pl.pallas_call(layout_kernel, grid=(steps, tmpl // batch), in_specs=[pl.B...  34.6 us
    ppermute x12, waiting for transfers between devices, spread(): lax.ppermute(data, 'tmpl', [(n, n ^ bit) for n in range(4)])  22.8 us
    pallas_call x2, Pallas kernels, second_section(): pl.pallas_call(second_kernel, grid=(segs,), in_specs=[pl.BlockSpec((parts...  21.1 us
    all_to_all x1, blocking collectives, exchange(): return lax.all_to_all(sent, 'freq', split_axis=0, concat_axis=0, tiled=True)  20.5 us
    ppermute x12, starting transfers between devices, spread(): lax.ppermute(data, 'tmpl', [(n, n ^ bit) for n in range(4)])  14.2 us
  transfers between devices with their start and end apart: 22, of which 5 were waited for; matrix products, arithmetic and copies ran while one was open for 4% of the time, Pallas kernels for 43%

profile of v9, /device:TPU:0, one launch (start us, length us, event | category | flops | bytes accessed | tf_op | source)
XLA Modules:
  0.0 374.8 jit_solution(14487686012358762800)
XLA Ops:
  6.5 4.2 %reshape.154 = f32[2,2,4,65536]{3,2,1,0:T(4,128)} reshape(f32[16,65536]{1,0:T(8,128)} %param.17) | data formatting | bytes 8388608 | tf_op jit(solution)/shard_map/reshape | solution.py:495
  10.7 4.1 %fusion.1 = (f16[2,1,4,65536]{3,2,0,1:T(4,128)(2,1)}, f16[2,1,4,65536]{3,2,0,1:T(4,128)(2,1)S(1)}) fusion(f32[2,2,4,65536]{3,2,1,0:T(4,128)} %reshape.154), kind=kLoop, calls=%fused_computation.2 | loop fusion | flops 2097152 | bytes 6291456 | tf_op jit(solution)/shard_map/convert_element_type | solution.py:430
  14.9 1.1 convert_element_type.53
  16.0 1.3 copy.63
  17.3 6.3 %all-to-all-start = ((f16[8,8,64,128]{3,2,1,0:T(8,128)(2,1)}), f16[8,8,64,128]{3,2,1,0:T(8,128)(2,1)S(1)}, u32[]{:S(2)}, u32[]{:S(2)}) async-start(f16[8,8,64,128]{3,2,1,0:T(8,128)(2,1)} %bitcast.47), calls=%async_computation | async-start | bytes 2097152 | tf_op jit(solution)/shard_map/all_to_all | solution.py:425
  23.7 0.7 all-gather.2.cloned.1.call-update
  24.4 17.2 %lay_out.2.refs_0_ = bf16[64,2,256,512]{3,2,1,0:T(8,128)(2,1)} custom-call(s32[257]{0:T(512)S(1)} %get-tuple-element.98.cut_ref, bf16[256,2,64,512]{3,2,1,0:T(8,128)(2,1)} %t_ref.3), custom_call_target="tpu_custom_call" | custom-call | bytes 67108864 | tf_op jit(solution)/shard_map/lay_out/pallas_call | solution.py:360
  41.7 17.0 %all-to-all-done = f16[8,8,64,128]{3,2,1,0:T(8,128)(2,1)S(1)} async-done(((f16[8,8,64,128]{3,2,1,0:T(8,128)(2,1)}), f16[8,8,64,128]{3,2,1,0:T(8,128)(2,1)S(1)}, u32[]{:S(2)}, u32[]{:S(2)}) %all-to-all-start) | async-done | bytes 1048608 | tf_op jit(solution)/shard_map/all_to_all | solution.py:425
  58.7 0.3 convert_multiply_fusion.3.x_ref
  59.0 2.6 first_section.2
  61.5 1.3 fusion.6
  62.8 3.6 all-to-all-start.1
  66.4 2.2 convert_element_type.57
  68.6 1.3 copy.62
  69.9 0.2 fusion.18
  70.1 0.2 fusion.16
  70.4 2.6 multiply_add_fusion
  73.0 1.1 slice.34
  74.0 0.2 copy.55
  74.3 17.4 %lay_out.3 = bf16[64,2,256,512]{3,2,1,0:T(8,128)(2,1)} custom-call(s32[257]{0:T(512)S(1)} %get-tuple-element.97.cut_ref, bf16[256,2,64,512]{3,2,1,0:T(8,128)(2,1)} %t_ref.3, bf16[64,2,256,512]{3,2,1,0:T(8,128)(2,1)} %lay_out.2.refs_0_), custom_call_target="tpu_custom_call", output_to_operand_aliasing={{}: (2, {})} | custom-call | bytes 67108864 | tf_op jit(solution)/shard_map/lay_out/pallas_call | solution.py:360
  91.6 0.9 multiply_rsqrt_fusion.wa_ref
  92.5 1.9 fusion.5.wm_ref
  94.4 5.3 %all-to-all-start.2 = ((f16[8,8,64,128]{3,2,1,0:T(8,128)(2,1)}), f16[8,8,64,128]{3,2,1,0:T(8,128)(2,1)S(1)}, u32[]{:S(2)}, u32[]{:S(2)}) async-start(f16[8,8,64,128]{3,2,1,0:T(8,128)(2,1)} %bitcast.56), calls=%async_computation.2 | async-start | bytes 2097152 | tf_op jit(solution)/shard_map/all_to_all | solution.py:425
  99.7 1.5 convert_multiply_fusion.2.y_ref
  101.2 10.6 %second_section.2 = bf16[8,1,2,64,512]{4,3,2,1,0:T(8,128)(2,1)} custom-call(f32[8,1,512,128]{3,2,1,0:T(8,128)} %convert_multiply_fusion.2.y_ref, f32[256,1024]{1,0:T(8,128)} %constant.98.clone.tc_ref, f32[256,1024]{1,0:T(8,128)} %constant.99.clone.ts_ref, f32[1,1024]{1,0:T(1,128)} %constant.100.clone.ec_ref, f32[1,1024]{1,0:T(1,128)} %constant.101.clone.es_ref, ...), custom_call_target="tpu_custom_call" | custom-call | flops 3321888768 | bytes 3145728 | tf_op jit(solution)/shard_map/second_section/pallas_call | solution.py:177
  111.7 14.5 %all-to-all-done.2 = f16[8,8,64,128]{3,2,1,0:T(8,128)(2,1)S(1)} async-done(((f16[8,8,64,128]{3,2,1,0:T(8,128)(2,1)}), f16[8,8,64,128]{3,2,1,0:T(8,128)(2,1)S(1)}, u32[]{:S(2)}, u32[]{:S(2)}) %all-to-all-start.2) | async-done | bytes 1048608 | tf_op jit(solution)/shard_map/all_to_all | solution.py:425
  126.2 3.6 all-to-all-start.3
  129.8 0.3 convert_multiply_fusion.1.x_ref
  130.1 2.6 first_section.3
  132.6 1.2 fusion.7
  133.9 22.4 %all-to-all-done.3 = bf16[8,1,2,64,512]{4,3,2,1,0:T(8,128)(2,1)S(1)} async-done(((bf16[8,1,2,64,512]{4,3,2,1,0:T(8,128)(2,1)}), bf16[8,1,2,64,512]{4,3,2,1,0:T(8,128)(2,1)S(1)}, u32[]{:S(2)}, u32[]{:S(2)}) %all-to-all-start.3) | async-done | bytes 1048608 | tf_op jit(solution)/shard_map/all_to_all | solution.py:425
  156.3 3.6 all-to-all-start.4
  160.0 0.4 copy.67
  160.5 1.6 collective-permute-start
  162.1 1.5 collective-permute-start.1
  163.6 0.5 collective-permute-start.2
  164.1 0.4 copy.66
  164.5 0.1 reshape.162.a_ref
  164.6 10.8 %collective-permute-done.b_ref = bf16[64,8,512]{2,1,0:T(8,128)(2,1)} collective-permute-done((bf16[64,8,512]{2,1,0:T(8,128)(2,1)S(1)}, bf16[64,8,512]{2,1,0:T(8,128)(2,1)}, u32[]{:S(2)}, u32[]{:S(2)}) %collective-permute-start) | collective-permute-done | bytes 524320 | tf_op jit(solution)/shard_map/ppermute | solution.py:325
  175.4 12.0 %collective-permute-done.1.x_ref = bf16[64,8,512]{2,1,0:T(8,128)(2,1)} collective-permute-done((bf16[64,8,512]{2,1,0:T(8,128)(2,1)S(1)}, bf16[64,8,512]{2,1,0:T(8,128)(2,1)}, u32[]{:S(2)}, u32[]{:S(2)}) %collective-permute-start.1) | collective-permute-done | bytes 524320 | tf_op jit(solution)/shard_map/ppermute | solution.py:325
  187.4 1.5 convert_multiply_fusion.y_ref
  188.9 10.5 %second_section.3 = bf16[8,1,2,64,512]{4,3,2,1,0:T(8,128)(2,1)} custom-call(f32[8,1,512,128]{3,2,1,0:T(8,128)} %convert_multiply_fusion.y_ref, f32[256,1024]{1,0:T(8,128)} %constant.98.clone.tc_ref, f32[256,1024]{1,0:T(8,128)} %constant.99.clone.ts_ref, f32[1,1024]{1,0:T(1,128)} %constant.100.clone.ec_ref, f32[1,1024]{1,0:T(1,128)} %constant.101.clone.es_ref, ...), custom_call_target="tpu_custom_call" | custom-call | flops 3321888768 | bytes 3145728 | tf_op jit(solution)/shard_map/second_section/pallas_call | solution.py:177
  199.5 15.1 %all-to-all-start.5 = ((bf16[8,1,2,64,512]{4,3,2,1,0:T(8,128)(2,1)}), bf16[8,1,2,64,512]{4,3,2,1,0:T(8,128)(2,1)S(1)}, u32[]{:S(2)}, u32[]{:S(2)}) async-start(bf16[8,1,2,64,512]{4,3,2,1,0:T(8,128)(2,1)} %second_section.3), calls=%async_computation.5 | async-start | bytes 2097152 | tf_op jit(solution)/shard_map/all_to_all | solution.py:425
  214.6 1.3 collective-permute-start.3
  215.9 0.8 collective-permute-start.4
  216.7 1.4 collective-permute-start.5
  218.1 28.1 %lag_products.4 = f32[16,32,256]{2,1,0:T(8,128)} custom-call(s32[1]{0:T(128)} %bitcast.11.place_ref, bf16[64,8,512]{2,1,0:T(8,128)(2,1)} %copy-done.4, bf16[64,8,512]{2,1,0:T(8,128)(2,1)} %collective-permute-done.b_ref, bf16[64,8,512]{2,1,0:T(8,128)(2,1)} %collective-permute-done.1.x_ref, bf16[64,8,512]{2,1,0:T(8,128)(2,1)} %collective-permute-done.2.y_ref, ...), custom_call_target="tpu_custom_call" | custom-call | flops 17179869184 | bytes 35651584 | tf_op jit(solution)/shard_map/lag_products/pallas_call | solution.py:292
  246.3 0.8 copy-done.14
  247.2 0.4 copy.65
  247.6 0.1 reshape.166.a_ref
  247.8 1.3 collective-permute-start.6
  249.1 0.8 collective-permute-start.7
  249.9 1.4 collective-permute-start.8
  251.4 28.1 %lag_products.5 = f32[16,32,256]{2,1,0:T(8,128)} custom-call(s32[1]{0:T(128)} %bitcast.11.place_ref, bf16[64,8,512]{2,1,0:T(8,128)(2,1)} %copy-done.3, bf16[64,8,512]{2,1,0:T(8,128)(2,1)} %copy-done.10, bf16[64,8,512]{2,1,0:T(8,128)(2,1)} %copy-done.12, bf16[64,8,512]{2,1,0:T(8,128)(2,1)} %copy-done.14, bf16[64,512,512]{2,1,0:T(8,128)(2,1)} %bitcast.53, ...), custom_call_target="tpu_custom_call" | custom-call | flops 17179869184 | bytes 35651584 | tf_op jit(solution)/shard_map/lag_products/pallas_call | solution.py:292
  279.6 0.4 copy.64
  280.2 1.3 collective-permute-start.9
  281.5 0.8 collective-permute-start.10
  282.3 1.4 collective-permute-start.11
  283.8 28.2 %lag_products.6 = f32[16,32,256]{2,1,0:T(8,128)} custom-call(s32[1]{0:T(128)} %bitcast.11.place_ref, bf16[64,8,512]{2,1,0:T(8,128)(2,1)} %copy-done.5, bf16[64,8,512]{2,1,0:T(8,128)(2,1)} %copy-done.11, bf16[64,8,512]{2,1,0:T(8,128)(2,1)} %copy-done.13, bf16[64,8,512]{2,1,0:T(8,128)(2,1)} %copy-done.15, bf16[64,512,512]{2,1,0:T(8,128)(2,1)} %bitcast.54, ...), custom_call_target="tpu_custom_call" | custom-call | flops 17179869184 | bytes 35651584 | tf_op jit(solution)/shard_map/lag_products/pallas_call | solution.py:292
  312.0 0.8 copy-done.17
  312.9 4.9 %all-to-all-start.6 = ((f32[8,2,32,256]{3,2,1,0:T(8,128)}), f32[8,2,32,256]{3,2,1,0:T(8,128)S(1)}, u32[]{:S(2)}, u32[]{:S(2)}) async-start(f32[8,2,32,256]{3,2,1,0:T(8,128)} %bitcast.67), calls=%async_computation.8 | async-start | bytes 1048576 | tf_op jit(solution)/shard_map/all_to_all | solution.py:425
  317.8 28.1 %lag_products.7 = f32[16,32,256]{2,1,0:T(8,128)} custom-call(s32[1]{0:T(128)} %bitcast.11.place_ref, bf16[64,8,512]{2,1,0:T(8,128)(2,1)} %copy-done.6, bf16[64,8,512]{2,1,0:T(8,128)(2,1)} %copy-done.16, bf16[64,8,512]{2,1,0:T(8,128)(2,1)} %copy-done.17, bf16[64,8,512]{2,1,0:T(8,128)(2,1)} %collective-permute-done.11.y_ref, bf16[64,512,512]{2,1,0:T(8,128)(2,1)} %bitcast.55, ...), custom_call_target="tpu_custom_call" | custom-call | flops 17179869184 | bytes 35651584 | tf_op jit(solution)/shard_map/lag_products/pallas_call | solution.py:292
  346.0 20.5 %all_to_all.40 = f32[8,2,32,256]{3,2,1,0:T(8,128)S(1)} all-to-all(f32[8,2,32,256]{3,2,1,0:T(8,128)} %bitcast.68), channel_id=1, replica_groups=mesh['tmpl'=4,'freq'=8] {'freq'}, dimensions={0} | all-to-all | bytes 1048576 | tf_op jit(solution)/shard_map/all_to_all | solution.py:425
  366.5 1.6 pad_maximum_fusion
  (67 shorter events, 0.8 us)
Async XLA Ops:
  16.0 8.4 %copy-start.8 = (s32[256]{0:T(256)S(1)}, s32[256]{0:T(256)}, u32[]{:S(2)}) copy-start(s32[256]{0:T(256)} %param.20) | copy-start | bytes 3076
  17.3 41.3 %all-to-all-start = ((f16[8,8,64,128]{3,2,1,0:T(8,128)(2,1)}), f16[8,8,64,128]{3,2,1,0:T(8,128)(2,1)S(1)}, u32[]{:S(2)}, u32[]{:S(2)}) async-start(f16[8,8,64,128]{3,2,1,0:T(8,128)(2,1)} %bitcast.47), calls=%async_computation | async-start | bytes 2097152 | tf_op jit(solution)/shard_map/all_to_all | solution.py:425
  23.6 49.3 %all-gather.2.cloned.1.call-start = ((), (), s32[]{:S(2)}) async-start(), calls=%async_computation.10 | async-start | bytes 1179648 | tf_op jit(solution)/shard_map/all_gather | solution.py:487
  41.7 17.3 %copy-start = (bf16[512,512]{1,0:T(8,128)(2,1)S(1)}, bf16[512,512]{1,0:T(8,128)(2,1)}, u32[]{:S(2)}) copy-start(bf16[512,512]{1,0:T(8,128)(2,1)} %constant.96.clone.high_ref) | copy-start | bytes 1572868
  41.7 17.3 %copy-start.1 = (bf16[512,512]{1,0:T(8,128)(2,1)S(1)}, bf16[512,512]{1,0:T(8,128)(2,1)}, u32[]{:S(2)}) copy-start(bf16[512,512]{1,0:T(8,128)(2,1)} %constant.97.clone.low_ref) | copy-start | bytes 1572868
  62.8 31.6 %all-to-all-start.1 = ((f16[8,1,512,128]{3,2,1,0:T(8,128)(2,1)}), f16[8,1,512,128]{3,2,1,0:T(8,128)(2,1)S(1)}, u32[]{:S(2)}, u32[]{:S(2)}) async-start(f16[8,1,512,128]{3,2,1,0:T(8,128)(2,1)} %fusion.6), calls=%async_computation.1 | async-start | bytes 2097152 | tf_op jit(solution)/shard_map/all_to_all | solution.py:425
  66.4 3.5 copy-start.9
  74.2 18.3 %copy-start.2 = (f32[512,512]{0,1:T(8,128)S(1)}, f32[512,512]{0,1:T(8,128)}, u32[]{:S(2)}) copy-start(f32[512,512]{0,1:T(8,128)} %all-gather.2.cloned.1.call-done) | copy-start | bytes 3145732
  74.3 18.2 %copy-start.7 = (f32[256,256]{1,0:T(8,128)S(1)}, f32[256,256]{1,0:T(8,128)}, u32[]{:S(2)}) copy-start(f32[256,256]{1,0:T(8,128)} %constant.95.clone) | copy-start | bytes 786436
  94.4 31.9 %all-to-all-start.2 = ((f16[8,8,64,128]{3,2,1,0:T(8,128)(2,1)}), f16[8,8,64,128]{3,2,1,0:T(8,128)(2,1)S(1)}, u32[]{:S(2)}, u32[]{:S(2)}) async-start(f16[8,8,64,128]{3,2,1,0:T(8,128)(2,1)} %bitcast.56), calls=%async_computation.2 | async-start | bytes 2097152 | tf_op jit(solution)/shard_map/all_to_all | solution.py:425
  126.2 30.1 %all-to-all-start.3 = ((bf16[8,1,2,64,512]{4,3,2,1,0:T(8,128)(2,1)}), bf16[8,1,2,64,512]{4,3,2,1,0:T(8,128)(2,1)S(1)}, u32[]{:S(2)}, u32[]{:S(2)}) async-start(bf16[8,1,2,64,512]{4,3,2,1,0:T(8,128)(2,1)} %second_section.2), calls=%async_computation.3 | async-start | bytes 2097152 | tf_op jit(solution)/shard_map/all_to_all | solution.py:425
  156.3 31.1 %all-to-all-start.4 = ((f16[8,1,512,128]{3,2,1,0:T(8,128)(2,1)}), f16[8,1,512,128]{3,2,1,0:T(8,128)(2,1)S(1)}, u32[]{:S(2)}, u32[]{:S(2)}) async-start(f16[8,1,512,128]{3,2,1,0:T(8,128)(2,1)} %bitcast.5), calls=%async_computation.4 | async-start | bytes 2097152 | tf_op jit(solution)/shard_map/all_to_all | solution.py:425
  160.5 28.4 %copy-start.4 = (bf16[64,8,512]{2,1,0:T(8,128)(2,1)}, bf16[64,8,512]{2,1,0:T(8,128)(2,1)S(1)}, u32[]{:S(2)}) copy-start(bf16[64,8,512]{2,1,0:T(8,128)(2,1)S(1)} %reshape.161.a_ref) | copy-start | bytes 1572868
  160.5 14.9 %collective-permute-start = (bf16[64,8,512]{2,1,0:T(8,128)(2,1)S(1)}, bf16[64,8,512]{2,1,0:T(8,128)(2,1)}, u32[]{:S(2)}, u32[]{:S(2)}) collective-permute-start(bf16[64,8,512]{2,1,0:T(8,128)(2,1)S(1)} %reshape.161.a_ref), channel_id=1, source_target_pairs={{0,8},{8,0},{16,24},{24,16},{1,9},{9,1},{17,25},{25,17},{2,10},{10... | collective-permute-start | bytes 1572872 | tf_op jit(solution)/shard_map/ppermute | solution.py:325
  162.1 25.3 %collective-permute-start.1 = (bf16[64,8,512]{2,1,0:T(8,128)(2,1)S(1)}, bf16[64,8,512]{2,1,0:T(8,128)(2,1)}, u32[]{:S(2)}, u32[]{:S(2)}) collective-permute-start(bf16[64,8,512]{2,1,0:T(8,128)(2,1)S(1)} %reshape.161.a_ref), channel_id=1, source_target_pairs={{0,16},{8,24},{16,0},{24,8},{1,17},{9,25},{17,1},{25,9},{2,18},{10... | collective-permute-start | bytes 1572872 | tf_op jit(solution)/shard_map/ppermute | solution.py:325
  163.6 23.8 %collective-permute-start.2 = (bf16[64,8,512]{2,1,0:T(8,128)(2,1)S(1)}, bf16[64,8,512]{2,1,0:T(8,128)(2,1)}, u32[]{:S(2)}, u32[]{:S(2)}) collective-permute-start(bf16[64,8,512]{2,1,0:T(8,128)(2,1)S(1)} %reshape.161.a_ref), channel_id=1, source_target_pairs={{0,24},{8,16},{16,8},{24,0},{1,25},{9,17},{17,9},{25,1},{2,26},{10... | collective-permute-start | bytes 1572872 | tf_op jit(solution)/shard_map/ppermute | solution.py:325
  164.6 52.1 %copy-start.3 = (bf16[64,8,512]{2,1,0:T(8,128)(2,1)}, bf16[64,8,512]{2,1,0:T(8,128)(2,1)S(1)}, u32[]{:S(2)}) copy-start(bf16[64,8,512]{2,1,0:T(8,128)(2,1)S(1)} %reshape.162.a_ref) | copy-start | bytes 1572868
  199.5 46.8 %all-to-all-start.5 = ((bf16[8,1,2,64,512]{4,3,2,1,0:T(8,128)(2,1)}), bf16[8,1,2,64,512]{4,3,2,1,0:T(8,128)(2,1)S(1)}, u32[]{:S(2)}, u32[]{:S(2)}) async-start(bf16[8,1,2,64,512]{4,3,2,1,0:T(8,128)(2,1)} %second_section.3), calls=%async_computation.5 | async-start | bytes 2097152 | tf_op jit(solution)/shard_map/all_to_all | solution.py:425
  214.5 131.4 %reduce-scatter.3.cloned.1.call-start = ((), (), s32[]{:S(2)}) async-start(), calls=%async_computation.11 | async-start | bytes 589824 | tf_op jit(solution)/shard_map/reduce_scatter | solution.py:527
  214.6 31.7 %collective-permute-start.3 = (bf16[64,8,512]{2,1,0:T(8,128)(2,1)S(1)}, bf16[64,8,512]{2,1,0:T(8,128)(2,1)S(1)}, u32[]{:S(2)}, u32[]{:S(2)}) collective-permute-start(bf16[64,8,512]{2,1,0:T(8,128)(2,1)S(1)} %reshape.162.a_ref), channel_id=1, source_target_pairs={{0,8},{8,0},{16,24},{24,16},{1,9},{9,1},{17,25},{25,17},{2,10},{10... | collective-permute-start | bytes 1572872 | tf_op jit(solution)/shard_map/ppermute | solution.py:325
  215.9 30.4 %collective-permute-start.4 = (bf16[64,8,512]{2,1,0:T(8,128)(2,1)S(1)}, bf16[64,8,512]{2,1,0:T(8,128)(2,1)S(1)}, u32[]{:S(2)}, u32[]{:S(2)}) collective-permute-start(bf16[64,8,512]{2,1,0:T(8,128)(2,1)S(1)} %reshape.162.a_ref), channel_id=1, source_target_pairs={{0,16},{8,24},{16,0},{24,8},{1,17},{9,25},{17,1},{25,9},{2,18},{10... | collective-permute-start | bytes 1572872 | tf_op jit(solution)/shard_map/ppermute | solution.py:325
  216.7 29.6 %collective-permute-start.5 = (bf16[64,8,512]{2,1,0:T(8,128)(2,1)S(1)}, bf16[64,8,512]{2,1,0:T(8,128)(2,1)S(1)}, u32[]{:S(2)}, u32[]{:S(2)}) collective-permute-start(bf16[64,8,512]{2,1,0:T(8,128)(2,1)S(1)} %reshape.162.a_ref), channel_id=1, source_target_pairs={{0,24},{8,16},{16,8},{24,0},{1,25},{9,17},{17,9},{25,1},{2,26},{10... | collective-permute-start | bytes 1572872 | tf_op jit(solution)/shard_map/ppermute | solution.py:325
  246.2 1.5 copy-start.10
  246.3 1.5 copy-start.12
  246.3 0.9 copy-start.14
  247.8 31.8 %copy-start.5 = (bf16[64,8,512]{2,1,0:T(8,128)(2,1)}, bf16[64,8,512]{2,1,0:T(8,128)(2,1)S(1)}, u32[]{:S(2)}) copy-start(bf16[64,8,512]{2,1,0:T(8,128)(2,1)S(1)} %reshape.166.a_ref) | copy-start | bytes 1572868
  247.8 32.3 %collective-permute-start.6 = (bf16[64,8,512]{2,1,0:T(8,128)(2,1)S(1)}, bf16[64,8,512]{2,1,0:T(8,128)(2,1)S(1)}, u32[]{:S(2)}, u32[]{:S(2)}) collective-permute-start(bf16[64,8,512]{2,1,0:T(8,128)(2,1)S(1)} %reshape.166.a_ref), channel_id=1, source_target_pairs={{0,8},{8,0},{16,24},{24,16},{1,9},{9,1},{17,25},{25,17},{2,10},{10... | collective-permute-start | bytes 1572872 | tf_op jit(solution)/shard_map/ppermute | solution.py:325
  249.1 31.1 %collective-permute-start.7 = (bf16[64,8,512]{2,1,0:T(8,128)(2,1)S(1)}, bf16[64,8,512]{2,1,0:T(8,128)(2,1)S(1)}, u32[]{:S(2)}, u32[]{:S(2)}) collective-permute-start(bf16[64,8,512]{2,1,0:T(8,128)(2,1)S(1)} %reshape.166.a_ref), channel_id=1, source_target_pairs={{0,16},{8,24},{16,0},{24,8},{1,17},{9,25},{17,1},{25,9},{2,18},{10... | collective-permute-start | bytes 1572872 | tf_op jit(solution)/shard_map/ppermute | solution.py:325
  249.9 30.3 %collective-permute-start.8 = (bf16[64,8,512]{2,1,0:T(8,128)(2,1)S(1)}, bf16[64,8,512]{2,1,0:T(8,128)(2,1)S(1)}, u32[]{:S(2)}, u32[]{:S(2)}) collective-permute-start(bf16[64,8,512]{2,1,0:T(8,128)(2,1)S(1)} %reshape.166.a_ref), channel_id=1, source_target_pairs={{0,24},{8,16},{16,8},{24,0},{1,25},{9,17},{17,9},{25,1},{2,26},{10... | collective-permute-start | bytes 1572872 | tf_op jit(solution)/shard_map/ppermute | solution.py:325
  251.4 94.6 %reduce-scatter.5.cloned.1.call-start = ((), (), s32[]{:S(2)}) async-start(), calls=%async_computation.12 | async-start | bytes 589824 | tf_op jit(solution)/shard_map/reduce_scatter | solution.py:527
  280.1 31.9 %copy-start.6 = (bf16[64,8,512]{2,1,0:T(8,128)(2,1)}, bf16[64,8,512]{2,1,0:T(8,128)(2,1)S(1)}, u32[]{:S(2)}) copy-start(bf16[64,8,512]{2,1,0:T(8,128)(2,1)S(1)} %reshape.167.a_ref) | copy-start | bytes 1572868
  280.1 3.6 copy-start.11
  280.2 3.6 copy-start.13
  280.2 3.6 copy-start.15
  280.2 31.8 %collective-permute-start.9 = (bf16[64,8,512]{2,1,0:T(8,128)(2,1)S(1)}, bf16[64,8,512]{2,1,0:T(8,128)(2,1)S(1)}, u32[]{:S(2)}, u32[]{:S(2)}) collective-permute-start(bf16[64,8,512]{2,1,0:T(8,128)(2,1)S(1)} %reshape.167.a_ref), channel_id=1, source_target_pairs={{0,8},{8,0},{16,24},{24,16},{1,9},{9,1},{17,25},{25,17},{2,10},{10... | collective-permute-start | bytes 1572872 | tf_op jit(solution)/shard_map/ppermute | solution.py:325
  281.5 30.5 %collective-permute-start.10 = (bf16[64,8,512]{2,1,0:T(8,128)(2,1)S(1)}, bf16[64,8,512]{2,1,0:T(8,128)(2,1)S(1)}, u32[]{:S(2)}, u32[]{:S(2)}) collective-permute-start(bf16[64,8,512]{2,1,0:T(8,128)(2,1)S(1)} %reshape.167.a_ref), channel_id=1, source_target_pairs={{0,16},{8,24},{16,0},{24,8},{1,17},{9,25},{17,1},{25,9},{2,18},{10... | collective-permute-start | bytes 1572872 | tf_op jit(solution)/shard_map/ppermute | solution.py:325
  282.3 29.7 %collective-permute-start.11 = (bf16[64,8,512]{2,1,0:T(8,128)(2,1)S(1)}, bf16[64,8,512]{2,1,0:T(8,128)(2,1)}, u32[]{:S(2)}, u32[]{:S(2)}) collective-permute-start(bf16[64,8,512]{2,1,0:T(8,128)(2,1)S(1)} %reshape.167.a_ref), channel_id=1, source_target_pairs={{0,24},{8,16},{16,8},{24,0},{1,25},{9,17},{17,9},{25,1},{2,26},{10... | collective-permute-start | bytes 1572872 | tf_op jit(solution)/shard_map/ppermute | solution.py:325
  312.0 5.8 %copy-start.16 = (bf16[64,8,512]{2,1,0:T(8,128)(2,1)}, bf16[64,8,512]{2,1,0:T(8,128)(2,1)S(1)}, u32[]{:S(2)}) copy-start(bf16[64,8,512]{2,1,0:T(8,128)(2,1)S(1)} %collective-permute-done.9.b_ref) | copy-start | bytes 1572868
  312.0 0.8 copy-start.17
  312.9 33.0 %all-to-all-start.6 = ((f32[8,2,32,256]{3,2,1,0:T(8,128)}), f32[8,2,32,256]{3,2,1,0:T(8,128)S(1)}, u32[]{:S(2)}, u32[]{:S(2)}) async-start(f32[8,2,32,256]{3,2,1,0:T(8,128)} %bitcast.67), calls=%async_computation.8 | async-start | bytes 1048576 | tf_op jit(solution)/shard_map/all_to_all | solution.py:425
Sparse Core Ops, SparseCore 0:
  26.1 33.3 all-gather.1
  251.5 31.2 reduce-scatter.2
  285.2 29.9 reduce-scatter.4
